TPU v7x, 32 devices: a whole 2x2x4 slice. The times are simulated.
32 devices in a mesh: seq: 16 (over z, y, core), tensor: 2 (over x).
Axes of the slice: x: 2, y: 2, z: 4, core: 2. Of those that a mesh axis runs over, the one named last changes fastest.
Arguments:
- q_in: float32 [4096, 5120], P('seq', 'tensor'), may hold values from -520 to 520
- k_in: float32 [4096, 5120], P('seq', 'tensor'), may hold values from -520 to 520
- v_in: bfloat16 [4096, 5120], P('seq', 'tensor'), may hold values from -12 to 12
- q_gain: float32 [5120], P('tensor'), may hold values from 0.8 to 2
- k_gain: float32 [5120], P('tensor'), may hold values from 0.8 to 2
- frames: int32 [32], replicated, may hold values from 0 to 2, never falling along the last dimension, each value on 1 to 12 neighbouring positions
- adjacent: int32 [32, 32], P('seq'), may hold values 0 or 1
Outputs:
- attended: float32 [4096, 5120], P('seq', 'tensor')
Inputs may be any that keep to these rules, and one draw needn't show every extreme that they name: `frames`: frame numbers never fall from one block to the next, and each frame spans 1 to 12 consecutive blocks.
All inputs are finite; a program needn't handle non-finite values. No bound on the sum of `adjacent` on one device may be relied on, other than what follows from the above.
Results may differ from a plain program's by a relative error of at most 0.012.
The roundings to bfloat16 on the way count: a program that leaves them out, or rounds other values in their place, can miss the bound.
Values may be sent and summed in bfloat16 or wider, within the bound.
No kernel may reach another device: no remote copies, remote signals or barrier semaphores. Data moves between devices by JAX's collectives and lax.ppermute only.
A program may use at most 128 MiB of HBM per device.

v0:
```python
import math

import jax
import jax.numpy as jnp
from jax import lax
from jax.sharding import PartitionSpec as P

HEAD_DIM = 128
BLOCK = 128


epsilon = 1e-06
blocked = -1e30


def normalized(inputs, gain_row, square_sum, full_width):
    return (inputs / jnp.sqrt(square_sum / full_width + epsilon)[:, None] * gain_row).astype(
        jnp.bfloat16
    )


def shards(q_in, k_in, v_in, q_gain, k_gain, frames, adjacent):
    tok_rows = q_in.shape[0]
    width_dev = q_in.shape[1]
    full_width = width_dev * lax.axis_size("tensor")
    q_sum, k_sum = lax.psum((jnp.sum(q_in * q_in, axis=1), jnp.sum(k_in * k_in, axis=1)), "tensor")
    q_norm = normalized(q_in, q_gain, q_sum, full_width)
    k_norm = normalized(k_in, k_gain, k_sum, full_width)
    blk_dev = tok_rows // BLOCK
    device = lax.axis_index("seq")
    first_block = device * blk_dev
    query_frames = lax.dynamic_slice_in_dim(frames, first_block, blk_dev, 0)
    score_scale = 1.0 / math.sqrt(HEAD_DIM)
    head_count = width_dev // HEAD_DIM
    q_three = q_norm.reshape(tok_rows, head_count, HEAD_DIM)

    def masked_scores(key_rows, key_start):
        key_block = key_start // BLOCK
        key_frames = lax.dynamic_slice_in_dim(frames, key_block, blk_dev, 0)
        adjacent_rows = lax.dynamic_slice_in_dim(adjacent, key_block, blk_dev, 1)
        frame_gap = jnp.abs(query_frames[:, None] - key_frames[None, :])
        allowed_here = (frame_gap == 0) | (frame_gap == 1) & (adjacent_rows == 1)
        key_three = key_rows.reshape(tok_rows, head_count, HEAD_DIM)
        raw_scores = (
            jnp.einsum("thd,uhd->htu", q_three, key_three, preferred_element_type=jnp.float32)
            * score_scale
        )
        tiled_scores = raw_scores.reshape(head_count, blk_dev, BLOCK, blk_dev, BLOCK)
        tiled_scores = jnp.where(allowed_here[None, :, None, :, None], tiled_scores, blocked)
        return tiled_scores.reshape(head_count, tok_rows, tok_rows)

    piece = lax.all_gather(k_norm, "seq", axis=0, tiled=True)
    shard_count = piece.shape[0] // tok_rows

    def one_shard(shard, current):
        key_rows = lax.dynamic_slice_in_dim(piece, shard * tok_rows, tok_rows, 0)
        return jnp.maximum(current, jnp.max(masked_scores(key_rows, shard * tok_rows), axis=2))

    row_max = lax.fori_loop(
        0, shard_count, one_shard, jnp.full((head_count, tok_rows), blocked, jnp.float32)
    )
    start_sums = (
        jnp.zeros((head_count, tok_rows), jnp.float32),
        jnp.zeros((tok_rows, head_count, HEAD_DIM), jnp.float32),
    )
    key_piece = lax.all_gather(k_norm, "seq", axis=0, tiled=True)
    value_piece = lax.all_gather(v_in, "seq", axis=0, tiled=True)
    shard_count = key_piece.shape[0] // tok_rows

    def one_shard(shard, current):
        totals, accumulated = current
        key_rows = lax.dynamic_slice_in_dim(key_piece, shard * tok_rows, tok_rows, 0)
        value_rows = lax.dynamic_slice_in_dim(value_piece, shard * tok_rows, tok_rows, 0).reshape(
            tok_rows, head_count, HEAD_DIM
        )
        weights = jnp.exp(masked_scores(key_rows, shard * tok_rows) - row_max[:, :, None])
        totals = totals + jnp.sum(weights, axis=2)
        accumulated = accumulated + jnp.einsum(
            "htu,uhd->thd",
            weights.astype(jnp.bfloat16),
            value_rows,
            preferred_element_type=jnp.float32,
        )
        return (totals, accumulated)

    totals, accumulated = lax.fori_loop(0, shard_count, one_shard, start_sums)
    return (accumulated / totals.T[:, :, None]).reshape(tok_rows, width_dev)


def solution(mesh):
    return jax.shard_map(
        shards,
        mesh=mesh,
        in_specs=(
            P("seq", "tensor"),
            P("seq", "tensor"),
            P("seq", "tensor"),
            P("tensor"),
            P("tensor"),
            P(),
            P("seq", None),
        ),
        out_specs=P("seq", "tensor"),
        check_vma=False,
    )
```

profile of v0, /device:TPU:0, one launch (start us, length us, event | category | flops | bytes accessed | tf_op | source)
XLA Modules:
  0.0 365.4 jit_solution(18207842040250031400)
XLA Ops:
  6.5 3.4 copy.18
  9.9 2.2 multiply_reduce_fusion
  12.1 5.8 %all-reduce = (f32[256]{0:T(256)S(1)}, f32[256]{0:T(256)S(1)}) all-reduce(f32[256]{0:T(256)S(1)} %get-tuple-element.561, f32[256]{0:T(256)S(1)} %get-tuple-element.560), channel_id=1, replica_groups=mesh['seq'=16,'tensor'=2] {'tensor'}, use_global_device_ids=true, to_apply=%region_1.0 | all-reduce | flops 512 | bytes 4096 | tf_op jit(solution)/shard_map/psum | solution.py:26
  17.9 3.2 multiply_convert_fusion.1
  21.2 2.6 copy.21
  23.9 2.1 copy.19
  26.0 3.2 multiply_convert_fusion
  29.3 2.6 copy.22
  32.0 108.1 %all-gather.3.cloned.1.call-done = bf16[4096,2560]{0,1:T(8,128)(2,1)} async-done(((bf16[256,2560]{0,1:T(8,128)(2,1)}), bf16[4096,2560]{0,1:T(8,128)(2,1)}) %all-gather.3.cloned.1.call-update) | async-done | bytes 20971536 | tf_op jit(solution)/shard_map/all_gather | solution.py:66
  140.0 54.7 %while.34 = (s32[]{:T(128)}, f32[20,256]{1,0:T(8,128)S(1)}, s32[2]{0:T(128)S(1)}, s32[32]{0:T(128)S(1)}, s32[2,32]{1,0:T(2,128)S(1)}, /*index=5*/bf16[4096,2560]...) while((s32[]{:T(128)}, f32[20,256]{1,0:T(8,128)S(1)}, ...), condition=%wide.region_6.7_spmd.clone, body=%wide.region_4.6_spmd.clone.sunk | while | flops 339481664 | bytes 10961372 | solution.py:59
  194.7 62.6 %all-gather.5.cloned.1.call-done = bf16[4096,2560]{0,1:T(8,128)(2,1)} async-done(((bf16[256,2560]{0,1:T(8,128)(2,1)}), bf16[4096,2560]{0,1:T(8,128)(2,1)}) %all-gather.5.cloned.1.call-update) | async-done | bytes 20971536 | tf_op jit(solution)/shard_map/all_gather | solution.py:67
  257.3 96.2 %while.35 = (s32[]{:T(128)}, f32[20,256]{1,0:T(8,128)S(1)}, f32[256,20,128]{0,2,1:T(8,128)S(1)}, s32[2]{0:T(128)S(1)}, s32[32]{0:T(128)S(1)}, /*index=5*/s32[2,3...) while((s32[]{:T(128)}, f32[20,256]{1,0:T(8,128)S(1)}, ...), condition=%wide.region_9.10_spmd.clone, body=%wide.region_7.9_spmd.clone.sunk | while | flops 682890304 | bytes 30728688 | solution.py:86
  257.8 2.0 constant_dynamic-slice_fusion.6
  261.6 1.7 bitcast_add_fusion.2
  263.9 2.0 constant_dynamic-slice_fusion.6
  267.6 1.7 bitcast_add_fusion.2
  269.9 2.0 constant_dynamic-slice_fusion.6
  275.9 2.0 constant_dynamic-slice_fusion.6
  281.9 2.0 constant_dynamic-slice_fusion.6
  287.9 2.0 constant_dynamic-slice_fusion.6
  293.9 2.0 constant_dynamic-slice_fusion.6
  299.9 2.0 constant_dynamic-slice_fusion.6
  305.9 2.0 constant_dynamic-slice_fusion.6
  312.0 2.0 constant_dynamic-slice_fusion.6
  318.0 2.0 constant_dynamic-slice_fusion.6
  324.0 2.0 constant_dynamic-slice_fusion.6
  330.0 2.0 constant_dynamic-slice_fusion.6
  336.0 2.0 constant_dynamic-slice_fusion.6
  342.0 2.0 constant_dynamic-slice_fusion.6
  348.0 2.0 constant_dynamic-slice_fusion.6
  353.5 1.8 broadcast_divide_fusion
  355.3 3.2 copy.23
  (340 shorter events, 112.6 us)
Async XLA Ops:
  6.5 3.4 copy-start
  6.5 133.5 %all-gather.3.cloned.1.call-start = ((), (), s32[]{:S(2)}) async-start(), calls=%async_computation | async-start | bytes 22282240 | tf_op jit(solution)/shard_map/all_gather | solution.py:66
  9.9 8.0 %copy-start.5 = (f32[2560]{0:T(1024)S(1)}, f32[2560]{0:T(1024)}, u32[]{:S(2)}) copy-start(f32[2560]{0:T(1024)} %param.15) | copy-start | bytes 30724
  21.2 2.7 copy-start.1
  21.2 236.1 %all-gather.5.cloned.1.call-start = ((), (), s32[]{:S(2)}) async-start(), calls=%async_computation.1 | async-start | bytes 22282240 | tf_op jit(solution)/shard_map/all_gather | solution.py:67
  23.9 2.1 copy-start.6
  26.0 5.9 %copy-start.7 = (s32[32]{0:T(128)S(1)}, s32[32]{0:T(128)}, u32[]{:S(2)}) copy-start(s32[32]{0:T(128)} %param.16) | copy-start | bytes 388
  26.0 114.0 %copy-start.4 = (s32[2,32]{1,0:T(2,128)S(1)}, s32[2,32]{1,0:T(2,128)}, u32[]{:S(2)}) copy-start(s32[2,32]{1,0:T(2,128)} %param.17) | copy-start | bytes 772
  147.3 1.8 copy-start.2
  150.8 1.8 copy-start.2
  161.1 1.7 copy-start.2
  164.5 1.8 copy-start.2
  167.9 1.8 copy-start.2
  171.4 1.7 copy-start.2
  181.6 1.8 copy-start.2
  185.0 1.8 copy-start.2
  257.8 2.1 copy-start.3
  263.8 2.1 copy-start.3
  269.9 2.1 copy-start.3
  275.9 2.1 copy-start.3
  281.9 2.1 copy-start.3
  287.9 2.1 copy-start.3
  293.9 2.1 copy-start.3
  299.9 2.1 copy-start.3
  305.9 2.1 copy-start.3
  311.9 2.1 copy-start.3
  318.0 2.1 copy-start.3
  324.0 2.1 copy-start.3
  330.0 2.1 copy-start.3
  336.0 2.1 copy-start.3
  342.0 2.1 copy-start.3
  348.0 2.1 copy-start.3
  (8 other events, 13.8 us)
Sparse Core Ops, SparseCore 0:
  21.3 118.6 all-gather.2
  141.5 115.7 all-gather.4
where the time goes:
time: 366 us; the launch traced here: 365 us
  waiting for transfers between devices  171 us (47%)
  local copies, waits for them, and re-layouts  89.5 us (24%)
  matrix products  69.7 us (19%)
  between operations  13.5 us (4%)
  other arithmetic  13.2 us (4%)
  blocking collectives  5.84 us (2%)
    all_gather x1, waiting for transfers between devices, shards(): key_piece = lax.all_gather(k_norm, 'seq', axis=0, tiled=True)  108 us
    all_gather x1, waiting for transfers between devices, shards(): value_piece = lax.all_gather(v_in, 'seq', axis=0, tiled=True)  62.6 us
    dot_general x32, matrix products, masked_scores(): jnp.einsum('thd,uhd->htu', q_three, key_three, preferred_element_type=jnp...  42.3 us
    dynamic_slice x16, local copies, waits for them, and re-layouts, one_shard(): lax.dynamic_slice_in_dim(value_piece, shard * tok_rows, tok_rows, 0)  32.1 us
    dot_general x16, matrix products, one_shard(): jnp.einsum('htu,uhd->thd', weights.astype(jnp.bfloat16), value_rows, pref...  27.4 us
    dynamic_slice x16, local copies, waits for them, and re-layouts, one_shard(): key_rows = lax.dynamic_slice_in_dim(piece, shard * tok_rows, tok_rows, 0)  24.3 us
    unnamed x16, local copies, waits for them, and re-layouts  10.7 us
    broadcast_in_dim x64, local copies, waits for them, and re-layouts, masked_scores(): jnp.where(allowed_here[None, :, None, :, None], tiled_scores, blocked)  9.93 us
  transfers between devices with their start and end apart: 2, of which 2 were waited for; matrix products, arithmetic and copies ran while one was open for 17% of the time, Pallas kernels for 0%

commit v1 on v0

--- a/solution.py
+++ b/solution.py
@@ -1,16 +1,288 @@
+import functools
 import math
 
 import jax
 import jax.numpy as jnp
 from jax import lax
+from jax.experimental import pallas as pl
+from jax.experimental.pallas import tpu as pltpu
 from jax.sharding import PartitionSpec as P
 
 HEAD_DIM = 128
 BLOCK = 128
-
-
 epsilon = 1e-06
 blocked = -1e30
+GROUP = 4
+MIB = 1024 * 1024
+
+
+def value_pieces_kernel(place_ref, v_ref, *outs, groups, chunks):
+    per_group = sum(chunks)
+    for shift in range(groups):
+        group = lax.rem(place_ref[0] + shift, groups)
+        first = 0
+        for c, heads in enumerate(chunks):
+            out = outs[c * groups + shift]
+            for h in range(heads):
+                column = pl.multiple_of((group * per_group + first + h) * HEAD_DIM, HEAD_DIM)
+                out[h] = v_ref[:, pl.ds(column, HEAD_DIM)]
+            first += heads
+
+
+def square_sums_kernel(q_ref, k_ref, out_ref):
+    q, k = q_ref[...], k_ref[...]
+    out_ref[:, 0:1] = jnp.sum(q * q, axis=1, keepdims=True)
+    out_ref[:, 1:2] = jnp.sum(k * k, axis=1, keepdims=True)
+
+
+def norm_pieces_kernel(
+    place_ref, sums_ref, q_ref, k_ref, q_gain_ref, k_gain_ref, *outs, groups, chunks, full_width
+):
+    per_group = sum(chunks)
+    count = groups * len(chunks)
+    for role, (x_ref, gain_ref) in enumerate(((q_ref, q_gain_ref), (k_ref, k_gain_ref))):
+        mean = sums_ref[:, role : role + 1] / full_width
+        inverse = 1.0 / jnp.sqrt(mean + epsilon)
+        for shift in range(groups):
+            group = lax.rem(place_ref[0] + shift, groups)
+            first = 0
+            for c, heads in enumerate(chunks):
+                out = outs[role * count + c * groups + shift]
+                for h in range(heads):
+                    column = pl.multiple_of((group * per_group + first + h) * HEAD_DIM, HEAD_DIM)
+                    x = x_ref[:, pl.ds(column, HEAD_DIM)]
+                    gain = gain_ref[:, pl.ds(column, HEAD_DIM)]
+                    out[h] = (x * inverse * gain).astype(jnp.bfloat16)
+                first += heads
+
+
+def attend_kernel(count_ref, list_ref, *refs, groups, layers, blk_dev, scale):
+    q_refs = refs[:groups]
+    k_refs = refs[groups : groups + layers]
+    v_refs = refs[groups + layers : groups + 2 * layers]
+    outs = refs[groups + 2 * layers : 2 * groups + 2 * layers]
+    k_all, v_all, scores = refs[2 * groups + 2 * layers :]
+    for layer in range(layers):
+        for g in range(groups):
+            for b in range(blk_dev):
+                slot = (layer * groups + g) * blk_dev + b
+                rows = pl.ds(b * BLOCK, BLOCK)
+                k_all[slot] = k_refs[layer][g, 0, rows, :]
+                v_all[slot] = v_refs[layer][g, 0, rows, :]
+    for g in range(groups):
+        for b in range(blk_dev):
+            query = g * blk_dev + b
+            rows = pl.ds(b * BLOCK, BLOCK)
+            q = q_refs[g][0, rows, :]
+            count = count_ref[query]
+            steps = lax.div(count + GROUP - 1, GROUP)
+
+            def score_step(step, top):
+                for u in range(GROUP):
+                    spot = step * GROUP + u
+                    block = lax.dot_general(
+                        q,
+                        k_all[list_ref[query, spot]],
+                        (((1,), (1,)), ((), ())),
+                        preferred_element_type=jnp.float32,
+                    )
+                    block = block + jnp.where(spot < count, 0.0, blocked)
+                    scores[spot] = block
+                    top = jnp.maximum(top, block)
+                return top
+
+            top = lax.fori_loop(
+                0, steps, score_step, jnp.full((BLOCK, BLOCK), blocked, jnp.float32)
+            )
+            row_max = jnp.max(top, axis=1, keepdims=True)
+
+            def weigh_step(step, current):
+                total, mixed = current
+                for u in range(GROUP):
+                    spot = step * GROUP + u
+                    weights = jnp.exp2((scores[spot] - row_max) * scale)
+                    total = total + weights
+                    mixed = mixed + jnp.dot(
+                        weights.astype(jnp.bfloat16),
+                        v_all[list_ref[query, spot]],
+                        preferred_element_type=jnp.float32,
+                    )
+                return total, mixed
+
+            zero = jnp.zeros((BLOCK, BLOCK), jnp.float32)
+            total, mixed = lax.fori_loop(0, steps, weigh_step, (zero, zero))
+            outs[g][0, rows, :] = (mixed / jnp.sum(total, axis=1, keepdims=True)).astype(
+                jnp.bfloat16
+            )
+
+
+def collect_kernel(place_ref, *refs, groups, chunks):
+    out = refs[-1]
+    per_group = sum(chunks)
+    for shift in range(groups):
+        group = lax.rem(place_ref[0] + shift, groups)
+        first = 0
+        for c, heads in enumerate(chunks):
+            piece = refs[c * groups + shift]
+            for h in range(heads):
+                column = pl.multiple_of((group * per_group + first + h) * HEAD_DIM, HEAD_DIM)
+                out[:, pl.ds(column, HEAD_DIM)] = piece[h].astype(jnp.float32)
+            first += heads
+
+
+VMEM = pl.BlockSpec(memory_space=pltpu.VMEM)
+SMEM = pl.BlockSpec(memory_space=pltpu.SMEM)
+
+
+def exchanged(q_in, k_in, v_in, q_gain, k_gain, frames, adjacent, *, groups, chunks):
+    rows, width = q_in.shape
+    devices = lax.axis_size("seq")
+    tensors = lax.axis_size("tensor")
+    layers = devices // groups
+    blk_dev = rows // BLOCK
+    blocks = devices * blk_dev
+    full_width = width * tensors
+    me = lax.axis_index("seq")
+    place, spot = me // layers, lax.rem(me, layers)
+    place_row = place.reshape(1).astype(jnp.int32)
+    f32, bf16 = jnp.float32, jnp.bfloat16
+    params = pltpu.CompilerParams(vmem_limit_bytes=48 * MIB)
+
+    def rotated(x, shift):
+        pairs = [
+            (z * layers + r, (z + shift) % groups * layers + r)
+            for z in range(groups)
+            for r in range(layers)
+        ]
+        return lax.ppermute(x, "seq", pairs)
+
+    def swapped(x, bit):
+        return lax.ppermute(x, "seq", [(i, i ^ bit) for i in range(devices)])
+
+    def piece_shapes(times):
+        return [
+            jax.ShapeDtypeStruct((heads, rows, HEAD_DIM), bf16)
+            for _ in range(times)
+            for heads in chunks
+            for _ in range(groups)
+        ]
+
+    def split(pieces):
+        return [pieces[c * groups : (c + 1) * groups] for c in range(len(chunks))]
+
+    v_pieces = pl.pallas_call(
+        functools.partial(value_pieces_kernel, groups=groups, chunks=chunks),
+        out_shape=piece_shapes(1),
+        in_specs=[SMEM, VMEM],
+        out_specs=[VMEM] * (groups * len(chunks)),
+        compiler_params=params,
+        name="value_pieces",
+    )(place_row, v_in)
+
+    sums = pl.pallas_call(
+        square_sums_kernel,
+        out_shape=jax.ShapeDtypeStruct((rows, 2), f32),
+        in_specs=[VMEM, VMEM],
+        out_specs=VMEM,
+        compiler_params=params,
+        name="square_sums",
+    )(q_in, k_in)
+    if tensors == 2:
+        sums = sums + lax.ppermute(sums, "tensor", [(0, 1), (1, 0)])
+    else:
+        sums = lax.psum(sums, "tensor")
+
+    normed = pl.pallas_call(
+        functools.partial(
+            norm_pieces_kernel, groups=groups, chunks=chunks, full_width=float(full_width)
+        ),
+        out_shape=piece_shapes(2),
+        in_specs=[SMEM] + [VMEM] * 5,
+        out_specs=[VMEM] * (2 * groups * len(chunks)),
+        compiler_params=params,
+        name="norm_pieces",
+    )(place_row, sums, q_in, k_in, q_gain.reshape(1, width), k_gain.reshape(1, width))
+    q_pieces, k_pieces = normed[: len(normed) // 2], normed[len(normed) // 2 :]
+
+    everyone = lax.all_gather(adjacent, "seq", axis=0, tiled=True)
+    gap = jnp.abs(frames[:, None] - frames[None, :])
+    allowed = (gap == 0) | (gap == 1) & (everyone == 1)
+    z_order = lax.rem(place - jnp.arange(groups) + groups, groups)
+    query_blocks = (
+        (z_order[:, None] * layers + spot) * blk_dev + jnp.arange(blk_dev)[None, :]
+    ).reshape(-1)
+    layer_order = jnp.bitwise_xor(spot, jnp.arange(layers))
+    key_blocks = (
+        (z_order[None, :, None] * layers + layer_order[:, None, None]) * blk_dev
+        + jnp.arange(blk_dev)[None, None, :]
+    ).reshape(-1)
+    query_hot = (query_blocks[:, None] == jnp.arange(blocks)[None, :]).astype(f32)
+    key_hot = (key_blocks[:, None] == jnp.arange(blocks)[None, :]).astype(f32)
+    table = (query_hot @ allowed.astype(f32) @ key_hot.T) > 0.5
+    upto = jnp.tril(jnp.ones((blocks, blocks), f32)).T
+    position = (table.astype(f32) @ upto).astype(jnp.int32) - 1
+    counts = jnp.sum(table, axis=1).astype(jnp.int32)
+    spots = jnp.arange(blocks + GROUP, dtype=jnp.int32)
+    chosen = table[:, :, None] & (position[:, :, None] == spots[None, None, :])
+    lists = jnp.sum(
+        jnp.where(chosen, jnp.arange(blocks, dtype=jnp.int32)[None, :, None], 0), axis=1
+    ).astype(jnp.int32)
+
+    scale = math.log2(math.e) / math.sqrt(HEAD_DIM)
+    outputs = []
+    for c, heads in enumerate(chunks):
+        v_z, k_z, q_z = [
+            [pieces[0]] + [rotated(pieces[s], s) for s in range(1, groups)]
+            for pieces in (split(v_pieces)[c], split(k_pieces)[c], split(q_pieces)[c])
+        ]
+        gathered = []
+        for pieces in (k_z, v_z):
+            parts = {0: jnp.stack(pieces)}
+            bit = layers // 2
+            while bit:
+                for have in list(parts):
+                    parts[have ^ bit] = swapped(parts[have], bit)
+                bit //= 2
+            gathered.append([parts[i] for i in range(layers)])
+        big = pl.BlockSpec((groups, 1, rows, HEAD_DIM), lambda h, *_: (0, h, 0, 0))
+        small = pl.BlockSpec((1, rows, HEAD_DIM), lambda h, *_: (h, 0, 0))
+        pairs = blocks * groups * blk_dev
+        attended = pl.pallas_call(
+            functools.partial(
+                attend_kernel, groups=groups, layers=layers, blk_dev=blk_dev, scale=scale
+            ),
+            grid_spec=pltpu.PrefetchScalarGridSpec(
+                num_scalar_prefetch=2,
+                grid=(heads,),
+                in_specs=[small] * groups + [big] * (2 * layers),
+                out_specs=[small] * groups,
+                scratch_shapes=[
+                    pltpu.VMEM((blocks, BLOCK, HEAD_DIM), bf16),
+                    pltpu.VMEM((blocks, BLOCK, HEAD_DIM), bf16),
+                    pltpu.VMEM((blocks + GROUP, BLOCK, BLOCK), f32),
+                ],
+            ),
+            out_shape=[jax.ShapeDtypeStruct((heads, rows, HEAD_DIM), bf16)] * groups,
+            compiler_params=params,
+            cost_estimate=pl.CostEstimate(
+                flops=heads * pairs * 4 * BLOCK**3,
+                bytes_accessed=heads * blocks * BLOCK * HEAD_DIM * 5,
+                transcendentals=heads * pairs * BLOCK**2,
+            ),
+            name=f"attend_{c}",
+        )(counts, lists, *q_z, *gathered[0], *gathered[1])
+        outputs += [attended[0]] + [
+            rotated(attended[s], groups - s) for s in range(1, groups)
+        ]
+
+    return pl.pallas_call(
+        functools.partial(collect_kernel, groups=groups, chunks=chunks),
+        out_shape=jax.ShapeDtypeStruct((rows, width), f32),
+        in_specs=[SMEM] + [VMEM] * (groups * len(chunks)),
+        out_specs=VMEM,
+        compiler_params=params,
+        name="collect",
+    )(place_row, *outputs)
 
 
 def normalized(inputs, gain_row, square_sum, full_width):
@@ -87,19 +359,39 @@
     return (accumulated / totals.T[:, :, None]).reshape(tok_rows, width_dev)
 
 
+def plan(mesh, heads):
+    devices = mesh.shape["seq"]
+    for layers in (4,):
+        groups = devices // layers
+        if devices % layers == 0 and groups > 1 and heads % groups == 0:
+            return groups
+    return None
+
+
 def solution(mesh):
-    return jax.shard_map(
-        shards,
-        mesh=mesh,
-        in_specs=(
-            P("seq", "tensor"),
-            P("seq", "tensor"),
-            P("seq", "tensor"),
-            P("tensor"),
-            P("tensor"),
-            P(),
-            P("seq", None),
-        ),
-        out_specs=P("seq", "tensor"),
-        check_vma=False,
-    )
+    def step(q_in, k_in, v_in, q_gain, k_gain, frames, adjacent):
+        heads = q_in.shape[1] // mesh.shape["tensor"] // HEAD_DIM
+        groups = plan(mesh, heads)
+        if groups is None:
+            body = shards
+        else:
+            per_group = heads // groups
+            chunks = (per_group - per_group // 2, per_group // 2)
+            body = functools.partial(exchanged, groups=groups, chunks=chunks)
+        return jax.shard_map(
+            body,
+            mesh=mesh,
+            in_specs=(
+                P("seq", "tensor"),
+                P("seq", "tensor"),
+                P("seq", "tensor"),
+                P("tensor"),
+                P("tensor"),
+                P(),
+                P("seq", None),
+            ),
+            out_specs=P("seq", "tensor"),
+            check_vma=False,
+        )(q_in, k_in, v_in, q_gain, k_gain, frames, adjacent)
+
+    return step

time: 366 us -> 272 us (0.74)
  waiting for transfers between devices: 171 us -> 56.1 us
  Pallas kernels: 0 us -> 96.2 us
  local copies, waits for them, and re-layouts: 89.5 us -> 11.4 us
  matrix products: 69.7 us -> 1.27 us
  starting transfers between devices: 0.04 us -> 59.9 us
  blocking collectives: 5.84 us -> 44.2 us
  between operations: 13.5 us -> 0.29 us
  other arithmetic: 13.2 us -> 0.76 us
    all_gather x2 -> x0, waiting for transfers between devices: 171 us -> none  [the longest x1 108 us: shards(): key_piece = lax.all_gather(k_norm, 'seq', axis=0, tiled=True)]
    pallas_call x0 -> x6, Pallas kernels: none -> 96.2 us  [the longest x2 91.1 us: exchanged(): pl.pallas_call(functools.partial(attend_kernel, groups=groups, layers=lay...]
    dot_general x48 -> x2, matrix products: 69.7 us -> 1.27 us  [the longest x1 1.15 us: exchanged(): table = query_hot @ allowed.astype(f32) @ key_hot.T > 0.5]
    ppermute x0 -> x37, starting transfers between devices: none -> 59.9 us  [the longest x24 51.1 us: rotated(): return lax.ppermute(x, 'seq', pairs)]
    dynamic_slice x65 -> x0, local copies, waits for them, and re-layouts: 59 us -> none  [the longest x16 32.1 us: one_shard(): lax.dynamic_slice_in_dim(value_piece, shard * tok_rows, tok_rows, 0)]
    ppermute x0 -> x37, waiting for transfers between devices: none -> 56.1 us  [the longest x24 54.7 us: rotated(): return lax.ppermute(x, 'seq', pairs)]
    all_gather x0 -> x1, blocking collectives: none -> 44.2 us  [exchanged(): everyone = lax.all_gather(adjacent, 'seq', axis=0, tiled=True)]
    broadcast_in_dim x64 -> x0, local copies, waits for them, and re-layouts: 9.93 us -> none  [masked_scores(): jnp.where(allowed_here[None, :, None, :, None], tiled_scores, blocked)]
  transfers between devices with their start and end apart: 2 -> 37, of which waited for: 2 -> 9; matrix products, arithmetic and copies ran while one was open for 17% -> 1% of each run, Pallas kernels for 0% -> 35%
where the time goes in v1:
time: 272 us; the launch traced here: 270 us
  Pallas kernels  96.2 us (35%)
  starting transfers between devices  59.9 us (22%)
  waiting for transfers between devices  56.1 us (21%)
  blocking collectives  44.2 us (16%)
  local copies, waits for them, and re-layouts  11.4 us (4%)
    pallas_call x2, Pallas kernels, exchanged(): pl.pallas_call(functools.partial(attend_kernel, groups=groups, layers=lay...  91.1 us
    ppermute x24, waiting for transfers between devices, rotated(): return lax.ppermute(x, 'seq', pairs)  54.7 us
    ppermute x24, starting transfers between devices, rotated(): return lax.ppermute(x, 'seq', pairs)  51.1 us
    all_gather x1, blocking collectives, exchanged(): everyone = lax.all_gather(adjacent, 'seq', axis=0, tiled=True)  44.2 us
    unnamed x42, local copies, waits for them, and re-layouts  10.1 us
    ppermute x12, starting transfers between devices, swapped(): return lax.ppermute(x, 'seq', [(i, i ^ bit) for i in range(devices)])  7.26 us
  transfers between devices with their start and end apart: 37, of which 9 were waited for; matrix products, arithmetic and copies ran while one was open for 1% of the time, Pallas kernels for 35%

profile of v1, /device:TPU:0, one launch (start us, length us, event | category | flops | bytes accessed | tf_op | source)
XLA Modules:
  0.0 270.1 jit_solution(17889187075240853378)
XLA Ops:
  1.6 3.1 %collective-permute-start.28 = (bf16[2,256,128]{2,1,0:T(8,128)(2,1)S(1)}, bf16[2,256,128]{2,1,0:T(8,128)(2,1)S(1)}, u32[]{:S(2)}, u32[]{:S(2)}) collective-permute-start(bf16[2,256,128]{2,1,0:T(8,128)(2,1)S(1)} %get-tuple-element.62), channel_id=1, source_target_pairs={{0,8},{2,10},{4,12},{6,14},{8,16},{10,18},{12,20},{14,22},{16,24},... | collective-permute-start | bytes 393224 | tf_op jit(solution)/shard_map/ppermute | solution.py:157
  4.6 1.7 copy-done
  6.4 1.7 copy-done.1
  8.5 1.5 collective-permute-start
  10.1 2.6 collective-permute-start.29
  12.7 1.3 collective-permute-start.30
  14.1 2.6 norm_pieces.1
  19.2 2.6 collective-permute-start.24
  23.0 7.0 %collective-permute-start.11 = (bf16[3,256,128]{2,1,0:T(8,128)(2,1)S(1)}, bf16[3,256,128]{2,1,0:T(8,128)(2,1)S(1)}, u32[]{:S(2)}, u32[]{:S(2)}) collective-permute-start(bf16[3,256,128]{2,1,0:T(8,128)(2,1)S(1)} %get-tuple-element.47), channel_id=1, source_target_pairs={{0,16},{2,18},{4,20},{6,22},{8,24},{10,26},{12,28},{14,30},{16,0},... | collective-permute-start | bytes 589832 | tf_op jit(solution)/shard_map/ppermute | solution.py:157
  29.9 3.0 %collective-permute-start.12 = (bf16[3,256,128]{2,1,0:T(8,128)(2,1)S(1)}, bf16[3,256,128]{2,1,0:T(8,128)(2,1)S(1)}, u32[]{:S(2)}, u32[]{:S(2)}) collective-permute-start(bf16[3,256,128]{2,1,0:T(8,128)(2,1)S(1)} %get-tuple-element.48), channel_id=1, source_target_pairs={{0,24},{2,26},{4,28},{6,30},{8,0},{10,2},{12,4},{14,6},{16,8},{18,... | collective-permute-start | bytes 589832 | tf_op jit(solution)/shard_map/ppermute | solution.py:157
  32.9 6.6 %collective-permute-done.23 = bf16[2,256,128]{2,1,0:T(8,128)(2,1)S(1)} collective-permute-done((bf16[2,256,128]{2,1,0:T(8,128)(2,1)S(1)}, bf16[2,256,128]{2,1,0:T(8,128)(2,1)S(1)}, u32[]{:S(2)}, u32[]{:S(2)}) %collective-permute-start.23) | collective-permute-done | bytes 131104 | tf_op jit(solution)/shard_map/ppermute | solution.py:157
  39.5 1.9 collective-permute-start.19
  41.5 5.1 %collective-permute-start.20 = (bf16[2,256,128]{2,1,0:T(8,128)(2,1)S(1)}, bf16[2,256,128]{2,1,0:T(8,128)(2,1)S(1)}, u32[]{:S(2)}, u32[]{:S(2)}) collective-permute-start(bf16[2,256,128]{2,1,0:T(8,128)(2,1)S(1)} %get-tuple-element.55), channel_id=1, source_target_pairs={{0,16},{2,18},{4,20},{6,22},{8,24},{10,26},{12,28},{14,30},{16,0},... | collective-permute-start | bytes 393224 | tf_op jit(solution)/shard_map/ppermute | solution.py:157
  46.6 3.0 %collective-permute-done.19.refs_1_ = bf16[2,256,128]{2,1,0:T(8,128)(2,1)S(1)} collective-permute-done((bf16[2,256,128]{2,1,0:T(8,128)(2,1)S(1)}, bf16[2,256,128]{2,1,0:T(8,128)(2,1)S(1)}, u32[]{:S(2)}, u32[]{:S(2)}) %collective-permute-start.19) | collective-permute-done | bytes 131104 | tf_op jit(solution)/shard_map/ppermute | solution.py:157
  49.7 6.2 %collective-permute-start.4 = (bf16[3,256,128]{2,1,0:T(8,128)(2,1)S(1)}, bf16[3,256,128]{2,1,0:T(8,128)(2,1)S(1)}, u32[]{:S(2)}, u32[]{:S(2)}) collective-permute-start(bf16[3,256,128]{2,1,0:T(8,128)(2,1)S(1)} %get-tuple-element.42), channel_id=1, source_target_pairs={{0,8},{2,10},{4,12},{6,14},{8,16},{10,18},{12,20},{14,22},{16,24},... | collective-permute-start | bytes 589832 | tf_op jit(solution)/shard_map/ppermute | solution.py:157
  55.8 10.4 %collective-permute-done.20.refs_2_ = bf16[2,256,128]{2,1,0:T(8,128)(2,1)S(1)} collective-permute-done((bf16[2,256,128]{2,1,0:T(8,128)(2,1)S(1)}, bf16[2,256,128]{2,1,0:T(8,128)(2,1)S(1)}, u32[]{:S(2)}, u32[]{:S(2)}) %collective-permute-start.20) | collective-permute-done | bytes 131104 | tf_op jit(solution)/shard_map/ppermute | solution.py:157
  66.3 1.6 collective-permute-start.32
  68.0 1.9 collective-permute-start.1
  70.1 2.9 %collective-permute-done.5 = bf16[3,256,128]{2,1,0:T(8,128)(2,1)S(1)} collective-permute-done((bf16[3,256,128]{2,1,0:T(8,128)(2,1)S(1)}, bf16[3,256,128]{2,1,0:T(8,128)(2,1)S(1)}, u32[]{:S(2)}, u32[]{:S(2)}) %collective-permute-start.5) | collective-permute-done | bytes 196640 | tf_op jit(solution)/shard_map/ppermute | solution.py:157
  73.0 4.7 %collective-permute-start.21 = (bf16[2,256,128]{2,1,0:T(8,128)(2,1)S(1)}, bf16[2,256,128]{2,1,0:T(8,128)(2,1)S(1)}, u32[]{:S(2)}, u32[]{:S(2)}) collective-permute-start(bf16[2,256,128]{2,1,0:T(8,128)(2,1)S(1)} %get-tuple-element.56), channel_id=1, source_target_pairs={{0,24},{2,26},{4,28},{6,30},{8,0},{10,2},{12,4},{14,6},{16,8},{18,... | collective-permute-start | bytes 393224 | tf_op jit(solution)/shard_map/ppermute | solution.py:157
  77.7 2.6 collective-permute-done.6
  80.4 1.4 collective-permute-done.21.refs_3_
  81.8 2.2 collective-permute-start.14
  84.1 6.3 %collective-permute-done.2.refs_2_ = bf16[3,256,128]{2,1,0:T(8,128)(2,1)S(1)} collective-permute-done((bf16[3,256,128]{2,1,0:T(8,128)(2,1)S(1)}, bf16[3,256,128]{2,1,0:T(8,128)(2,1)S(1)}, u32[]{:S(2)}, u32[]{:S(2)}) %collective-permute-start.2) | collective-permute-done | bytes 196640 | tf_op jit(solution)/shard_map/ppermute | solution.py:157
  91.1 1.5 collective-permute-start.26
  95.4 44.2 %all-gather = s32[16,2,32]{2,1,0:T(2,128)S(1)} all-gather(s32[1,2,32]{2,1,0:T(2,128)S(1)} %bitcast.35), channel_id=1, replica_groups=mesh['seq'=16,'tensor'=2] {'seq'}, dimensions={0}, use_global_device_ids=true | all-gather | bytes 4352 | tf_op jit(solution)/shard_map/all_gather | solution.py:207
  147.6 36.8 %attend_1.1 = (bf16[2,256,128]{2,1,0:T(8,128)(2,1)S(1)}, bf16[2,256,128]{2,1,0:T(8,128)(2,1)S(1)}, bf16[2,256,128]{2,1,0:T(8,128)(2,1)S(1)}, bf16[2,256,128]{2,1,0:T(8,128)(2,1)S(1)}) custom-call(s32[8]{0:T(128)S(1)} %get-tuple-element.69.count_ref, s32[8,36]{1,0:T(8,128)S(1)} %select_reduce_fusion.list_ref, ...), custom_call_target="tpu_custom_call" | custom-call | flops 4294967296 | bytes 5242880 | tf_op jit(solution)/shard_map/attend_1/pallas_call | solution.py:250
  185.6 54.3 %attend_0.1 = (bf16[3,256,128]{2,1,0:T(8,128)(2,1)S(1)}, bf16[3,256,128]{2,1,0:T(8,128)(2,1)S(1)}, bf16[3,256,128]{2,1,0:T(8,128)(2,1)S(1)}, bf16[3,256,128]{2,1,0:T(8,128)(2,1)S(1)}) custom-call(s32[8]{0:T(128)S(1)} %get-tuple-element.69.count_ref, s32[8,36]{1,0:T(8,128)S(1)} %select_reduce_fusion.list_ref, bf16[3,256,128]{2,1,0:T(8,128)(2,1)S(1)} %copy-done.6, ...), custom_call_target="tpu_custom_call" | custom-call | flops 6442450944 | bytes 7864320 | tf_op jit(solution)/shard_map/attend_0/pallas_call | solution.py:250
  242.4 1.9 collective-permute-start.18
  244.9 1.9 collective-permute-start.36
  246.8 21.4 %collective-permute-done.35.refs_6_ = bf16[2,256,128]{2,1,0:T(8,128)(2,1)S(1)} collective-permute-done((bf16[2,256,128]{2,1,0:T(8,128)(2,1)S(1)}, bf16[2,256,128]{2,1,0:T(8,128)(2,1)S(1)}, u32[]{:S(2)}, u32[]{:S(2)}) %collective-permute-start.35) | collective-permute-done | bytes 131104 | tf_op jit(solution)/shard_map/ppermute | solution.py:157
  268.2 1.8 collect.1
  (110 shorter events, 21.9 us)
Async XLA Ops:
  1.6 17.6 %collective-permute-start.28 = (bf16[2,256,128]{2,1,0:T(8,128)(2,1)S(1)}, bf16[2,256,128]{2,1,0:T(8,128)(2,1)S(1)}, u32[]{:S(2)}, u32[]{:S(2)}) collective-permute-start(bf16[2,256,128]{2,1,0:T(8,128)(2,1)S(1)} %get-tuple-element.62), channel_id=1, source_target_pairs={{0,8},{2,10},{4,12},{6,14},{8,16},{10,18},{12,20},{14,22},{16,24},... | collective-permute-start | bytes 393224 | tf_op jit(solution)/shard_map/ppermute | solution.py:157
  10.1 11.7 %collective-permute-start.29 = (bf16[2,256,128]{2,1,0:T(8,128)(2,1)S(1)}, bf16[2,256,128]{2,1,0:T(8,128)(2,1)S(1)}, u32[]{:S(2)}, u32[]{:S(2)}) collective-permute-start(bf16[2,256,128]{2,1,0:T(8,128)(2,1)S(1)} %get-tuple-element.63), channel_id=1, source_target_pairs={{0,16},{2,18},{4,20},{6,22},{8,24},{10,26},{12,28},{14,30},{16,0},... | collective-permute-start | bytes 393224 | tf_op jit(solution)/shard_map/ppermute | solution.py:157
  12.7 10.3 %collective-permute-start.30 = (bf16[2,256,128]{2,1,0:T(8,128)(2,1)S(1)}, bf16[2,256,128]{2,1,0:T(8,128)(2,1)S(1)}, u32[]{:S(2)}, u32[]{:S(2)}) collective-permute-start(bf16[2,256,128]{2,1,0:T(8,128)(2,1)S(1)} %get-tuple-element.64), channel_id=1, source_target_pairs={{0,24},{2,26},{4,28},{6,30},{8,0},{10,2},{12,4},{14,6},{16,8},{18,... | collective-permute-start | bytes 393224 | tf_op jit(solution)/shard_map/ppermute | solution.py:157
  16.7 13.2 %collective-permute-start.22 = (bf16[2,256,128]{2,1,0:T(8,128)(2,1)S(1)}, bf16[2,256,128]{2,1,0:T(8,128)(2,1)S(1)}, u32[]{:S(2)}, u32[]{:S(2)}) collective-permute-start(bf16[2,256,128]{2,1,0:T(8,128)(2,1)S(1)} %get-tuple-element.58), channel_id=1, source_target_pairs={{0,8},{2,10},{4,12},{6,14},{8,16},{10,18},{12,20},{14,22},{16,24},... | collective-permute-start | bytes 393224 | tf_op jit(solution)/shard_map/ppermute | solution.py:157
  17.9 21.7 %collective-permute-start.23 = (bf16[2,256,128]{2,1,0:T(8,128)(2,1)S(1)}, bf16[2,256,128]{2,1,0:T(8,128)(2,1)S(1)}, u32[]{:S(2)}, u32[]{:S(2)}) collective-permute-start(bf16[2,256,128]{2,1,0:T(8,128)(2,1)S(1)} %get-tuple-element.59), channel_id=1, source_target_pairs={{0,16},{2,18},{4,20},{6,22},{8,24},{10,26},{12,28},{14,30},{16,0},... | collective-permute-start | bytes 393224 | tf_op jit(solution)/shard_map/ppermute | solution.py:157
  19.2 22.3 %collective-permute-start.24 = (bf16[2,256,128]{2,1,0:T(8,128)(2,1)S(1)}, bf16[2,256,128]{2,1,0:T(8,128)(2,1)S(1)}, u32[]{:S(2)}, u32[]{:S(2)}) collective-permute-start(bf16[2,256,128]{2,1,0:T(8,128)(2,1)S(1)} %get-tuple-element.60), channel_id=1, source_target_pairs={{0,24},{2,26},{4,28},{6,30},{8,0},{10,2},{12,4},{14,6},{16,8},{18,... | collective-permute-start | bytes 393224 | tf_op jit(solution)/shard_map/ppermute | solution.py:157
  21.8 44.5 %collective-permute-start.10 = (bf16[3,256,128]{2,1,0:T(8,128)(2,1)S(1)}, bf16[3,256,128]{2,1,0:T(8,128)(2,1)S(1)}, u32[]{:S(2)}, u32[]{:S(2)}) collective-permute-start(bf16[3,256,128]{2,1,0:T(8,128)(2,1)S(1)} %get-tuple-element.46), channel_id=1, source_target_pairs={{0,8},{2,10},{4,12},{6,14},{8,16},{10,18},{12,20},{14,22},{16,24},... | collective-permute-start | bytes 589832 | tf_op jit(solution)/shard_map/ppermute | solution.py:157
  23.0 43.4 %collective-permute-start.11 = (bf16[3,256,128]{2,1,0:T(8,128)(2,1)S(1)}, bf16[3,256,128]{2,1,0:T(8,128)(2,1)S(1)}, u32[]{:S(2)}, u32[]{:S(2)}) collective-permute-start(bf16[3,256,128]{2,1,0:T(8,128)(2,1)S(1)} %get-tuple-element.47), channel_id=1, source_target_pairs={{0,16},{2,18},{4,20},{6,22},{8,24},{10,26},{12,28},{14,30},{16,0},... | collective-permute-start | bytes 589832 | tf_op jit(solution)/shard_map/ppermute | solution.py:157
  29.9 38.0 %collective-permute-start.12 = (bf16[3,256,128]{2,1,0:T(8,128)(2,1)S(1)}, bf16[3,256,128]{2,1,0:T(8,128)(2,1)S(1)}, u32[]{:S(2)}, u32[]{:S(2)}) collective-permute-start(bf16[3,256,128]{2,1,0:T(8,128)(2,1)S(1)} %get-tuple-element.48), channel_id=1, source_target_pairs={{0,24},{2,26},{4,28},{6,30},{8,0},{10,2},{12,4},{14,6},{16,8},{18,... | collective-permute-start | bytes 589832 | tf_op jit(solution)/shard_map/ppermute | solution.py:157
  41.5 24.8 %collective-permute-start.20 = (bf16[2,256,128]{2,1,0:T(8,128)(2,1)S(1)}, bf16[2,256,128]{2,1,0:T(8,128)(2,1)S(1)}, u32[]{:S(2)}, u32[]{:S(2)}) collective-permute-start(bf16[2,256,128]{2,1,0:T(8,128)(2,1)S(1)} %get-tuple-element.55), channel_id=1, source_target_pairs={{0,16},{2,18},{4,20},{6,22},{8,24},{10,26},{12,28},{14,30},{16,0},... | collective-permute-start | bytes 393224 | tf_op jit(solution)/shard_map/ppermute | solution.py:157
  49.7 18.3 %collective-permute-start.4 = (bf16[3,256,128]{2,1,0:T(8,128)(2,1)S(1)}, bf16[3,256,128]{2,1,0:T(8,128)(2,1)S(1)}, u32[]{:S(2)}, u32[]{:S(2)}) collective-permute-start(bf16[3,256,128]{2,1,0:T(8,128)(2,1)S(1)} %get-tuple-element.42), channel_id=1, source_target_pairs={{0,8},{2,10},{4,12},{6,14},{8,16},{10,18},{12,20},{14,22},{16,24},... | collective-permute-start | bytes 589832 | tf_op jit(solution)/shard_map/ppermute | solution.py:157
  66.3 14.0 %collective-permute-start.6 = (bf16[3,256,128]{2,1,0:T(8,128)(2,1)S(1)}, bf16[3,256,128]{2,1,0:T(8,128)(2,1)S(1)}, u32[]{:S(2)}, u32[]{:S(2)}) collective-permute-start(bf16[3,256,128]{2,1,0:T(8,128)(2,1)S(1)} %get-tuple-element.44), channel_id=1, source_target_pairs={{0,24},{2,26},{4,28},{6,30},{8,0},{10,2},{12,4},{14,6},{16,8},{18,... | collective-permute-start | bytes 589832 | tf_op jit(solution)/shard_map/ppermute | solution.py:157
  66.3 26.3 %collective-permute-start.32 = (bf16[4,2,256,128]{3,2,1,0:T(8,128)(2,1)S(1)}, bf16[4,2,256,128]{3,2,1,0:T(8,128)(2,1)}, u32[]{:S(2)}, u32[]{:S(2)}) collective-permute-start(bf16[4,2,256,128]{3,2,1,0:T(8,128)(2,1)S(1)} %pad_maximum_fusion.3.refs_8_), channel_id=1, source_target_pairs={{0,4},{2,6},{4,0},{6,2},{8,12},{10,14},{12,8},{14,10},{16,20},{18,... | collective-permute-start | bytes 1572872 | tf_op jit(solution)/shard_map/ppermute | solution.py:160
  67.9 24.7 %collective-permute-start.31 = (bf16[4,2,256,128]{3,2,1,0:T(8,128)(2,1)S(1)}, bf16[4,2,256,128]{3,2,1,0:T(8,128)(2,1)S(1)}, u32[]{:S(2)}, u32[]{:S(2)}) collective-permute-start(bf16[4,2,256,128]{3,2,1,0:T(8,128)(2,1)S(1)} %pad_maximum_fusion.3.refs_8_), channel_id=1, source_target_pairs={{0,2},{2,0},{4,6},{6,4},{8,10},{10,8},{12,14},{14,12},{16,18},{18,... | collective-permute-start | bytes 1572872 | tf_op jit(solution)/shard_map/ppermute | solution.py:160
  68.0 15.9 %collective-permute-start.1 = (bf16[3,256,128]{2,1,0:T(8,128)(2,1)S(1)}, bf16[3,256,128]{2,1,0:T(8,128)(2,1)S(1)}, u32[]{:S(2)}, u32[]{:S(2)}) collective-permute-start(bf16[3,256,128]{2,1,0:T(8,128)(2,1)S(1)} %get-tuple-element.38), channel_id=1, source_target_pairs={{0,8},{2,10},{4,12},{6,14},{8,16},{10,18},{12,20},{14,22},{16,24},... | collective-permute-start | bytes 589832 | tf_op jit(solution)/shard_map/ppermute | solution.py:157
  80.2 10.2 %collective-permute-start.2 = (bf16[3,256,128]{2,1,0:T(8,128)(2,1)S(1)}, bf16[3,256,128]{2,1,0:T(8,128)(2,1)S(1)}, u32[]{:S(2)}, u32[]{:S(2)}) collective-permute-start(bf16[3,256,128]{2,1,0:T(8,128)(2,1)S(1)} %get-tuple-element.39), channel_id=1, source_target_pairs={{0,16},{2,18},{4,20},{6,22},{8,24},{10,26},{12,28},{14,30},{16,0},... | collective-permute-start | bytes 589832 | tf_op jit(solution)/shard_map/ppermute | solution.py:157
  81.8 58.4 %collective-permute-start.14 = (bf16[4,3,256,128]{3,2,1,0:T(8,128)(2,1)S(1)}, bf16[4,3,256,128]{3,2,1,0:T(8,128)(2,1)}, u32[]{:S(2)}, u32[]{:S(2)}) collective-permute-start(bf16[4,3,256,128]{3,2,1,0:T(8,128)(2,1)S(1)} %pad_maximum_fusion.1.refs_8_), channel_id=1, source_target_pairs={{0,4},{2,6},{4,0},{6,2},{8,12},{10,14},{12,8},{14,10},{16,20},{18,... | collective-permute-start | bytes 2359304 | tf_op jit(solution)/shard_map/ppermute | solution.py:160
  83.9 56.6 %collective-permute-start.8 = (bf16[4,3,256,128]{3,2,1,0:T(8,128)(2,1)S(1)}, bf16[4,3,256,128]{3,2,1,0:T(8,128)(2,1)S(1)}, u32[]{:S(2)}, u32[]{:S(2)}) collective-permute-start(bf16[4,3,256,128]{3,2,1,0:T(8,128)(2,1)S(1)} %pad_maximum_fusion.refs_4_), channel_id=1, source_target_pairs={{0,4},{2,6},{4,0},{6,2},{8,12},{10,14},{12,8},{14,10},{16,20},{18,... | collective-permute-start | bytes 2359304 | tf_op jit(solution)/shard_map/ppermute | solution.py:160
  91.1 48.5 %collective-permute-start.26 = (bf16[4,2,256,128]{3,2,1,0:T(8,128)(2,1)S(1)}, bf16[4,2,256,128]{3,2,1,0:T(8,128)(2,1)}, u32[]{:S(2)}, u32[]{:S(2)}) collective-permute-start(bf16[4,2,256,128]{3,2,1,0:T(8,128)(2,1)S(1)} %pad_maximum_fusion.2.refs_4_), channel_id=1, source_target_pairs={{0,4},{2,6},{4,0},{6,2},{8,12},{10,14},{12,8},{14,10},{16,20},{18,... | collective-permute-start | bytes 1572872 | tf_op jit(solution)/shard_map/ppermute | solution.py:160
  92.7 47.4 %collective-permute-start.25 = (bf16[4,2,256,128]{3,2,1,0:T(8,128)(2,1)S(1)}, bf16[4,2,256,128]{3,2,1,0:T(8,128)(2,1)}, u32[]{:S(2)}, u32[]{:S(2)}) collective-permute-start(bf16[4,2,256,128]{3,2,1,0:T(8,128)(2,1)S(1)} %pad_maximum_fusion.2.refs_4_), channel_id=1, source_target_pairs={{0,2},{2,0},{4,6},{6,4},{8,10},{10,8},{12,14},{14,12},{16,18},{18,... | collective-permute-start | bytes 1572872 | tf_op jit(solution)/shard_map/ppermute | solution.py:160
  93.5 47.3 %collective-permute-start.33 = (bf16[4,2,256,128]{3,2,1,0:T(8,128)(2,1)}, bf16[4,2,256,128]{3,2,1,0:T(8,128)(2,1)}, u32[]{:S(2)}, u32[]{:S(2)}) collective-permute-start(bf16[4,2,256,128]{3,2,1,0:T(8,128)(2,1)} %collective-permute-done.32.refs_10_), channel_id=1, source_target_pairs={{0,2},{2,0},{4,6},{6,4},{8,10},{10,8},{12,14},{14,12},{16,18},{18,... | collective-permute-start | bytes 1572872 | tf_op jit(solution)/shard_map/ppermute | solution.py:160
  139.6 45.9 %collective-permute-start.13 = (bf16[4,3,256,128]{3,2,1,0:T(8,128)(2,1)S(1)}, bf16[4,3,256,128]{3,2,1,0:T(8,128)(2,1)}, u32[]{:S(2)}, u32[]{:S(2)}) collective-permute-start(bf16[4,3,256,128]{3,2,1,0:T(8,128)(2,1)S(1)} %pad_maximum_fusion.1.refs_8_), channel_id=1, source_target_pairs={{0,2},{2,0},{4,6},{6,4},{8,10},{10,8},{12,14},{14,12},{16,18},{18,... | collective-permute-start | bytes 2359304 | tf_op jit(solution)/shard_map/ppermute | solution.py:160
  140.0 45.5 %collective-permute-start.7 = (bf16[4,3,256,128]{3,2,1,0:T(8,128)(2,1)S(1)}, bf16[4,3,256,128]{3,2,1,0:T(8,128)(2,1)}, u32[]{:S(2)}, u32[]{:S(2)}) collective-permute-start(bf16[4,3,256,128]{3,2,1,0:T(8,128)(2,1)S(1)} %pad_maximum_fusion.refs_4_), channel_id=1, source_target_pairs={{0,2},{2,0},{4,6},{6,4},{8,10},{10,8},{12,14},{14,12},{16,18},{18,... | collective-permute-start | bytes 2359304 | tf_op jit(solution)/shard_map/ppermute | solution.py:160
  140.5 45.0 %collective-permute-start.15 = (bf16[4,3,256,128]{3,2,1,0:T(8,128)(2,1)}, bf16[4,3,256,128]{3,2,1,0:T(8,128)(2,1)}, u32[]{:S(2)}, u32[]{:S(2)}) collective-permute-start(bf16[4,3,256,128]{3,2,1,0:T(8,128)(2,1)} %collective-permute-done.14.refs_10_), channel_id=1, source_target_pairs={{0,2},{2,0},{4,6},{6,4},{8,10},{10,8},{12,14},{14,12},{16,18},{18,... | collective-permute-start | bytes 2359304 | tf_op jit(solution)/shard_map/ppermute | solution.py:160
  140.7 44.8 %collective-permute-start.9 = (bf16[4,3,256,128]{3,2,1,0:T(8,128)(2,1)S(1)}, bf16[4,3,256,128]{3,2,1,0:T(8,128)(2,1)}, u32[]{:S(2)}, u32[]{:S(2)}) collective-permute-start(bf16[4,3,256,128]{3,2,1,0:T(8,128)(2,1)S(1)} %collective-permute-done.8.refs_6_), channel_id=1, source_target_pairs={{0,2},{2,0},{4,6},{6,4},{8,10},{10,8},{12,14},{14,12},{16,18},{18,... | collective-permute-start | bytes 2359304 | tf_op jit(solution)/shard_map/ppermute | solution.py:160
  143.8 40.5 %collective-permute-start.3 = (bf16[3,256,128]{2,1,0:T(8,128)(2,1)}, bf16[3,256,128]{2,1,0:T(8,128)(2,1)S(1)}, u32[]{:S(2)}, u32[]{:S(2)}) collective-permute-start(bf16[3,256,128]{2,1,0:T(8,128)(2,1)} %copy-done.7), channel_id=1, source_target_pairs={{0,24},{2,26},{4,28},{6,30},{8,0},{10,2},{12,4},{14,6},{16,8},{18,... | collective-permute-start | bytes 589832 | tf_op jit(solution)/shard_map/ppermute | solution.py:157
  184.4 60.5 %collective-permute-start.34 = (bf16[2,256,128]{2,1,0:T(8,128)(2,1)S(1)}, bf16[2,256,128]{2,1,0:T(8,128)(2,1)S(1)}, u32[]{:S(2)}, u32[]{:S(2)}) collective-permute-start(bf16[2,256,128]{2,1,0:T(8,128)(2,1)S(1)} %get-tuple-element.66), channel_id=1, source_target_pairs={{0,24},{2,26},{4,28},{6,30},{8,0},{10,2},{12,4},{14,6},{16,8},{18,... | collective-permute-start | bytes 393224 | tf_op jit(solution)/shard_map/ppermute | solution.py:157
  239.9 28.3 %collective-permute-start.16 = (bf16[3,256,128]{2,1,0:T(8,128)(2,1)S(1)}, bf16[3,256,128]{2,1,0:T(8,128)(2,1)S(1)}, u32[]{:S(2)}, u32[]{:S(2)}) collective-permute-start(bf16[3,256,128]{2,1,0:T(8,128)(2,1)S(1)} %get-tuple-element.50), channel_id=1, source_target_pairs={{0,24},{2,26},{4,28},{6,30},{8,0},{10,2},{12,4},{14,6},{16,8},{18,... | collective-permute-start | bytes 589832 | tf_op jit(solution)/shard_map/ppermute | solution.py:157
  241.1 27.1 %collective-permute-start.17 = (bf16[3,256,128]{2,1,0:T(8,128)(2,1)S(1)}, bf16[3,256,128]{2,1,0:T(8,128)(2,1)S(1)}, u32[]{:S(2)}, u32[]{:S(2)}) collective-permute-start(bf16[3,256,128]{2,1,0:T(8,128)(2,1)S(1)} %get-tuple-element.51), channel_id=1, source_target_pairs={{0,16},{2,18},{4,20},{6,22},{8,24},{10,26},{12,28},{14,30},{16,0},... | collective-permute-start | bytes 589832 | tf_op jit(solution)/shard_map/ppermute | solution.py:157
  242.4 25.9 %collective-permute-start.18 = (bf16[3,256,128]{2,1,0:T(8,128)(2,1)S(1)}, bf16[3,256,128]{2,1,0:T(8,128)(2,1)S(1)}, u32[]{:S(2)}, u32[]{:S(2)}) collective-permute-start(bf16[3,256,128]{2,1,0:T(8,128)(2,1)S(1)} %get-tuple-element.52), channel_id=1, source_target_pairs={{0,8},{2,10},{4,12},{6,14},{8,16},{10,18},{12,20},{14,22},{16,24},... | collective-permute-start | bytes 589832 | tf_op jit(solution)/shard_map/ppermute | solution.py:157
  244.3 23.9 %collective-permute-start.35 = (bf16[2,256,128]{2,1,0:T(8,128)(2,1)S(1)}, bf16[2,256,128]{2,1,0:T(8,128)(2,1)S(1)}, u32[]{:S(2)}, u32[]{:S(2)}) collective-permute-start(bf16[2,256,128]{2,1,0:T(8,128)(2,1)S(1)} %get-tuple-element.67), channel_id=1, source_target_pairs={{0,16},{2,18},{4,20},{6,22},{8,24},{10,26},{12,28},{14,30},{16,0},... | collective-permute-start | bytes 393224 | tf_op jit(solution)/shard_map/ppermute | solution.py:157
  244.9 23.3 %collective-permute-start.36 = (bf16[2,256,128]{2,1,0:T(8,128)(2,1)S(1)}, bf16[2,256,128]{2,1,0:T(8,128)(2,1)S(1)}, u32[]{:S(2)}, u32[]{:S(2)}) collective-permute-start(bf16[2,256,128]{2,1,0:T(8,128)(2,1)S(1)} %get-tuple-element.68), channel_id=1, source_target_pairs={{0,8},{2,10},{4,12},{6,14},{8,16},{10,18},{12,20},{14,22},{16,24},... | collective-permute-start | bytes 393224 | tf_op jit(solution)/shard_map/ppermute | solution.py:157
  (26 other events, 447.1 us)

commit v2 on v0

--- a/solution.py
+++ b/solution.py
@@ -1,16 +1,275 @@
+import functools
 import math
 
 import jax
 import jax.numpy as jnp
 from jax import lax
+from jax.experimental import pallas as pl
+from jax.experimental.pallas import tpu as pltpu
 from jax.sharding import PartitionSpec as P
 
 HEAD_DIM = 128
 BLOCK = 128
-
-
 epsilon = 1e-06
 blocked = -1e30
+MASK_ROWS = 16
+MIB = 1024 * 1024
+VMEM = pl.BlockSpec(memory_space=pltpu.VMEM)
+SMEM = pl.BlockSpec(memory_space=pltpu.SMEM)
+ANY = pl.BlockSpec(memory_space=pl.ANY)
+
+
+def column_of(place_ref, shift, head, groups, per_group):
+    group = lax.rem(place_ref[0] + shift, groups)
+    return pl.multiple_of((group * per_group + head) * HEAD_DIM, HEAD_DIM)
+
+
+def value_kernel(place_ref, v_ref, mask_ref, *outs, per_group):
+    groups = len(outs)
+    rows = v_ref.shape[0]
+    for shift, out in enumerate(outs):
+        for head in range(per_group):
+            column = column_of(place_ref, shift, head, groups, per_group)
+            out[head * rows : (head + 1) * rows, :] = v_ref[:, pl.ds(column, HEAD_DIM)]
+        out[per_group * rows :, :] = mask_ref[...]
+
+
+def square_sums_kernel(q_ref, k_ref, out_ref):
+    q, k = q_ref[...], k_ref[...]
+    out_ref[:, 0:1] = jnp.sum(q * q, axis=1, keepdims=True)
+    out_ref[:, 1:2] = jnp.sum(k * k, axis=1, keepdims=True)
+
+
+def normed_columns(x_ref, inverse, gain_ref, column):
+    here = pl.ds(column, HEAD_DIM)
+    return (x_ref[:, here] * inverse * gain_ref[:, here]).astype(jnp.bfloat16)
+
+
+def key_kernel(place_ref, sums_ref, k_ref, gain_ref, *outs, per_group, full_width):
+    groups = len(outs)
+    rows = k_ref.shape[0]
+    inverse = 1.0 / jnp.sqrt(sums_ref[:, 1:2] / full_width + epsilon)
+    for shift, out in enumerate(outs):
+        for head in range(per_group):
+            column = column_of(place_ref, shift, head, groups, per_group)
+            x = normed_columns(k_ref, inverse, gain_ref, column)
+            for b in range(rows // BLOCK):
+                low = head * rows + b * HEAD_DIM
+                out[low : low + HEAD_DIM, :] = x[b * BLOCK : (b + 1) * BLOCK].T
+
+
+def query_kernel(place_ref, sums_ref, q_ref, gain_ref, _, *outs, per_group, full_width):
+    groups = len(outs)
+    rows = q_ref.shape[0]
+    inverse = 1.0 / jnp.sqrt(sums_ref[:, 0:1] / full_width + epsilon)
+    for shift, out in enumerate(outs):
+        for head in range(per_group):
+            column = column_of(place_ref, shift, head, groups, per_group)
+            out[head * rows : (head + 1) * rows, :] = normed_columns(
+                q_ref, inverse, gain_ref, column
+            )
+
+
+def attend_kernel(bias_ref, q_ref, *refs, slot_of_queries, groups, layers, scale):
+    k_refs, v_refs = refs[:layers], refs[layers : 2 * layers]
+    out, scores = refs[-2:]
+    rows = q_ref.shape[0]
+    blk = rows // BLOCK
+    slots = groups * layers
+    q = q_ref[...]
+    top = jnp.full((rows, BLOCK), blocked, jnp.float32)
+    for slot in range(slots):
+        keys = k_refs[slot // groups][slot % groups]
+        for b in range(blk):
+            block = jnp.dot(
+                q, keys[b * HEAD_DIM : (b + 1) * HEAD_DIM], preferred_element_type=jnp.float32
+            )
+            first = (slot_of_queries * slots + slot) * blk
+            block = jnp.concatenate(
+                [
+                    block[a * BLOCK : (a + 1) * BLOCK] + bias_ref[(first + a) * blk + b]
+                    for a in range(blk)
+                ],
+                axis=0,
+            )
+            scores[slot, :, b * BLOCK : (b + 1) * BLOCK] = block
+            top = jnp.maximum(top, block)
+    row_max = jnp.max(top, axis=1, keepdims=True)
+    total = mixed = jnp.zeros((rows, BLOCK), jnp.float32)
+    for slot in range(slots):
+        weights = jnp.exp2((scores[slot] - row_max) * scale)
+        for b in range(blk):
+            total = total + weights[:, b * BLOCK : (b + 1) * BLOCK]
+        mixed = mixed + jnp.dot(
+            weights.astype(jnp.bfloat16),
+            v_refs[slot // groups][slot % groups],
+            preferred_element_type=jnp.float32,
+        )
+    out[...] = (mixed / jnp.sum(total, axis=1, keepdims=True)).astype(jnp.bfloat16)
+
+
+def collect_kernel(place_ref, *refs, per_group):
+    out = refs[-1]
+    groups = len(refs) - 1
+    rows = out.shape[0]
+    for shift in range(groups):
+        for head in range(per_group):
+            column = column_of(place_ref, shift, head, groups, per_group)
+            piece = refs[shift][head * rows : (head + 1) * rows, :]
+            out[:, pl.ds(column, HEAD_DIM)] = piece.astype(jnp.float32)
+
+
+def exchanged(q_in, k_in, v_in, q_gain, k_gain, frames, adjacent, *, groups):
+    rows, width = q_in.shape
+    devices = lax.axis_size("seq")
+    tensors = lax.axis_size("tensor")
+    layers = devices // groups
+    blk = rows // BLOCK
+    blocks = devices * blk
+    per_group = width // HEAD_DIM // groups
+    me = lax.axis_index("seq")
+    place, spot = me // layers, lax.rem(me, layers)
+    place_row = place.reshape(1).astype(jnp.int32)
+    f32, bf16 = jnp.float32, jnp.bfloat16
+    params = pltpu.CompilerParams(vmem_limit_bytes=48 * MIB)
+    def rotated(x, shift):
+        pairs = [
+            (z * layers + r, (z + shift) % groups * layers + r)
+            for z in range(groups)
+            for r in range(layers)
+        ]
+        return lax.ppermute(x, "seq", pairs)
+
+    def exchange(pieces):
+        return [pieces[0]] + [rotated(pieces[s], s) for s in range(1, groups)]
+
+    def swapped(x, bit):
+        return lax.ppermute(x, "seq", [(i, i ^ bit) for i in range(devices)])
+
+    own_frames = lax.dynamic_slice_in_dim(frames, me * blk, blk, 0)
+    gap = jnp.abs(own_frames[:, None] - frames[None, :])
+    allowed = ((gap == 0) | (gap == 1) & (adjacent == 1)).astype(bf16)
+    mask_rows = jnp.pad(allowed, ((0, MASK_ROWS - blk), (0, BLOCK - blocks)))
+
+    v_pieces = pl.pallas_call(
+        functools.partial(value_kernel, per_group=per_group),
+        out_shape=[jax.ShapeDtypeStruct((per_group * rows + MASK_ROWS, HEAD_DIM), bf16)] * groups,
+        in_specs=[SMEM, VMEM, VMEM],
+        out_specs=[VMEM] * groups,
+        compiler_params=params,
+        name="value_pieces",
+    )(place_row, v_in, mask_rows)
+    q_in, k_in, v_pieces = lax.optimization_barrier((q_in, k_in, v_pieces))
+    sums = pl.pallas_call(
+        square_sums_kernel,
+        out_shape=jax.ShapeDtypeStruct((rows, 2), f32),
+        in_specs=[VMEM, VMEM],
+        out_specs=VMEM,
+        compiler_params=params,
+        name="square_sums",
+    )(q_in, k_in)
+    v_arrived = exchange(v_pieces)
+    if tensors == 2:
+        sums = sums + lax.ppermute(sums, "tensor", [(0, 1), (1, 0)])
+    else:
+        sums = lax.psum(sums, "tensor")
+
+    normed = dict(per_group=per_group, full_width=float(width * tensors))
+    k_arrived = exchange(
+        pl.pallas_call(
+            functools.partial(key_kernel, **normed),
+            out_shape=[jax.ShapeDtypeStruct((per_group * rows, HEAD_DIM), bf16)] * groups,
+            in_specs=[SMEM] + [VMEM] * 3,
+            out_specs=[VMEM] * groups,
+            compiler_params=params,
+            name="key_pieces",
+        )(place_row, sums, k_in, k_gain.reshape(1, width))
+    )
+    v_stack = jnp.stack([x[: per_group * rows] for x in v_arrived])
+    q_arrived = exchange(
+        pl.pallas_call(
+            functools.partial(query_kernel, **normed),
+            out_shape=[jax.ShapeDtypeStruct((per_group * rows, HEAD_DIM), bf16)] * groups,
+            in_specs=[SMEM] + [VMEM] * 3 + [ANY],
+            out_specs=[VMEM] * groups,
+            compiler_params=params,
+            name="query_pieces",
+        )(place_row, sums, q_in, q_gain.reshape(1, width), v_stack)
+    )
+
+    def spread(parts, bit):
+        return parts | {have ^ bit: swapped(part, bit) for have, part in parts.items()}
+
+    bits = [1 << i for i in reversed(range(layers.bit_length() - 1))]
+    values, keys = {0: v_stack}, {}
+    for bit in bits:
+        values = spread(values, bit)
+        if bit == bits[0]:
+            k_arrived, values = lax.optimization_barrier((k_arrived, values))
+            keys = {0: jnp.stack(k_arrived)}
+    for bit in bits:
+        keys = spread(keys, bit)
+        if bit == bits[0]:
+            q_arrived, keys = lax.optimization_barrier((q_arrived, keys))
+    values = [values[i] for i in range(layers)]
+    keys = [keys[i] for i in range(layers)]
+
+    low = per_group * rows
+    known = jnp.stack([x[low : low + blk, :blocks] for x in v_arrived]).astype(f32)
+    z_order = lax.rem(place - jnp.arange(groups) + groups, groups)
+    layer_order = jnp.bitwise_xor(spot, jnp.arange(layers))
+    key_blocks = (
+        (z_order[None, :, None] * layers + layer_order[:, None, None]) * blk
+        + jnp.arange(blk)[None, None, :]
+    ).reshape(-1)
+    key_hot = (key_blocks[:, None] == jnp.arange(blocks)[None, :]).astype(f32)
+    table = jnp.einsum("gab,kb->gak", known, key_hot).reshape(groups, blk, devices, blk)
+    bias = jnp.where(table > 0.5, 0.0, blocked).astype(f32).transpose(0, 2, 1, 3).reshape(-1)
+
+    scale = math.log2(math.e) / math.sqrt(HEAD_DIM)
+    big = pl.BlockSpec((groups, rows, HEAD_DIM), lambda h, *_: (0, h, 0))
+    small = pl.BlockSpec((rows, HEAD_DIM), lambda h, *_: (h, 0))
+
+    def attend(g, bias):
+        return pl.pallas_call(
+            functools.partial(
+                attend_kernel, slot_of_queries=g, groups=groups, layers=layers, scale=scale
+            ),
+            grid_spec=pltpu.PrefetchScalarGridSpec(
+                num_scalar_prefetch=1,
+                grid=(per_group,),
+                in_specs=[small] + [big] * (2 * layers),
+                out_specs=small,
+                scratch_shapes=[pltpu.VMEM((devices, rows, rows), f32)],
+            ),
+            out_shape=jax.ShapeDtypeStruct((per_group * rows, HEAD_DIM), bf16),
+            compiler_params=params,
+            cost_estimate=pl.CostEstimate(
+                flops=per_group * rows * devices * rows * HEAD_DIM * 4,
+                bytes_accessed=per_group * devices * rows * HEAD_DIM * 5,
+                transcendentals=per_group * rows * devices * rows,
+            ),
+            name=f"attend_{g}",
+        )(bias, q_arrived[g], *keys, *values)
+
+    outputs = [None] * groups
+    for g in [*range(1, groups), 0]:
+        own = attend(g, bias)
+        outputs[g] = rotated(own, groups - g) if g else own
+        if g:
+            earlier = [outputs[g - 1]] if g > 1 else []
+            own, bias, earlier = lax.optimization_barrier((own, bias, earlier))
+            if g > 1:
+                outputs[g - 1] = earlier[0]
+
+    return pl.pallas_call(
+        functools.partial(collect_kernel, per_group=per_group),
+        out_shape=jax.ShapeDtypeStruct((rows, width), f32),
+        in_specs=[SMEM] + [VMEM] * groups,
+        out_specs=VMEM,
+        compiler_params=params,
+        name="collect",
+    )(place_row, *outputs)
 
 
 def normalized(inputs, gain_row, square_sum, full_width):
@@ -87,19 +346,32 @@
     return (accumulated / totals.T[:, :, None]).reshape(tok_rows, width_dev)
 
 
+def groups_of(mesh, heads):
+    layers = 4
+    groups = mesh.shape["seq"] // layers
+    fits = mesh.shape["seq"] % layers == 0 and heads % groups == 0 and heads >= 2 * groups
+    return groups if fits else 1
+
+
 def solution(mesh):
-    return jax.shard_map(
-        shards,
-        mesh=mesh,
-        in_specs=(
-            P("seq", "tensor"),
-            P("seq", "tensor"),
-            P("seq", "tensor"),
-            P("tensor"),
-            P("tensor"),
-            P(),
-            P("seq", None),
-        ),
-        out_specs=P("seq", "tensor"),
-        check_vma=False,
-    )
+    def step(q_in, k_in, v_in, q_gain, k_gain, frames, adjacent):
+        heads = q_in.shape[1] // mesh.shape["tensor"] // HEAD_DIM
+        groups = groups_of(mesh, heads)
+        body = shards if groups == 1 else functools.partial(exchanged, groups=groups)
+        return jax.shard_map(
+            body,
+            mesh=mesh,
+            in_specs=(
+                P("seq", "tensor"),
+                P("seq", "tensor"),
+                P("seq", "tensor"),
+                P("tensor"),
+                P("tensor"),
+                P(),
+                P("seq", None),
+            ),
+            out_specs=P("seq", "tensor"),
+            check_vma=False,
+        )(q_in, k_in, v_in, q_gain, k_gain, frames, adjacent)
+
+    return step

time: 366 us -> 171 us (0.47)
  waiting for transfers between devices: 171 us -> 70.2 us
  local copies, waits for them, and re-layouts: 89.5 us -> 9.89 us
  matrix products: 69.7 us -> 0.19 us
  Pallas kernels: 0 us -> 52.8 us
  starting transfers between devices: 0.04 us -> 35.7 us
  between operations: 13.5 us -> 0.28 us
  other arithmetic: 13.2 us -> 1.27 us
  blocking collectives: 5.84 us -> 0 us
    all_gather x2 -> x0, waiting for transfers between devices: 171 us -> none  [the longest x1 108 us: shards(): key_piece = lax.all_gather(k_norm, 'seq', axis=0, tiled=True)]
    ppermute x0 -> x19, waiting for transfers between devices: none -> 70.2 us  [the longest x12 65.7 us: rotated(): return lax.ppermute(x, 'seq', pairs)]
    dot_general x48 -> x1, matrix products: 69.7 us -> 0.19 us  [exchanged(): jnp.einsum('gab,kb->gak', known, key_hot).reshape(groups, blk, devices, blk)]
    dynamic_slice x65 -> x1, local copies, waits for them, and re-layouts: 59 us -> 0.73 us  [exchanged(): own_frames = lax.dynamic_slice_in_dim(frames, me * blk, blk, 0)]
    pallas_call x0 -> x9, Pallas kernels: none -> 52.8 us  [the longest x4 49.3 us: attend(): pl.pallas_call(functools.partial(attend_kernel, slot_of_queries=g, groups...]
    ppermute x0 -> x19, starting transfers between devices: none -> 35.7 us  [the longest x12 30.5 us: rotated(): return lax.ppermute(x, 'seq', pairs)]
    broadcast_in_dim x64 -> x0, local copies, waits for them, and re-layouts: 9.93 us -> none  [masked_scores(): jnp.where(allowed_here[None, :, None, :, None], tiled_scores, blocked)]
    while x96 -> x0, local copies, waits for them, and re-layouts: 6.65 us -> none
  transfers between devices with their start and end apart: 2 -> 19, of which waited for: 2 -> 10; matrix products, arithmetic and copies ran while one was open for 17% -> 2% of each run, Pallas kernels for 0% -> 23%
where the time goes in v2:
time: 171 us; the launch traced here: 170 us
  waiting for transfers between devices  70.2 us (41%)
  Pallas kernels  52.8 us (31%)
  starting transfers between devices  35.7 us (21%)
  local copies, waits for them, and re-layouts  9.89 us (6%)
    ppermute x12, waiting for transfers between devices, rotated(): return lax.ppermute(x, 'seq', pairs)  65.7 us
    pallas_call x4, Pallas kernels, attend(): pl.pallas_call(functools.partial(attend_kernel, slot_of_queries=g, groups...  49.3 us
    ppermute x12, starting transfers between devices, rotated(): return lax.ppermute(x, 'seq', pairs)  30.5 us
    unnamed x28, local copies, waits for them, and re-layouts  5.66 us
    ppermute x6, starting transfers between devices, swapped(): return lax.ppermute(x, 'seq', [(i, i ^ bit) for i in range(devices)])  3.68 us
    ppermute x1, waiting for transfers between devices, exchanged(): sums = sums + lax.ppermute(sums, 'tensor', [(0, 1), (1, 0)])  3.46 us
  transfers between devices with their start and end apart: 19, of which 10 were waited for; matrix products, arithmetic and copies ran while one was open for 2% of the time, Pallas kernels for 23%

profile of v2, /device:TPU:0, one launch (start us, length us, event | category | flops | bytes accessed | tf_op | source)
XLA Modules:
  0.0 170.3 jit_solution(11385386589120674417)
XLA Ops:
  0.0 0.7 dynamic_slice.3
  0.7 0.8 and_or_fusion
  1.5 1.3 copy-done.3
  3.1 5.1 %collective-permute-start.2 = (bf16[1296,128]{1,0:T(8,128)(2,1)S(1)}, bf16[1296,128]{1,0:T(8,128)(2,1)S(1)}, u32[]{:S(2)}, u32[]{:S(2)}) collective-permute-start(bf16[1296,128]{1,0:T(8,128)(2,1)S(1)} %get-tuple-element.47), channel_id=1, source_target_pairs={{0,24},{2,26},{4,28},{6,30},{8,0},{10,2},{12,4},{14,6},{16,8},{18,... | collective-permute-start | bytes 995336 | tf_op jit(solution)/shard_map/ppermute | solution.py:141
  8.2 1.0 collective-permute-start
  9.2 7.2 %collective-permute-done.2 = bf16[1296,128]{1,0:T(8,128)(2,1)S(1)} collective-permute-done((bf16[1296,128]{1,0:T(8,128)(2,1)S(1)}, bf16[1296,128]{1,0:T(8,128)(2,1)S(1)}, u32[]{:S(2)}, u32[]{:S(2)}) %collective-permute-start.2) | collective-permute-done | bytes 331808 | tf_op jit(solution)/shard_map/ppermute | solution.py:141
  16.5 20.0 %collective-permute-done.1 = bf16[1296,128]{1,0:T(8,128)(2,1)S(1)} collective-permute-done((bf16[1296,128]{1,0:T(8,128)(2,1)S(1)}, bf16[1296,128]{1,0:T(8,128)(2,1)S(1)}, u32[]{:S(2)}, u32[]{:S(2)}) %collective-permute-start.1) | collective-permute-done | bytes 331808 | tf_op jit(solution)/shard_map/ppermute | solution.py:141
  37.2 0.8 copy-done.11
  38.2 1.6 collective-permute-start.10
  40.6 1.5 collective-permute-start.3
  42.2 3.5 %collective-permute-done.3 = f32[256,2]{1,0:T(8,128)S(1)} collective-permute-done((f32[256,2]{1,0:T(8,128)S(1)}, f32[256,2]{1,0:T(8,128)S(1)}, u32[]{:S(2)}, u32[]{:S(2)}) %collective-permute-start.3) | collective-permute-done | bytes 2080 | tf_op jit(solution)/shard_map/ppermute | solution.py:173
  46.4 2.0 %collective-permute-start.8 = (bf16[1280,128]{1,0:T(8,128)(2,1)S(1)}, bf16[1280,128]{1,0:T(8,128)(2,1)S(1)}, u32[]{:S(2)}, u32[]{:S(2)}) collective-permute-start(bf16[1280,128]{1,0:T(8,128)(2,1)S(1)} %get-tuple-element.56), channel_id=1, source_target_pairs={{0,16},{2,18},{4,20},{6,22},{8,24},{10,26},{12,28},{14,30},{16,0},... | collective-permute-start | bytes 983048 | tf_op jit(solution)/shard_map/ppermute | solution.py:141
  48.4 2.8 %collective-permute-start.9 = (bf16[1280,128]{1,0:T(8,128)(2,1)S(1)}, bf16[1280,128]{1,0:T(8,128)(2,1)S(1)}, u32[]{:S(2)}, u32[]{:S(2)}) collective-permute-start(bf16[1280,128]{1,0:T(8,128)(2,1)S(1)} %get-tuple-element.57), channel_id=1, source_target_pairs={{0,24},{2,26},{4,28},{6,30},{8,0},{10,2},{12,4},{14,6},{16,8},{18,... | collective-permute-start | bytes 983048 | tf_op jit(solution)/shard_map/ppermute | solution.py:141
  51.2 7.6 %collective-permute-done.7 = bf16[1280,128]{1,0:T(8,128)(2,1)S(1)} collective-permute-done((bf16[1280,128]{1,0:T(8,128)(2,1)S(1)}, bf16[1280,128]{1,0:T(8,128)(2,1)S(1)}, u32[]{:S(2)}, u32[]{:S(2)}) %collective-permute-start.7) | collective-permute-done | bytes 327712 | tf_op jit(solution)/shard_map/ppermute | solution.py:141
  58.8 11.3 %collective-permute-done.8 = bf16[1280,128]{1,0:T(8,128)(2,1)S(1)} collective-permute-done((bf16[1280,128]{1,0:T(8,128)(2,1)S(1)}, bf16[1280,128]{1,0:T(8,128)(2,1)S(1)}, u32[]{:S(2)}, u32[]{:S(2)}) %collective-permute-start.8) | collective-permute-done | bytes 327712 | tf_op jit(solution)/shard_map/ppermute | solution.py:141
  70.3 1.6 collective-permute-start.11
  72.4 6.7 %collective-permute-start.4 = (bf16[1280,128]{1,0:T(8,128)(2,1)S(1)}, bf16[1280,128]{1,0:T(8,128)(2,1)S(1)}, u32[]{:S(2)}, u32[]{:S(2)}) collective-permute-start(bf16[1280,128]{1,0:T(8,128)(2,1)S(1)} %get-tuple-element.51), channel_id=1, source_target_pairs={{0,8},{2,10},{4,12},{6,14},{8,16},{10,18},{12,20},{14,22},{16,24},... | collective-permute-start | bytes 983048 | tf_op jit(solution)/shard_map/ppermute | solution.py:141
  79.1 2.2 %collective-permute-start.5 = (bf16[1280,128]{1,0:T(8,128)(2,1)S(1)}, bf16[1280,128]{1,0:T(8,128)(2,1)S(1)}, u32[]{:S(2)}, u32[]{:S(2)}) collective-permute-start(bf16[1280,128]{1,0:T(8,128)(2,1)S(1)} %get-tuple-element.52), channel_id=1, source_target_pairs={{0,16},{2,18},{4,20},{6,22},{8,24},{10,26},{12,28},{14,30},{16,0},... | collective-permute-start | bytes 983048 | tf_op jit(solution)/shard_map/ppermute | solution.py:141
  81.6 7.8 %collective-permute-done.4.q_ref = bf16[1280,128]{1,0:T(8,128)(2,1)S(1)} collective-permute-done((bf16[1280,128]{1,0:T(8,128)(2,1)S(1)}, bf16[1280,128]{1,0:T(8,128)(2,1)S(1)}, u32[]{:S(2)}, u32[]{:S(2)}) %collective-permute-start.4) | collective-permute-done | bytes 327712 | tf_op jit(solution)/shard_map/ppermute | solution.py:141
  89.4 0.7 copy-done.6
  90.2 9.8 %collective-permute-done.5.q_ref = bf16[1280,128]{1,0:T(8,128)(2,1)S(1)} collective-permute-done((bf16[1280,128]{1,0:T(8,128)(2,1)S(1)}, bf16[1280,128]{1,0:T(8,128)(2,1)S(1)}, u32[]{:S(2)}, u32[]{:S(2)}) %collective-permute-start.5) | collective-permute-done | bytes 327712 | tf_op jit(solution)/shard_map/ppermute | solution.py:141
  100.0 0.7 copy-done.4
  105.0 0.9 collective-permute-done.13.refs_3_
  106.0 1.0 copy-done.7
  107.0 12.3 %attend_1.1 = bf16[1280,128]{1,0:T(8,128)(2,1)S(1)} custom-call(f32[256]{0:T(256)S(1)} %reshape.86.bias_ref, bf16[1280,128]{1,0:T(8,128)(2,1)S(1)} %copy-done.7, bf16[4,1280,128]{2,1,0:T(8,128)(2,1)S(1)} %pad_maximum_fusion.1.refs_0_, bf16[4,1280,128]{2,1,0:T(8,128)(2,1)} %collective-permute-done.12.refs_1_, ...), custom_call_target="tpu_custom_call" | custom-call | flops 2684354560 | bytes 13107200 | tf_op jit(solution)/shard_map/attend_1/pallas_call | solution.py:234
  119.3 9.3 %collective-permute-start.16 = (bf16[1280,128]{1,0:T(8,128)(2,1)S(1)}, bf16[1280,128]{1,0:T(8,128)(2,1)S(1)}, u32[]{:S(2)}, u32[]{:S(2)}) collective-permute-start(bf16[1280,128]{1,0:T(8,128)(2,1)S(1)} %attend_1.1), channel_id=1, source_target_pairs={{0,24},{2,26},{4,28},{6,30},{8,0},{10,2},{12,4},{14,6},{16,8},{18,... | collective-permute-start | bytes 983048 | tf_op jit(solution)/shard_map/ppermute | solution.py:141
  128.6 12.3 %attend_2.1 = bf16[1280,128]{1,0:T(8,128)(2,1)S(1)} custom-call(f32[256]{0:T(256)S(1)} %reshape.86.bias_ref, bf16[1280,128]{1,0:T(8,128)(2,1)S(1)} %copy-done.5, bf16[4,1280,128]{2,1,0:T(8,128)(2,1)S(1)} %pad_maximum_fusion.1.refs_0_, bf16[4,1280,128]{2,1,0:T(8,128)(2,1)} %collective-permute-done.12.refs_1_, ...), custom_call_target="tpu_custom_call" | custom-call | flops 2684354560 | bytes 13107200 | tf_op jit(solution)/shard_map/attend_2/pallas_call | solution.py:234
  141.0 12.3 %attend_3.1 = bf16[1280,128]{1,0:T(8,128)(2,1)S(1)} custom-call(f32[256]{0:T(256)S(1)} %reshape.86.bias_ref, bf16[1280,128]{1,0:T(8,128)(2,1)S(1)} %collective-permute-done.6.q_ref, bf16[4,1280,128]{2,1,0:T(8,128)(2,1)S(1)} %pad_maximum_fusion.1.refs_0_, bf16[4,1280,128]{2,1,0:T(8,128)(2,1)} %collective-permute-done.12.refs_1_, ...), custom_call_target="tpu_custom_call" | custom-call | flops 2684354560 | bytes 13107200 | tf_op jit(solution)/shard_map/attend_3/pallas_call | solution.py:234
  153.4 0.8 collective-permute-start.18
  154.2 1.9 %collective-permute-done.17.refs_2_ = bf16[1280,128]{1,0:T(8,128)(2,1)S(1)} collective-permute-done((bf16[1280,128]{1,0:T(8,128)(2,1)S(1)}, bf16[1280,128]{1,0:T(8,128)(2,1)S(1)}, u32[]{:S(2)}, u32[]{:S(2)}) %collective-permute-start.17) | collective-permute-done | bytes 327712 | tf_op jit(solution)/shard_map/ppermute | solution.py:141
  156.1 12.3 %attend_0.1.refs_0_ = bf16[1280,128]{1,0:T(8,128)(2,1)S(1)} custom-call(f32[256]{0:T(256)S(1)} %reshape.86.bias_ref, bf16[1280,128]{1,0:T(8,128)(2,1)S(1)} %get-tuple-element.72.q_ref, bf16[4,1280,128]{2,1,0:T(8,128)(2,1)S(1)} %pad_maximum_fusion.1.refs_0_, bf16[4,1280,128]{2,1,0:T(8,128)(2,1)} %collective-permute-done.12.refs_1_, ...), custom_call_target="tpu_custom_call" | custom-call | flops 2684354560 | bytes 13107200 | tf_op jit(solution)/shard_map/attend_0/pallas_call | solution.py:234
  168.4 1.8 %collect.1 = f32[256,2560]{1,0:T(8,128)} custom-call(s32[1]{0:T(128)} %bitcast.place_ref, bf16[1280,128]{1,0:T(8,128)(2,1)S(1)} %attend_0.1.refs_0_, bf16[1280,128]{1,0:T(8,128)(2,1)S(1)} %collective-permute-done.16.refs_1_, bf16[1280,128]{1,0:T(8,128)(2,1)S(1)} %collective-permute-done.17.refs_2_, bf16[1280,128]{1,0:T(8,128)(2,1)S(1)} %collective-permute-done.18.refs_3_), custom_call_target="tpu_custom_call" | custom-call | tf_op jit(solution)/shard_map/collect/pallas_call | solution.py:265
  (71 shorter events, 8.2 us)
Async XLA Ops:
  1.5 1.3 copy-start.3
  2.8 37.0 %copy-start.2 = (f32[256,2560]{1,0:T(8,128)S(1)}, f32[256,2560]{1,0:T(8,128)}, u32[]{:S(2)}) copy-start(f32[256,2560]{1,0:T(8,128)} %q_ref.1) | copy-start | bytes 7864324
  3.1 33.4 %copy-start.8 = (bf16[1296,128]{1,0:T(8,128)(2,1)}, bf16[1296,128]{1,0:T(8,128)(2,1)S(1)}, u32[]{:S(2)}) copy-start(bf16[1296,128]{1,0:T(8,128)(2,1)S(1)} %get-tuple-element.44) | copy-start | bytes 995332
  3.1 13.3 %collective-permute-start.2 = (bf16[1296,128]{1,0:T(8,128)(2,1)S(1)}, bf16[1296,128]{1,0:T(8,128)(2,1)S(1)}, u32[]{:S(2)}, u32[]{:S(2)}) collective-permute-start(bf16[1296,128]{1,0:T(8,128)(2,1)S(1)} %get-tuple-element.47), channel_id=1, source_target_pairs={{0,24},{2,26},{4,28},{6,30},{8,0},{10,2},{12,4},{14,6},{16,8},{18,... | collective-permute-start | bytes 995336 | tf_op jit(solution)/shard_map/ppermute | solution.py:141
  8.2 28.3 %collective-permute-start.1 = (bf16[1296,128]{1,0:T(8,128)(2,1)S(1)}, bf16[1296,128]{1,0:T(8,128)(2,1)S(1)}, u32[]{:S(2)}, u32[]{:S(2)}) collective-permute-start(bf16[1296,128]{1,0:T(8,128)(2,1)S(1)} %get-tuple-element.46), channel_id=1, source_target_pairs={{0,16},{2,18},{4,20},{6,22},{8,24},{10,26},{12,28},{14,30},{16,0},... | collective-permute-start | bytes 995336 | tf_op jit(solution)/shard_map/ppermute | solution.py:141
  8.2 28.3 %collective-permute-start = (bf16[1296,128]{1,0:T(8,128)(2,1)S(1)}, bf16[1296,128]{1,0:T(8,128)(2,1)S(1)}, u32[]{:S(2)}, u32[]{:S(2)}) collective-permute-start(bf16[1296,128]{1,0:T(8,128)(2,1)S(1)} %get-tuple-element.45), channel_id=1, source_target_pairs={{0,8},{2,10},{4,12},{6,14},{8,16},{10,18},{12,20},{14,22},{16,24},... | collective-permute-start | bytes 995336 | tf_op jit(solution)/shard_map/ppermute | solution.py:141
  16.4 20.1 %copy-start.9 = (bf16[1296,128]{1,0:T(8,128)(2,1)}, bf16[1296,128]{1,0:T(8,128)(2,1)S(1)}, u32[]{:S(2)}) copy-start(bf16[1296,128]{1,0:T(8,128)(2,1)S(1)} %collective-permute-done.2) | copy-start | bytes 995332
  36.5 0.8 copy-start.10
  37.2 0.8 copy-start.11
  38.0 2.2 %copy-start.1 = (f32[256,2560]{1,0:T(8,128)S(1)}, f32[256,2560]{1,0:T(8,128)}, u32[]{:S(2)}) copy-start(f32[256,2560]{1,0:T(8,128)} %k_ref.1) | copy-start | bytes 7864324
  38.2 43.4 %copy-start = (bf16[4,1280,128]{2,1,0:T(8,128)(2,1)}, bf16[4,1280,128]{2,1,0:T(8,128)(2,1)S(1)}, u32[]{:S(2)}) copy-start(bf16[4,1280,128]{2,1,0:T(8,128)(2,1)S(1)} %pad_maximum_fusion._.refs_4_) | copy-start | bytes 3932164
  38.2 4.0 %copy-start.12 = (f32[2560]{0:T(1024)S(1)}, f32[2560]{0:T(1024)}, u32[]{:S(2)}) copy-start(f32[2560]{0:T(1024)} %param.11) | copy-start | bytes 30724
  38.2 31.9 %collective-permute-start.10 = (bf16[4,1280,128]{2,1,0:T(8,128)(2,1)S(1)}, bf16[4,1280,128]{2,1,0:T(8,128)(2,1)}, u32[]{:S(2)}, u32[]{:S(2)}) collective-permute-start(bf16[4,1280,128]{2,1,0:T(8,128)(2,1)S(1)} %pad_maximum_fusion._.refs_4_), channel_id=1, source_target_pairs={{0,4},{2,6},{4,0},{6,2},{8,12},{10,14},{12,8},{14,10},{16,20},{18,... | collective-permute-start | bytes 3932168 | tf_op jit(solution)/shard_map/ppermute | solution.py:147
  40.6 5.0 %collective-permute-start.3 = (f32[256,2]{1,0:T(8,128)S(1)}, f32[256,2]{1,0:T(8,128)S(1)}, u32[]{:S(2)}, u32[]{:S(2)}) collective-permute-start(f32[256,2]{1,0:T(8,128)S(1)} %square_sums.1), channel_id=1, source_target_pairs={{0,1},{1,0},{2,3},{3,2},{4,5},{5,4},{6,7},{7,6},{8,9},{9,8},{10,11... | collective-permute-start | bytes 6152 | tf_op jit(solution)/shard_map/ppermute | solution.py:173
  46.2 12.6 %collective-permute-start.7 = (bf16[1280,128]{1,0:T(8,128)(2,1)S(1)}, bf16[1280,128]{1,0:T(8,128)(2,1)S(1)}, u32[]{:S(2)}, u32[]{:S(2)}) collective-permute-start(bf16[1280,128]{1,0:T(8,128)(2,1)S(1)} %get-tuple-element.55), channel_id=1, source_target_pairs={{0,8},{2,10},{4,12},{6,14},{8,16},{10,18},{12,20},{14,22},{16,24},... | collective-permute-start | bytes 983048 | tf_op jit(solution)/shard_map/ppermute | solution.py:141
  46.4 23.7 %collective-permute-start.8 = (bf16[1280,128]{1,0:T(8,128)(2,1)S(1)}, bf16[1280,128]{1,0:T(8,128)(2,1)S(1)}, u32[]{:S(2)}, u32[]{:S(2)}) collective-permute-start(bf16[1280,128]{1,0:T(8,128)(2,1)S(1)} %get-tuple-element.56), channel_id=1, source_target_pairs={{0,16},{2,18},{4,20},{6,22},{8,24},{10,26},{12,28},{14,30},{16,0},... | collective-permute-start | bytes 983048 | tf_op jit(solution)/shard_map/ppermute | solution.py:141
  48.4 21.7 %collective-permute-start.9 = (bf16[1280,128]{1,0:T(8,128)(2,1)S(1)}, bf16[1280,128]{1,0:T(8,128)(2,1)S(1)}, u32[]{:S(2)}, u32[]{:S(2)}) collective-permute-start(bf16[1280,128]{1,0:T(8,128)(2,1)S(1)} %get-tuple-element.57), channel_id=1, source_target_pairs={{0,24},{2,26},{4,28},{6,30},{8,0},{10,2},{12,4},{14,6},{16,8},{18,... | collective-permute-start | bytes 983048 | tf_op jit(solution)/shard_map/ppermute | solution.py:141
  70.1 1.8 %copy-start.13 = (f32[2560]{0:T(1024)S(1)}, f32[2560]{0:T(1024)}, u32[]{:S(2)}) copy-start(f32[2560]{0:T(1024)} %param.10) | copy-start | bytes 30724
  70.3 30.4 %collective-permute-start.11 = (bf16[4,1280,128]{2,1,0:T(8,128)(2,1)S(1)}, bf16[4,1280,128]{2,1,0:T(8,128)(2,1)}, u32[]{:S(2)}, u32[]{:S(2)}) collective-permute-start(bf16[4,1280,128]{2,1,0:T(8,128)(2,1)S(1)} %pad_maximum_fusion.1.refs_0_), channel_id=1, source_target_pairs={{0,4},{2,6},{4,0},{6,2},{8,12},{10,14},{12,8},{14,10},{16,20},{18,... | collective-permute-start | bytes 3932168 | tf_op jit(solution)/shard_map/ppermute | solution.py:147
  72.4 17.1 %collective-permute-start.4 = (bf16[1280,128]{1,0:T(8,128)(2,1)S(1)}, bf16[1280,128]{1,0:T(8,128)(2,1)S(1)}, u32[]{:S(2)}, u32[]{:S(2)}) collective-permute-start(bf16[1280,128]{1,0:T(8,128)(2,1)S(1)} %get-tuple-element.51), channel_id=1, source_target_pairs={{0,8},{2,10},{4,12},{6,14},{8,16},{10,18},{12,20},{14,22},{16,24},... | collective-permute-start | bytes 983048 | tf_op jit(solution)/shard_map/ppermute | solution.py:141
  79.1 20.9 %collective-permute-start.5 = (bf16[1280,128]{1,0:T(8,128)(2,1)S(1)}, bf16[1280,128]{1,0:T(8,128)(2,1)S(1)}, u32[]{:S(2)}, u32[]{:S(2)}) collective-permute-start(bf16[1280,128]{1,0:T(8,128)(2,1)S(1)} %get-tuple-element.52), channel_id=1, source_target_pairs={{0,16},{2,18},{4,20},{6,22},{8,24},{10,26},{12,28},{14,30},{16,0},... | collective-permute-start | bytes 983048 | tf_op jit(solution)/shard_map/ppermute | solution.py:141
  81.2 19.5 %collective-permute-start.6 = (bf16[1280,128]{1,0:T(8,128)(2,1)S(1)}, bf16[1280,128]{1,0:T(8,128)(2,1)S(1)}, u32[]{:S(2)}, u32[]{:S(2)}) collective-permute-start(bf16[1280,128]{1,0:T(8,128)(2,1)S(1)} %get-tuple-element.53), channel_id=1, source_target_pairs={{0,24},{2,26},{4,28},{6,30},{8,0},{10,2},{12,4},{14,6},{16,8},{18,... | collective-permute-start | bytes 983048 | tf_op jit(solution)/shard_map/ppermute | solution.py:141
  81.6 23.3 %collective-permute-start.14 = (bf16[4,1280,128]{2,1,0:T(8,128)(2,1)S(1)}, bf16[4,1280,128]{2,1,0:T(8,128)(2,1)}, u32[]{:S(2)}, u32[]{:S(2)}) collective-permute-start(bf16[4,1280,128]{2,1,0:T(8,128)(2,1)S(1)} %pad_maximum_fusion._.refs_4_), channel_id=1, source_target_pairs={{0,2},{2,0},{4,6},{6,4},{8,10},{10,8},{12,14},{14,12},{16,18},{18,... | collective-permute-start | bytes 3932168 | tf_op jit(solution)/shard_map/ppermute | solution.py:147
  89.4 0.7 copy-start.6
  90.2 14.8 %collective-permute-start.15 = (bf16[4,1280,128]{2,1,0:T(8,128)(2,1)}, bf16[4,1280,128]{2,1,0:T(8,128)(2,1)}, u32[]{:S(2)}, u32[]{:S(2)}) collective-permute-start(bf16[4,1280,128]{2,1,0:T(8,128)(2,1)} %collective-permute-done.10.refs_6_), channel_id=1, source_target_pairs={{0,2},{2,0},{4,6},{6,4},{8,10},{10,8},{12,14},{14,12},{16,18},{18,... | collective-permute-start | bytes 3932168 | tf_op jit(solution)/shard_map/ppermute | solution.py:147
  100.7 4.3 %collective-permute-start.12 = (bf16[4,1280,128]{2,1,0:T(8,128)(2,1)S(1)}, bf16[4,1280,128]{2,1,0:T(8,128)(2,1)}, u32[]{:S(2)}, u32[]{:S(2)}) collective-permute-start(bf16[4,1280,128]{2,1,0:T(8,128)(2,1)S(1)} %pad_maximum_fusion.1.refs_0_), channel_id=1, source_target_pairs={{0,2},{2,0},{4,6},{6,4},{8,10},{10,8},{12,14},{14,12},{16,18},{18,... | collective-permute-start | bytes 3932168 | tf_op jit(solution)/shard_map/ppermute | solution.py:147
  100.7 5.2 %collective-permute-start.13 = (bf16[4,1280,128]{2,1,0:T(8,128)(2,1)}, bf16[4,1280,128]{2,1,0:T(8,128)(2,1)}, u32[]{:S(2)}, u32[]{:S(2)}) collective-permute-start(bf16[4,1280,128]{2,1,0:T(8,128)(2,1)} %collective-permute-done.11.refs_2_), channel_id=1, source_target_pairs={{0,2},{2,0},{4,6},{6,4},{8,10},{10,8},{12,14},{14,12},{16,18},{18,... | collective-permute-start | bytes 3932168 | tf_op jit(solution)/shard_map/ppermute | solution.py:147
  104.9 23.7 %copy-start.5 = (bf16[1280,128]{1,0:T(8,128)(2,1)S(1)}, bf16[1280,128]{1,0:T(8,128)(2,1)}, u32[]{:S(2)}) copy-start(bf16[1280,128]{1,0:T(8,128)(2,1)} %copy-done.4) | copy-start | bytes 983044
  106.0 1.0 copy-start.7
  119.3 21.7 %collective-permute-start.16 = (bf16[1280,128]{1,0:T(8,128)(2,1)S(1)}, bf16[1280,128]{1,0:T(8,128)(2,1)S(1)}, u32[]{:S(2)}, u32[]{:S(2)}) collective-permute-start(bf16[1280,128]{1,0:T(8,128)(2,1)S(1)} %attend_1.1), channel_id=1, source_target_pairs={{0,24},{2,26},{4,28},{6,30},{8,0},{10,2},{12,4},{14,6},{16,8},{18,... | collective-permute-start | bytes 983048 | tf_op jit(solution)/shard_map/ppermute | solution.py:141
  140.9 15.1 %collective-permute-start.17 = (bf16[1280,128]{1,0:T(8,128)(2,1)S(1)}, bf16[1280,128]{1,0:T(8,128)(2,1)S(1)}, u32[]{:S(2)}, u32[]{:S(2)}) collective-permute-start(bf16[1280,128]{1,0:T(8,128)(2,1)S(1)} %attend_2.1), channel_id=1, source_target_pairs={{0,16},{2,18},{4,20},{6,22},{8,24},{10,26},{12,28},{14,30},{16,0},... | collective-permute-start | bytes 983048 | tf_op jit(solution)/shard_map/ppermute | solution.py:141
  153.4 15.0 %collective-permute-start.18 = (bf16[1280,128]{1,0:T(8,128)(2,1)S(1)}, bf16[1280,128]{1,0:T(8,128)(2,1)S(1)}, u32[]{:S(2)}, u32[]{:S(2)}) collective-permute-start(bf16[1280,128]{1,0:T(8,128)(2,1)S(1)} %attend_3.1), channel_id=1, source_target_pairs={{0,8},{2,10},{4,12},{6,14},{8,16},{10,18},{12,20},{14,22},{16,24},... | collective-permute-start | bytes 983048 | tf_op jit(solution)/shard_map/ppermute | solution.py:141
  (1 other events, 0.7 us)

commit v3 on v2

v3 whole, which is shorter than its diff:
```python
import functools
import math

import jax
import jax.numpy as jnp
from jax import lax
from jax.experimental import pallas as pl
from jax.experimental.pallas import tpu as pltpu
from jax.sharding import PartitionSpec as P

HEAD_DIM = 128
BLOCK = 128
epsilon = 1e-06
blocked = -1e30
MASK_ROWS = 16
MIB = 1024 * 1024
VMEM = pl.BlockSpec(memory_space=pltpu.VMEM)
SMEM = pl.BlockSpec(memory_space=pltpu.SMEM)
ANY = pl.BlockSpec(memory_space=pl.ANY)


def column_of(place_ref, shift, head, groups, per_group):
    group = lax.rem(place_ref[0] + shift, groups)
    return pl.multiple_of((group * per_group + head) * HEAD_DIM, HEAD_DIM)


def value_kernel(place_ref, v_ref, *outs, per_group):
    groups = len(outs)
    rows = v_ref.shape[0]
    for shift, out in enumerate(outs):
        for head in range(per_group):
            column = column_of(place_ref, shift, head, groups, per_group)
            out[head * rows : (head + 1) * rows, :] = v_ref[:, pl.ds(column, HEAD_DIM)]


def square_sums_kernel(q_ref, k_ref, out_ref):
    q, k = q_ref[...], k_ref[...]
    out_ref[:, 0:1] = jnp.sum(q * q, axis=1, keepdims=True)
    out_ref[:, 1:2] = jnp.sum(k * k, axis=1, keepdims=True)


def normed_columns(x_ref, inverse, gain_ref, column):
    here = pl.ds(column, HEAD_DIM)
    return (x_ref[:, here] * inverse * gain_ref[:, here]).astype(jnp.bfloat16)


def norm_kernel(
    place_ref, sums_ref, q_ref, k_ref, q_gain_ref, k_gain_ref, mask_ref, *outs, per_group, full_width
):
    groups = len(outs) // 2
    rows = k_ref.shape[0]
    inverse = 1.0 / jnp.sqrt(sums_ref[...] / full_width + epsilon)
    for shift in range(groups):
        k_out, q_out = outs[shift], outs[groups + shift]
        for head in range(per_group):
            column = column_of(place_ref, shift, head, groups, per_group)
            q_out[head * rows : (head + 1) * rows, :] = normed_columns(
                q_ref, inverse[:, 0:1], q_gain_ref, column
            )
            k = normed_columns(k_ref, inverse[:, 1:2], k_gain_ref, column)
            for b in range(rows // BLOCK):
                low = head * rows + b * HEAD_DIM
                k_out[low : low + HEAD_DIM, :] = k[b * BLOCK : (b + 1) * BLOCK].T
        k_out[per_group * rows :, :] = mask_ref[...]


def attend_kernel(bias_ref, q_ref, *refs, query_slot, groups, layers, heads, scale):
    k_refs, v_refs = refs[:layers], refs[layers : 2 * layers]
    out, scores = refs[-2:]
    rows = out.shape[0] // len(heads)
    blk = rows // BLOCK
    slots = groups * layers
    lowest = jnp.full((rows, BLOCK), blocked, jnp.float32)
    ones = jnp.ones((rows, HEAD_DIM), jnp.bfloat16)

    def score(head, slot, top, q):
        keys = k_refs[slot // groups][slot % groups, head * rows : (head + 1) * rows, :]
        wide = jnp.concatenate(
            [keys[b * HEAD_DIM : (b + 1) * HEAD_DIM] for b in range(blk)], axis=1
        )
        products = jnp.dot(q, wide, preferred_element_type=jnp.float32)
        first = (query_slot * slots + slot) * blk
        for b in range(blk):
            columns = slice(b * BLOCK, (b + 1) * BLOCK)
            block = jnp.concatenate(
                [
                    products[a * BLOCK : (a + 1) * BLOCK, columns] + bias_ref[(first + a) * blk + b]
                    for a in range(blk)
                ],
                axis=0,
            )
            scores[head % 2, slot, :, columns] = block
            top = jnp.maximum(top, block)
        return top

    def weigh(head, slot, row_max, mixed):
        weights = jnp.exp2((scores[head % 2, slot] - row_max) * scale).astype(jnp.bfloat16)
        values = v_refs[slot // groups][slot % groups, head * rows : (head + 1) * rows, :]
        return mixed + jnp.dot(
            weights, jnp.concatenate([values, ones], axis=1), preferred_element_type=jnp.float32
        )

    top, q = lowest, q_ref[heads[0] * rows : (heads[0] + 1) * rows, :]
    for slot in range(slots):
        top = score(heads[0], slot, top, q)
    for head in heads:
        row_max = jnp.max(top, axis=1, keepdims=True)
        mixed, top = jnp.zeros((rows, 2 * HEAD_DIM), jnp.float32), lowest
        if head + 1 in heads:
            q = q_ref[(head + 1) * rows : (head + 2) * rows, :]
        for slot in range(slots):
            if head + 1 in heads:
                top = score(head + 1, slot, top, q)
            mixed = weigh(head, slot, row_max, mixed)
        low = (head - heads[0]) * rows
        out[low : low + rows, :] = (
            mixed[:, :HEAD_DIM] / mixed[:, HEAD_DIM : HEAD_DIM + 1]
        ).astype(jnp.bfloat16)


def collect_kernel(place_ref, *refs, groups, per_group):
    out = refs[-1]
    rows = out.shape[0]
    first = refs[0].shape[0] // rows
    for shift in range(groups):
        for head in range(per_group):
            if shift:
                ref, low = refs[shift + 1], head * rows
            elif head < first:
                ref, low = refs[0], head * rows
            else:
                ref, low = refs[1], (head - first) * rows
            column = column_of(place_ref, shift, head, groups, per_group)
            out[:, pl.ds(column, HEAD_DIM)] = ref[low : low + rows, :].astype(jnp.float32)


def exchanged(q_in, k_in, v_in, q_gain, k_gain, frames, adjacent, *, groups):
    rows, width = q_in.shape
    devices = lax.axis_size("seq")
    tensors = lax.axis_size("tensor")
    layers = devices // groups
    blk = rows // BLOCK
    blocks = devices * blk
    per_group = width // HEAD_DIM // groups
    me = lax.axis_index("seq")
    place, spot = me // layers, lax.rem(me, layers)
    place_row = place.reshape(1).astype(jnp.int32)
    f32, bf16 = jnp.float32, jnp.bfloat16
    params = pltpu.CompilerParams(vmem_limit_bytes=20 * MIB)
    def rotated(x, shift):
        pairs = [
            (z * layers + r, (z + shift) % groups * layers + r)
            for z in range(groups)
            for r in range(layers)
        ]
        return lax.ppermute(x, "seq", pairs)

    def exchange(pieces, after=None):
        arrived = [pieces[0]]
        for s in range(1, groups):
            piece = pieces[s]
            if after is not None:
                piece, after[s] = lax.optimization_barrier((piece, after[s]))
            arrived.append(rotated(piece, s))
        return arrived

    def swapped(x, bit):
        return lax.ppermute(x, "seq", [(i, i ^ bit) for i in range(devices)])

    own_frames = lax.dynamic_slice_in_dim(frames, me * blk, blk, 0)
    gap = jnp.abs(own_frames[:, None] - frames[None, :])
    allowed = ((gap == 0) | (gap == 1) & (adjacent == 1)).astype(bf16)
    mask_rows = jnp.pad(allowed, ((0, MASK_ROWS - blk), (0, BLOCK - blocks)))

    v_pieces = pl.pallas_call(
        functools.partial(value_kernel, per_group=per_group),
        out_shape=[jax.ShapeDtypeStruct((per_group * rows, HEAD_DIM), bf16)] * groups,
        in_specs=[SMEM, VMEM],
        out_specs=[VMEM] * groups,
        compiler_params=params,
        name="value_pieces",
    )(place_row, v_in)
    q_in, k_in, v_pieces = lax.optimization_barrier((q_in, k_in, v_pieces))
    sums = pl.pallas_call(
        square_sums_kernel,
        out_shape=jax.ShapeDtypeStruct((rows, 2), f32),
        in_specs=[VMEM, VMEM],
        out_specs=VMEM,
        compiler_params=params,
        name="square_sums",
    )(q_in, k_in)
    v_arrived = exchange(v_pieces)
    sums = lax.psum(sums, "tensor")

    piece = jax.ShapeDtypeStruct((per_group * rows, HEAD_DIM), bf16)
    masked_piece = jax.ShapeDtypeStruct((per_group * rows + MASK_ROWS, HEAD_DIM), bf16)
    pieces = pl.pallas_call(
        functools.partial(
            norm_kernel, per_group=per_group, full_width=float(width * tensors)
        ),
        out_shape=[masked_piece] * groups + [piece] * groups,
        in_specs=[SMEM] + [VMEM] * 6,
        out_specs=[VMEM] * (2 * groups),
        compiler_params=params,
        name="norm_pieces",
    )(place_row, sums, q_in, k_in, q_gain.reshape(1, width), k_gain.reshape(1, width), mask_rows)
    k_arrived = exchange(pieces[:groups], v_arrived)
    v_stack = jnp.stack(v_arrived)
    q_arrived = exchange(pieces[groups:], k_arrived)

    low = per_group * rows
    known = jnp.stack([x[low : low + blk, :blocks] for x in k_arrived]).astype(f32)
    z_order = lax.rem(place - jnp.arange(groups) + groups, groups)
    layer_order = jnp.bitwise_xor(spot, jnp.arange(layers))
    key_blocks = (
        (z_order[None, :, None] * layers + layer_order[:, None, None]) * blk
        + jnp.arange(blk)[None, None, :]
    ).reshape(-1)
    key_hot = (key_blocks[:, None] == jnp.arange(blocks)[None, :]).astype(f32)
    table = jnp.einsum("gab,kb->gak", known, key_hot).reshape(groups, blk, devices, blk)
    bias = jnp.where(table > 0.5, 0.0, blocked).astype(f32).transpose(0, 2, 1, 3).reshape(-1)

    def spread(parts, bit):
        return parts | {have ^ bit: swapped(part, bit) for have, part in parts.items()}

    bits = [1 << i for i in reversed(range(layers.bit_length() - 1))]
    values, keys = {0: v_stack}, {}
    for bit in bits:
        values = spread(values, bit)
        if bit == bits[0]:
            k_arrived, values = lax.optimization_barrier((k_arrived, values))
            keys = {0: jnp.stack([x[: per_group * rows] for x in k_arrived])}
    for bit in bits:
        keys = spread(keys, bit)
        if bit == bits[0]:
            q_arrived, keys, bias = lax.optimization_barrier((q_arrived, keys, bias))
    values = [values[i] for i in range(layers)]
    keys = [keys[i] for i in range(layers)]

    scale = math.log2(math.e) / math.sqrt(HEAD_DIM)
    def attend(g, heads, bias):
        return pl.pallas_call(
            functools.partial(
                attend_kernel,
                query_slot=g,
                groups=groups,
                layers=layers,
                heads=heads,
                scale=scale,
            ),
            in_specs=[SMEM] + [VMEM] * (1 + 2 * layers),
            out_specs=VMEM,
            scratch_shapes=[pltpu.VMEM((2, devices, rows, rows), f32)],
            out_shape=jax.ShapeDtypeStruct((len(heads) * rows, HEAD_DIM), bf16),
            compiler_params=params,
            name=f"attend_{g}_{heads[0]}",
        )(bias, q_arrived[g], *keys, *values)

    order = sorted(range(1, groups), key=lambda s: abs(2 * s - groups))
    outputs, last = [None] * groups, None
    for g in order:
        own = attend(g, range(per_group), bias)
        outputs[g] = rotated(own, groups - g)
        own, bias = lax.optimization_barrier((own, bias))
    parts = []
    for i, heads in enumerate((range(per_group - 2), range(per_group - 2, per_group))):
        if i < len(order) - 1:
            outputs[order[i]], bias = lax.optimization_barrier((outputs[order[i]], bias))
        parts.append(attend(0, heads, bias))
        parts[-1], bias = lax.optimization_barrier((parts[-1], bias))

    return pl.pallas_call(
        functools.partial(collect_kernel, groups=groups, per_group=per_group),
        out_shape=jax.ShapeDtypeStruct((rows, width), f32),
        in_specs=[SMEM] + [VMEM] * (groups + 1),
        out_specs=VMEM,
        compiler_params=params,
        name="collect",
    )(place_row, *parts, *outputs[1:])


def normalized(inputs, gain_row, square_sum, full_width):
    return (inputs / jnp.sqrt(square_sum / full_width + epsilon)[:, None] * gain_row).astype(
        jnp.bfloat16
    )


def shards(q_in, k_in, v_in, q_gain, k_gain, frames, adjacent):
    tok_rows = q_in.shape[0]
    width_dev = q_in.shape[1]
    full_width = width_dev * lax.axis_size("tensor")
    q_sum, k_sum = lax.psum((jnp.sum(q_in * q_in, axis=1), jnp.sum(k_in * k_in, axis=1)), "tensor")
    q_norm = normalized(q_in, q_gain, q_sum, full_width)
    k_norm = normalized(k_in, k_gain, k_sum, full_width)
    blk_dev = tok_rows // BLOCK
    device = lax.axis_index("seq")
    first_block = device * blk_dev
    query_frames = lax.dynamic_slice_in_dim(frames, first_block, blk_dev, 0)
    score_scale = 1.0 / math.sqrt(HEAD_DIM)
    head_count = width_dev // HEAD_DIM
    q_three = q_norm.reshape(tok_rows, head_count, HEAD_DIM)

    def masked_scores(key_rows, key_start):
        key_block = key_start // BLOCK
        key_frames = lax.dynamic_slice_in_dim(frames, key_block, blk_dev, 0)
        adjacent_rows = lax.dynamic_slice_in_dim(adjacent, key_block, blk_dev, 1)
        frame_gap = jnp.abs(query_frames[:, None] - key_frames[None, :])
        allowed_here = (frame_gap == 0) | (frame_gap == 1) & (adjacent_rows == 1)
        key_three = key_rows.reshape(tok_rows, head_count, HEAD_DIM)
        raw_scores = (
            jnp.einsum("thd,uhd->htu", q_three, key_three, preferred_element_type=jnp.float32)
            * score_scale
        )
        tiled_scores = raw_scores.reshape(head_count, blk_dev, BLOCK, blk_dev, BLOCK)
        tiled_scores = jnp.where(allowed_here[None, :, None, :, None], tiled_scores, blocked)
        return tiled_scores.reshape(head_count, tok_rows, tok_rows)

    piece = lax.all_gather(k_norm, "seq", axis=0, tiled=True)
    shard_count = piece.shape[0] // tok_rows

    def one_shard(shard, current):
        key_rows = lax.dynamic_slice_in_dim(piece, shard * tok_rows, tok_rows, 0)
        return jnp.maximum(current, jnp.max(masked_scores(key_rows, shard * tok_rows), axis=2))

    row_max = lax.fori_loop(
        0, shard_count, one_shard, jnp.full((head_count, tok_rows), blocked, jnp.float32)
    )
    start_sums = (
        jnp.zeros((head_count, tok_rows), jnp.float32),
        jnp.zeros((tok_rows, head_count, HEAD_DIM), jnp.float32),
    )
    key_piece = lax.all_gather(k_norm, "seq", axis=0, tiled=True)
    value_piece = lax.all_gather(v_in, "seq", axis=0, tiled=True)
    shard_count = key_piece.shape[0] // tok_rows

    def one_shard(shard, current):
        totals, accumulated = current
        key_rows = lax.dynamic_slice_in_dim(key_piece, shard * tok_rows, tok_rows, 0)
        value_rows = lax.dynamic_slice_in_dim(value_piece, shard * tok_rows, tok_rows, 0).reshape(
            tok_rows, head_count, HEAD_DIM
        )
        weights = jnp.exp(masked_scores(key_rows, shard * tok_rows) - row_max[:, :, None])
        totals = totals + jnp.sum(weights, axis=2)
        accumulated = accumulated + jnp.einsum(
            "htu,uhd->thd",
            weights.astype(jnp.bfloat16),
            value_rows,
            preferred_element_type=jnp.float32,
        )
        return (totals, accumulated)

    totals, accumulated = lax.fori_loop(0, shard_count, one_shard, start_sums)
    return (accumulated / totals.T[:, :, None]).reshape(tok_rows, width_dev)


def groups_of(mesh, heads):
    layers = 4
    groups = mesh.shape["seq"] // layers
    fits = mesh.shape["seq"] % layers == 0 and heads % groups == 0 and heads >= 2 * groups
    return groups if fits else 1


def solution(mesh):
    def step(q_in, k_in, v_in, q_gain, k_gain, frames, adjacent):
        heads = q_in.shape[1] // mesh.shape["tensor"] // HEAD_DIM
        groups = groups_of(mesh, heads)
        body = shards if groups == 1 else functools.partial(exchanged, groups=groups)
        return jax.shard_map(
            body,
            mesh=mesh,
            in_specs=(
                P("seq", "tensor"),
                P("seq", "tensor"),
                P("seq", "tensor"),
                P("tensor"),
                P("tensor"),
                P(),
                P("seq", None),
            ),
            out_specs=P("seq", "tensor"),
            check_vma=False,
        )(q_in, k_in, v_in, q_gain, k_gain, frames, adjacent)

    return step
```

time: 171 us -> 154 us (0.901)
  Pallas kernels: 52.8 us -> 37.8 us
  starting transfers between devices: 35.7 us -> 25.5 us
  blocking collectives: 0 us -> 10.1 us
  waiting for transfers between devices: 70.2 us -> 65.6 us
  local copies, waits for them, and re-layouts: 9.89 us -> 12.6 us
    pallas_call x7, Pallas kernels: 52.1 us -> 36.3 us  [the longest x5 33.6 us: attend(): pl.pallas_call(functools.partial(attend_kernel, query_slot=g, groups=grou...]
    psum x0 -> x1, blocking collectives: none -> 10.1 us  [exchanged(): sums = lax.psum(sums, 'tensor')]
    ppermute x12, starting transfers between devices: 30.5 us -> 22.8 us  [rotated(): return lax.ppermute(x, 'seq', pairs)]
    ppermute x12, waiting for transfers between devices: 65.7 us -> 61 us  [rotated(): return lax.ppermute(x, 'seq', pairs)]
    ppermute x6, waiting for transfers between devices: 1.04 us -> 4.61 us  [swapped(): return lax.ppermute(x, 'seq', [(i, i ^ bit) for i in range(devices)])]
    ppermute x1 -> x0, waiting for transfers between devices: 3.46 us -> none  [exchanged(): sums = sums + lax.ppermute(sums, 'tensor', [(0, 1), (1, 0)])]
    unnamed x28 -> x36, local copies, waits for them, and re-layouts: 5.66 us -> 9.03 us
  transfers between devices with their start and end apart: 19 -> 18, of which waited for: 10 -> 8; matrix products, arithmetic and copies ran while one was open for 2% -> 3% of each run, Pallas kernels for 23% -> 18%
where the time goes in v3:
time: 154 us
  waiting for transfers between devices  65.6 us (43%)
  Pallas kernels  37.8 us (25%)
  starting transfers between devices  25.5 us (17%)
  local copies, waits for them, and re-layouts  12.6 us (8%)
  blocking collectives  10.1 us (7%)
  other arithmetic  1.74 us (1%)
    ppermute x12, waiting for transfers between devices, rotated(): return lax.ppermute(x, 'seq', pairs)  61 us
    pallas_call x5, Pallas kernels, attend(): pl.pallas_call(functools.partial(attend_kernel, query_slot=g, groups=grou...  33.6 us
    ppermute x12, starting transfers between devices, rotated(): return lax.ppermute(x, 'seq', pairs)  22.8 us
    psum x1, blocking collectives, exchanged(): sums = lax.psum(sums, 'tensor')  10.1 us
    unnamed x36, local copies, waits for them, and re-layouts  9.03 us
    ppermute x6, waiting for transfers between devices, swapped(): return lax.ppermute(x, 'seq', [(i, i ^ bit) for i in range(devices)])  4.61 us
  transfers between devices with their start and end apart: 18, of which 8 were waited for; matrix products, arithmetic and copies ran while one was open for 3% of the time, Pallas kernels for 18%

profile of v3, /device:TPU:0, one launch (start us, length us, event | category | flops | bytes accessed | tf_op | source)
XLA Modules:
  0.0 153.9 jit_solution(193165513754644888)
XLA Ops:
  0.0 1.3 copy-done.6
  1.3 1.1 value_pieces.1
  2.4 3.0 %collective-permute-start = (bf16[1280,128]{1,0:T(8,128)(2,1)}, bf16[1280,128]{1,0:T(8,128)(2,1)}, u32[]{:S(2)}, u32[]{:S(2)}) collective-permute-start(bf16[1280,128]{1,0:T(8,128)(2,1)} %get-tuple-element.67), channel_id=1, source_target_pairs={{0,8},{2,10},{4,12},{6,14},{8,16},{10,18},{12,20},{14,22},{16,24},... | collective-permute-start | bytes 983048 | tf_op jit(solution)/shard_map/ppermute | solution.py:156
  5.4 2.6 %collective-permute-start.3 = (bf16[1280,128]{1,0:T(8,128)(2,1)}, bf16[1280,128]{1,0:T(8,128)(2,1)}, u32[]{:S(2)}, u32[]{:S(2)}) collective-permute-start(bf16[1280,128]{1,0:T(8,128)(2,1)} %get-tuple-element.72), channel_id=1, source_target_pairs={{0,16},{2,18},{4,20},{6,22},{8,24},{10,26},{12,28},{14,30},{16,0},... | collective-permute-start | bytes 983048 | tf_op jit(solution)/shard_map/ppermute | solution.py:156
  8.0 1.3 collective-permute-start.6
  9.4 1.7 %copy-done.2 = f32[256,2560]{1,0:T(8,128)S(1)} copy-done((f32[256,2560]{1,0:T(8,128)S(1)}, f32[256,2560]{1,0:T(8,128)}, u32[]{:S(2)}) %copy-start.2) | copy-done | bytes 2621464
  11.1 1.7 %copy-done.4 = f32[256,2560]{1,0:T(8,128)S(1)} copy-done((f32[256,2560]{1,0:T(8,128)S(1)}, f32[256,2560]{1,0:T(8,128)}, u32[]{:S(2)}) %copy-start.4) | copy-done | bytes 2621464
  13.3 10.1 %psum.7.sums_ref = f32[256,2]{1,0:T(8,128)S(1)} all-reduce(f32[256,2]{1,0:T(8,128)S(1)} %square_sums.1), channel_id=1, replica_groups=mesh['seq'=16,'tensor'=2] {'tensor'}, use_global_device_ids=true, to_apply=%region_0.1 | all-reduce | flops 512 | bytes 4096 | tf_op jit(solution)/shard_map/psum | solution.py:193
  23.6 1.7 %copy-done.5 = f32[256,2560]{1,0:T(8,128)S(1)} copy-done((f32[256,2560]{1,0:T(8,128)S(1)}, f32[256,2560]{1,0:T(8,128)}, u32[]{:S(2)}) %copy-start.5) | copy-done | bytes 2621464
  26.3 3.4 %collective-permute-done.3 = bf16[1280,128]{1,0:T(8,128)(2,1)} collective-permute-done((bf16[1280,128]{1,0:T(8,128)(2,1)}, bf16[1280,128]{1,0:T(8,128)(2,1)}, u32[]{:S(2)}, u32[]{:S(2)}) %collective-permute-start.3) | collective-permute-done | bytes 327712 | tf_op jit(solution)/shard_map/ppermute | solution.py:156
  29.7 1.3 pad_maximum_fusion.refs_4_
  31.0 1.6 %collective-permute-start.9 = (bf16[4,1280,128]{2,1,0:T(8,128)(2,1)S(1)}, bf16[4,1280,128]{2,1,0:T(8,128)(2,1)S(1)}, u32[]{:S(2)}, u32[]{:S(2)}) collective-permute-start(bf16[4,1280,128]{2,1,0:T(8,128)(2,1)S(1)} %pad_maximum_fusion.refs_4_), channel_id=1, source_target_pairs={{0,4},{2,6},{4,0},{6,2},{8,12},{10,14},{12,8},{14,10},{16,20},{18,... | collective-permute-start | bytes 3932168 | tf_op jit(solution)/shard_map/ppermute | solution.py:168
  32.6 8.5 %collective-permute-start.7 = (bf16[1296,128]{1,0:T(8,128)(2,1)S(1)}, bf16[1296,128]{1,0:T(8,128)(2,1)S(1)}, u32[]{:S(2)}, u32[]{:S(2)}) collective-permute-start(bf16[1296,128]{1,0:T(8,128)(2,1)S(1)} %get-tuple-element.78), channel_id=1, source_target_pairs={{0,24},{2,26},{4,28},{6,30},{8,0},{10,2},{12,4},{14,6},{16,8},{18,... | collective-permute-start | bytes 995336 | tf_op jit(solution)/shard_map/ppermute | solution.py:156
  41.7 7.6 %collective-permute-done.7 = bf16[1296,128]{1,0:T(8,128)(2,1)S(1)} collective-permute-done((bf16[1296,128]{1,0:T(8,128)(2,1)S(1)}, bf16[1296,128]{1,0:T(8,128)(2,1)S(1)}, u32[]{:S(2)}, u32[]{:S(2)}) %collective-permute-start.7) | collective-permute-done | bytes 331808 | tf_op jit(solution)/shard_map/ppermute | solution.py:156
  49.4 20.9 %collective-permute-done.4 = bf16[1296,128]{1,0:T(8,128)(2,1)S(1)} collective-permute-done((bf16[1296,128]{1,0:T(8,128)(2,1)S(1)}, bf16[1296,128]{1,0:T(8,128)(2,1)S(1)}, u32[]{:S(2)}, u32[]{:S(2)}) %collective-permute-start.4) | collective-permute-done | bytes 331808 | tf_op jit(solution)/shard_map/ppermute | solution.py:156
  70.3 1.1 copy-done
  73.2 1.4 collective-permute-start.5
  74.6 1.4 collective-permute-start.2
  78.8 3.9 %collective-permute-done.8.q_ref = bf16[1280,128]{1,0:T(8,128)(2,1)S(1)} collective-permute-done((bf16[1280,128]{1,0:T(8,128)(2,1)}, bf16[1280,128]{1,0:T(8,128)(2,1)S(1)}, u32[]{:S(2)}, u32[]{:S(2)}) %collective-permute-start.8) | collective-permute-done | bytes 327712 | tf_op jit(solution)/shard_map/ppermute | solution.py:156
  82.7 19.7 %collective-permute-done.5.q_ref = bf16[1280,128]{1,0:T(8,128)(2,1)} collective-permute-done((bf16[1280,128]{1,0:T(8,128)(2,1)}, bf16[1280,128]{1,0:T(8,128)(2,1)}, u32[]{:S(2)}, u32[]{:S(2)}) %collective-permute-start.5) | collective-permute-done | bytes 327712 | tf_op jit(solution)/shard_map/ppermute | solution.py:156
  103.0 3.7 %collective-permute-done.11.refs_1_ = bf16[4,1280,128]{2,1,0:T(8,128)(2,1)S(1)} collective-permute-done((bf16[4,1280,128]{2,1,0:T(8,128)(2,1)S(1)}, bf16[4,1280,128]{2,1,0:T(8,128)(2,1)S(1)}, u32[]{:S(2)}, u32[]{:S(2)}) %collective-permute-start.11) | collective-permute-done | bytes 1310752 | tf_op jit(solution)/shard_map/ppermute | solution.py:168
  106.6 0.9 collective-permute-done.12.refs_3_
  107.6 1.3 copy-done.1
  108.9 7.9 %attend_2_0.1 = bf16[1280,128]{1,0:T(8,128)(2,1)S(1)} custom-call(f32[256]{0:T(256)S(1)} %reshape.88.bias_ref, bf16[1280,128]{1,0:T(8,128)(2,1)} %collective-permute-done.5.q_ref, bf16[4,1280,128]{2,1,0:T(8,128)(2,1)S(1)} %pad_maximum_fusion.1.refs_0_, bf16[4,1280,128]{2,1,0:T(8,128)(2,1)S(1)} %collective-permute-done.11.refs_1_, ...), custom_call_target="tpu_custom_call" | custom-call | tf_op jit(solution)/shard_map/attend_2_0/pallas_call | solution.py:242
  116.8 1.6 %collective-permute-start.15 = (bf16[1280,128]{1,0:T(8,128)(2,1)S(1)}, bf16[1280,128]{1,0:T(8,128)(2,1)S(1)}, u32[]{:S(2)}, u32[]{:S(2)}) collective-permute-start(bf16[1280,128]{1,0:T(8,128)(2,1)S(1)} %attend_2_0.1), channel_id=1, source_target_pairs={{0,16},{2,18},{4,20},{6,22},{8,24},{10,26},{12,28},{14,30},{16,0},... | collective-permute-start | bytes 983048 | tf_op jit(solution)/shard_map/ppermute | solution.py:156
  118.4 8.1 %attend_1_0.1 = bf16[1280,128]{1,0:T(8,128)(2,1)S(1)} custom-call(f32[256]{0:T(256)S(1)} %reshape.88.bias_ref, bf16[1280,128]{1,0:T(8,128)(2,1)} %collective-permute-done.2.q_ref, bf16[4,1280,128]{2,1,0:T(8,128)(2,1)S(1)} %pad_maximum_fusion.1.refs_0_, bf16[4,1280,128]{2,1,0:T(8,128)(2,1)S(1)} %collective-permute-done.11.refs_1_, ...), custom_call_target="tpu_custom_call" | custom-call | tf_op jit(solution)/shard_map/attend_1_0/pallas_call | solution.py:242
  127.0 7.8 %attend_3_0.1 = bf16[1280,128]{1,0:T(8,128)(2,1)S(1)} custom-call(f32[256]{0:T(256)S(1)} %reshape.88.bias_ref, bf16[1280,128]{1,0:T(8,128)(2,1)S(1)} %collective-permute-done.8.q_ref, bf16[4,1280,128]{2,1,0:T(8,128)(2,1)S(1)} %pad_maximum_fusion.1.refs_0_, bf16[4,1280,128]{2,1,0:T(8,128)(2,1)S(1)} %collective-permute-done.11.refs_1_, ...), custom_call_target="tpu_custom_call" | custom-call | tf_op jit(solution)/shard_map/attend_3_0/pallas_call | solution.py:242
  134.8 1.9 %collective-permute-start.17 = (bf16[1280,128]{1,0:T(8,128)(2,1)S(1)}, bf16[1280,128]{1,0:T(8,128)(2,1)S(1)}, u32[]{:S(2)}, u32[]{:S(2)}) collective-permute-start(bf16[1280,128]{1,0:T(8,128)(2,1)S(1)} %attend_3_0.1), channel_id=1, source_target_pairs={{0,8},{2,10},{4,12},{6,14},{8,16},{10,18},{12,20},{14,22},{16,24},... | collective-permute-start | bytes 983048 | tf_op jit(solution)/shard_map/ppermute | solution.py:156
  136.7 5.4 %attend_0_0.1.refs_0_ = bf16[768,128]{1,0:T(8,128)(2,1)S(1)} custom-call(f32[256]{0:T(256)S(1)} %reshape.88.bias_ref, bf16[1280,128]{1,0:T(8,128)(2,1)S(1)} %get-tuple-element.104.q_ref, bf16[4,1280,128]{2,1,0:T(8,128)(2,1)S(1)} %pad_maximum_fusion.1.refs_0_, bf16[4,1280,128]{2,1,0:T(8,128)(2,1)S(1)} %collective-permute-done.11.refs_1_, ...), custom_call_target="tpu_custom_call" | custom-call | tf_op jit(solution)/shard_map/attend_0_0/pallas_call | solution.py:242
  142.2 5.5 %collective-permute-done.16.refs_2_ = bf16[1280,128]{1,0:T(8,128)(2,1)S(1)} collective-permute-done((bf16[1280,128]{1,0:T(8,128)(2,1)S(1)}, bf16[1280,128]{1,0:T(8,128)(2,1)S(1)}, u32[]{:S(2)}, u32[]{:S(2)}) %collective-permute-start.16) | collective-permute-done | bytes 327712 | tf_op jit(solution)/shard_map/ppermute | solution.py:156
  147.6 4.4 %attend_0_3.1.refs_1_ = bf16[512,128]{1,0:T(8,128)(2,1)S(1)} custom-call(f32[256]{0:T(256)S(1)} %reshape.88.bias_ref, bf16[1280,128]{1,0:T(8,128)(2,1)S(1)} %get-tuple-element.104.q_ref, bf16[4,1280,128]{2,1,0:T(8,128)(2,1)S(1)} %pad_maximum_fusion.1.refs_0_, bf16[4,1280,128]{2,1,0:T(8,128)(2,1)S(1)} %collective-permute-done.11.refs_1_, ...), custom_call_target="tpu_custom_call" | custom-call | tf_op jit(solution)/shard_map/attend_0_3/pallas_call | solution.py:242
  152.0 1.8 %collect.1 = f32[256,2560]{1,0:T(8,128)} custom-call(s32[1]{0:T(128)} %bitcast.place_ref, bf16[768,128]{1,0:T(8,128)(2,1)S(1)} %attend_0_0.1.refs_0_, bf16[512,128]{1,0:T(8,128)(2,1)S(1)} %attend_0_3.1.refs_1_, bf16[1280,128]{1,0:T(8,128)(2,1)S(1)} %collective-permute-done.16.refs_2_, bf16[1280,128]{1,0:T(8,128)(2,1)S(1)} %collective-permute-done.15.refs_3_, ...), custom_call_target="tpu_custom_call" | custom-call | tf_op jit(solution)/shard_map/collect/pallas_call | solution.py:272
  (75 shorter events, 7.8 us)
Async XLA Ops:
  0.0 9.4 %copy-start.14 = (f32[2560]{0:T(1024)S(1)}, f32[2560]{0:T(1024)}, u32[]{:S(2)}) copy-start(f32[2560]{0:T(1024)} %param.10) | copy-start | bytes 30724
  0.0 9.4 %copy-start.15 = (f32[2560]{0:T(1024)S(1)}, f32[2560]{0:T(1024)}, u32[]{:S(2)}) copy-start(f32[2560]{0:T(1024)} %param.11) | copy-start | bytes 30724
  0.0 1.3 copy-start.6
  2.4 23.9 %collective-permute-start = (bf16[1280,128]{1,0:T(8,128)(2,1)}, bf16[1280,128]{1,0:T(8,128)(2,1)}, u32[]{:S(2)}, u32[]{:S(2)}) collective-permute-start(bf16[1280,128]{1,0:T(8,128)(2,1)} %get-tuple-element.67), channel_id=1, source_target_pairs={{0,8},{2,10},{4,12},{6,14},{8,16},{10,18},{12,20},{14,22},{16,24},... | collective-permute-start | bytes 983048 | tf_op jit(solution)/shard_map/ppermute | solution.py:156
  5.4 24.2 %collective-permute-start.3 = (bf16[1280,128]{1,0:T(8,128)(2,1)}, bf16[1280,128]{1,0:T(8,128)(2,1)}, u32[]{:S(2)}, u32[]{:S(2)}) collective-permute-start(bf16[1280,128]{1,0:T(8,128)(2,1)} %get-tuple-element.72), channel_id=1, source_target_pairs={{0,16},{2,18},{4,20},{6,22},{8,24},{10,26},{12,28},{14,30},{16,0},... | collective-permute-start | bytes 983048 | tf_op jit(solution)/shard_map/ppermute | solution.py:156
  8.0 21.6 %collective-permute-start.6 = (bf16[1280,128]{1,0:T(8,128)(2,1)}, bf16[1280,128]{1,0:T(8,128)(2,1)}, u32[]{:S(2)}, u32[]{:S(2)}) collective-permute-start(bf16[1280,128]{1,0:T(8,128)(2,1)} %get-tuple-element.77), channel_id=1, source_target_pairs={{0,24},{2,26},{4,28},{6,30},{8,0},{10,2},{12,4},{14,6},{16,8},{18,... | collective-permute-start | bytes 983048 | tf_op jit(solution)/shard_map/ppermute | solution.py:156
  9.4 1.7 %copy-start.2 = (f32[256,2560]{1,0:T(8,128)S(1)}, f32[256,2560]{1,0:T(8,128)}, u32[]{:S(2)}) copy-start(f32[256,2560]{1,0:T(8,128)} %q_ref.1) | copy-start | bytes 7864324
  11.1 1.7 %copy-start.4 = (f32[256,2560]{1,0:T(8,128)S(1)}, f32[256,2560]{1,0:T(8,128)}, u32[]{:S(2)}) copy-start(f32[256,2560]{1,0:T(8,128)} %k_ref.1) | copy-start | bytes 7864324
  12.9 10.5 %copy-start.17 = (s32[32]{0:T(128)S(1)}, s32[32]{0:T(128)}, u32[]{:S(2)}) copy-start(s32[32]{0:T(128)} %param.12) | copy-start | bytes 388
  12.9 10.6 %copy-start.16 = (s32[2,32]{1,0:T(2,128)S(1)}, s32[2,32]{1,0:T(2,128)}, u32[]{:S(2)}) copy-start(s32[2,32]{1,0:T(2,128)} %param.13) | copy-start | bytes 772
  12.9 10.7 %copy-start.3 = (f32[256,2560]{1,0:T(8,128)S(1)}, f32[256,2560]{1,0:T(8,128)}, u32[]{:S(2)}) copy-start(f32[256,2560]{1,0:T(8,128)} %q_ref.1) | copy-start | bytes 7864324
  23.6 1.7 %copy-start.5 = (f32[256,2560]{1,0:T(8,128)S(1)}, f32[256,2560]{1,0:T(8,128)}, u32[]{:S(2)}) copy-start(f32[256,2560]{1,0:T(8,128)} %k_ref.1) | copy-start | bytes 7864324
  26.2 45.2 %copy-start.7 = (bf16[1296,128]{1,0:T(8,128)(2,1)}, bf16[1296,128]{1,0:T(8,128)(2,1)S(1)}, u32[]{:S(2)}) copy-start(bf16[1296,128]{1,0:T(8,128)(2,1)S(1)} %get-tuple-element.88) | copy-start | bytes 995332
  26.2 45.5 %copy-start.8 = (bf16[1280,128]{1,0:T(8,128)(2,1)}, bf16[1280,128]{1,0:T(8,128)(2,1)S(1)}, u32[]{:S(2)}) copy-start(bf16[1280,128]{1,0:T(8,128)(2,1)S(1)} %get-tuple-element.69) | copy-start | bytes 983044
  26.2 45.5 %copy-start.9 = (bf16[1280,128]{1,0:T(8,128)(2,1)}, bf16[1280,128]{1,0:T(8,128)(2,1)S(1)}, u32[]{:S(2)}) copy-start(bf16[1280,128]{1,0:T(8,128)(2,1)S(1)} %get-tuple-element.74) | copy-start | bytes 983044
  26.3 45.5 %copy-start.10 = (bf16[1280,128]{1,0:T(8,128)(2,1)}, bf16[1280,128]{1,0:T(8,128)(2,1)S(1)}, u32[]{:S(2)}) copy-start(bf16[1280,128]{1,0:T(8,128)(2,1)S(1)} %get-tuple-element.79) | copy-start | bytes 983044
  31.0 39.3 %collective-permute-start.9 = (bf16[4,1280,128]{2,1,0:T(8,128)(2,1)S(1)}, bf16[4,1280,128]{2,1,0:T(8,128)(2,1)S(1)}, u32[]{:S(2)}, u32[]{:S(2)}) collective-permute-start(bf16[4,1280,128]{2,1,0:T(8,128)(2,1)S(1)} %pad_maximum_fusion.refs_4_), channel_id=1, source_target_pairs={{0,4},{2,6},{4,0},{6,2},{8,12},{10,14},{12,8},{14,10},{16,20},{18,... | collective-permute-start | bytes 3932168 | tf_op jit(solution)/shard_map/ppermute | solution.py:168
  32.6 16.8 %collective-permute-start.7 = (bf16[1296,128]{1,0:T(8,128)(2,1)S(1)}, bf16[1296,128]{1,0:T(8,128)(2,1)S(1)}, u32[]{:S(2)}, u32[]{:S(2)}) collective-permute-start(bf16[1296,128]{1,0:T(8,128)(2,1)S(1)} %get-tuple-element.78), channel_id=1, source_target_pairs={{0,24},{2,26},{4,28},{6,30},{8,0},{10,2},{12,4},{14,6},{16,8},{18,... | collective-permute-start | bytes 995336 | tf_op jit(solution)/shard_map/ppermute | solution.py:156
  41.1 29.2 %collective-permute-start.4 = (bf16[1296,128]{1,0:T(8,128)(2,1)S(1)}, bf16[1296,128]{1,0:T(8,128)(2,1)S(1)}, u32[]{:S(2)}, u32[]{:S(2)}) collective-permute-start(bf16[1296,128]{1,0:T(8,128)(2,1)S(1)} %get-tuple-element.73), channel_id=1, source_target_pairs={{0,16},{2,18},{4,20},{6,22},{8,24},{10,26},{12,28},{14,30},{16,0},... | collective-permute-start | bytes 995336 | tf_op jit(solution)/shard_map/ppermute | solution.py:156
  41.5 28.7 %collective-permute-start.1 = (bf16[1296,128]{1,0:T(8,128)(2,1)S(1)}, bf16[1296,128]{1,0:T(8,128)(2,1)S(1)}, u32[]{:S(2)}, u32[]{:S(2)}) collective-permute-start(bf16[1296,128]{1,0:T(8,128)(2,1)S(1)} %get-tuple-element.68), channel_id=1, source_target_pairs={{0,8},{2,10},{4,12},{6,14},{8,16},{10,18},{12,20},{14,22},{16,24},... | collective-permute-start | bytes 995336 | tf_op jit(solution)/shard_map/ppermute | solution.py:156
  49.4 22.1 %copy-start.11 = (bf16[1296,128]{1,0:T(8,128)(2,1)}, bf16[1296,128]{1,0:T(8,128)(2,1)S(1)}, u32[]{:S(2)}) copy-start(bf16[1296,128]{1,0:T(8,128)(2,1)S(1)} %collective-permute-done.7) | copy-start | bytes 995332
  71.8 30.7 %collective-permute-start.10 = (bf16[4,1280,128]{2,1,0:T(8,128)(2,1)S(1)}, bf16[4,1280,128]{2,1,0:T(8,128)(2,1)}, u32[]{:S(2)}, u32[]{:S(2)}) collective-permute-start(bf16[4,1280,128]{2,1,0:T(8,128)(2,1)S(1)} %pad_maximum_fusion.1.refs_0_), channel_id=1, source_target_pairs={{0,4},{2,6},{4,0},{6,2},{8,12},{10,14},{12,8},{14,10},{16,20},{18,... | collective-permute-start | bytes 3932168 | tf_op jit(solution)/shard_map/ppermute | solution.py:168
  73.2 9.5 %collective-permute-start.8 = (bf16[1280,128]{1,0:T(8,128)(2,1)}, bf16[1280,128]{1,0:T(8,128)(2,1)S(1)}, u32[]{:S(2)}, u32[]{:S(2)}) collective-permute-start(bf16[1280,128]{1,0:T(8,128)(2,1)} %copy-done.10), channel_id=1, source_target_pairs={{0,24},{2,26},{4,28},{6,30},{8,0},{10,2},{12,4},{14,6},{16,8},{18,... | collective-permute-start | bytes 983048 | tf_op jit(solution)/shard_map/ppermute | solution.py:156
  73.2 29.2 %collective-permute-start.5 = (bf16[1280,128]{1,0:T(8,128)(2,1)}, bf16[1280,128]{1,0:T(8,128)(2,1)}, u32[]{:S(2)}, u32[]{:S(2)}) collective-permute-start(bf16[1280,128]{1,0:T(8,128)(2,1)} %copy-done.9), channel_id=1, source_target_pairs={{0,16},{2,18},{4,20},{6,22},{8,24},{10,26},{12,28},{14,30},{16,0},... | collective-permute-start | bytes 983048 | tf_op jit(solution)/shard_map/ppermute | solution.py:156
  74.6 27.9 %collective-permute-start.2 = (bf16[1280,128]{1,0:T(8,128)(2,1)}, bf16[1280,128]{1,0:T(8,128)(2,1)}, u32[]{:S(2)}, u32[]{:S(2)}) collective-permute-start(bf16[1280,128]{1,0:T(8,128)(2,1)} %copy-done.8), channel_id=1, source_target_pairs={{0,8},{2,10},{4,12},{6,14},{8,16},{10,18},{12,20},{14,22},{16,24},... | collective-permute-start | bytes 983048 | tf_op jit(solution)/shard_map/ppermute | solution.py:156
  78.7 24.2 %collective-permute-start.13 = (bf16[4,1280,128]{2,1,0:T(8,128)(2,1)S(1)}, bf16[4,1280,128]{2,1,0:T(8,128)(2,1)S(1)}, u32[]{:S(2)}, u32[]{:S(2)}) collective-permute-start(bf16[4,1280,128]{2,1,0:T(8,128)(2,1)S(1)} %pad_maximum_fusion.refs_4_), channel_id=1, source_target_pairs={{0,2},{2,0},{4,6},{6,4},{8,10},{10,8},{12,14},{14,12},{16,18},{18,... | collective-permute-start | bytes 3932168 | tf_op jit(solution)/shard_map/ppermute | solution.py:168
  82.7 20.2 %collective-permute-start.14 = (bf16[4,1280,128]{2,1,0:T(8,128)(2,1)}, bf16[4,1280,128]{2,1,0:T(8,128)(2,1)S(1)}, u32[]{:S(2)}, u32[]{:S(2)}) collective-permute-start(bf16[4,1280,128]{2,1,0:T(8,128)(2,1)} %copy-done), channel_id=1, source_target_pairs={{0,2},{2,0},{4,6},{6,4},{8,10},{10,8},{12,14},{14,12},{16,18},{18,... | collective-permute-start | bytes 3932168 | tf_op jit(solution)/shard_map/ppermute | solution.py:168
  102.4 4.2 %collective-permute-start.11 = (bf16[4,1280,128]{2,1,0:T(8,128)(2,1)S(1)}, bf16[4,1280,128]{2,1,0:T(8,128)(2,1)S(1)}, u32[]{:S(2)}, u32[]{:S(2)}) collective-permute-start(bf16[4,1280,128]{2,1,0:T(8,128)(2,1)S(1)} %pad_maximum_fusion.1.refs_0_), channel_id=1, source_target_pairs={{0,2},{2,0},{4,6},{6,4},{8,10},{10,8},{12,14},{14,12},{16,18},{18,... | collective-permute-start | bytes 3932168 | tf_op jit(solution)/shard_map/ppermute | solution.py:168
  102.4 5.1 %collective-permute-start.12 = (bf16[4,1280,128]{2,1,0:T(8,128)(2,1)}, bf16[4,1280,128]{2,1,0:T(8,128)(2,1)S(1)}, u32[]{:S(2)}, u32[]{:S(2)}) collective-permute-start(bf16[4,1280,128]{2,1,0:T(8,128)(2,1)} %collective-permute-done.10.refs_2_), channel_id=1, source_target_pairs={{0,2},{2,0},{4,6},{6,4},{8,10},{10,8},{12,14},{14,12},{16,18},{18,... | collective-permute-start | bytes 3932168 | tf_op jit(solution)/shard_map/ppermute | solution.py:168
  116.8 19.9 %collective-permute-start.15 = (bf16[1280,128]{1,0:T(8,128)(2,1)S(1)}, bf16[1280,128]{1,0:T(8,128)(2,1)S(1)}, u32[]{:S(2)}, u32[]{:S(2)}) collective-permute-start(bf16[1280,128]{1,0:T(8,128)(2,1)S(1)} %attend_2_0.1), channel_id=1, source_target_pairs={{0,16},{2,18},{4,20},{6,22},{8,24},{10,26},{12,28},{14,30},{16,0},... | collective-permute-start | bytes 983048 | tf_op jit(solution)/shard_map/ppermute | solution.py:156
  126.5 21.1 %collective-permute-start.16 = (bf16[1280,128]{1,0:T(8,128)(2,1)S(1)}, bf16[1280,128]{1,0:T(8,128)(2,1)S(1)}, u32[]{:S(2)}, u32[]{:S(2)}) collective-permute-start(bf16[1280,128]{1,0:T(8,128)(2,1)S(1)} %attend_1_0.1), channel_id=1, source_target_pairs={{0,24},{2,26},{4,28},{6,30},{8,0},{10,2},{12,4},{14,6},{16,8},{18,... | collective-permute-start | bytes 983048 | tf_op jit(solution)/shard_map/ppermute | solution.py:156
  134.8 17.2 %collective-permute-start.17 = (bf16[1280,128]{1,0:T(8,128)(2,1)S(1)}, bf16[1280,128]{1,0:T(8,128)(2,1)S(1)}, u32[]{:S(2)}, u32[]{:S(2)}) collective-permute-start(bf16[1280,128]{1,0:T(8,128)(2,1)S(1)} %attend_3_0.1), channel_id=1, source_target_pairs={{0,8},{2,10},{4,12},{6,14},{8,16},{10,18},{12,20},{14,22},{16,24},... | collective-permute-start | bytes 983048 | tf_op jit(solution)/shard_map/ppermute | solution.py:156
  (4 other events, 5.0 us)

commit v4 on v3

--- a/solution.py
+++ b/solution.py
@@ -64,22 +64,26 @@
         k_out[per_group * rows :, :] = mask_ref[...]
 
 
-def attend_kernel(bias_ref, q_ref, *refs, query_slot, groups, layers, heads, scale):
+def attend_kernel(bias_ref, *refs, query_slots, groups, layers, heads, scale):
+    count = len(query_slots)
+    q_refs, refs = refs[:count], refs[count:]
     k_refs, v_refs = refs[:layers], refs[layers : 2 * layers]
-    out, scores = refs[-2:]
-    rows = out.shape[0] // len(heads)
+    outs, scores = refs[2 * layers : -1], refs[-1]
+    rows = outs[0].shape[0] // heads
     blk = rows // BLOCK
     slots = groups * layers
     lowest = jnp.full((rows, BLOCK), blocked, jnp.float32)
     ones = jnp.ones((rows, HEAD_DIM), jnp.bfloat16)
-
-    def score(head, slot, top, q):
+    units = [(i, head) for head in range(heads) for i in range(count)]
+
+    def score(u, slot, top, q):
+        i, head = units[u]
         keys = k_refs[slot // groups][slot % groups, head * rows : (head + 1) * rows, :]
         wide = jnp.concatenate(
             [keys[b * HEAD_DIM : (b + 1) * HEAD_DIM] for b in range(blk)], axis=1
         )
         products = jnp.dot(q, wide, preferred_element_type=jnp.float32)
-        first = (query_slot * slots + slot) * blk
+        first = (query_slots[i] * slots + slot) * blk
         for b in range(blk):
             columns = slice(b * BLOCK, (b + 1) * BLOCK)
             block = jnp.concatenate(
@@ -89,49 +93,48 @@
                 ],
                 axis=0,
             )
-            scores[head % 2, slot, :, columns] = block
+            scores[u % 2, slot, :, columns] = block
             top = jnp.maximum(top, block)
         return top
 
-    def weigh(head, slot, row_max, mixed):
-        weights = jnp.exp2((scores[head % 2, slot] - row_max) * scale).astype(jnp.bfloat16)
+    def weigh(u, slot, row_max, mixed):
+        head = units[u][1]
+        weights = jnp.exp2((scores[u % 2, slot] - row_max) * scale).astype(jnp.bfloat16)
         values = v_refs[slot // groups][slot % groups, head * rows : (head + 1) * rows, :]
         return mixed + jnp.dot(
             weights, jnp.concatenate([values, ones], axis=1), preferred_element_type=jnp.float32
         )
 
-    top, q = lowest, q_ref[heads[0] * rows : (heads[0] + 1) * rows, :]
+    def queries(u):
+        i, head = units[u]
+        return q_refs[i][head * rows : (head + 1) * rows, :]
+
+    top, q = lowest, queries(0)
     for slot in range(slots):
-        top = score(heads[0], slot, top, q)
-    for head in heads:
+        top = score(0, slot, top, q)
+    for u, (i, head) in enumerate(units):
         row_max = jnp.max(top, axis=1, keepdims=True)
         mixed, top = jnp.zeros((rows, 2 * HEAD_DIM), jnp.float32), lowest
-        if head + 1 in heads:
-            q = q_ref[(head + 1) * rows : (head + 2) * rows, :]
+        if u + 1 < len(units):
+            q = queries(u + 1)
         for slot in range(slots):
-            if head + 1 in heads:
-                top = score(head + 1, slot, top, q)
-            mixed = weigh(head, slot, row_max, mixed)
-        low = (head - heads[0]) * rows
-        out[low : low + rows, :] = (
+            if u + 1 < len(units):
+                top = score(u + 1, slot, top, q)
+            mixed = weigh(u, slot, row_max, mixed)
+        outs[i][head * rows : (head + 1) * rows, :] = (
             mixed[:, :HEAD_DIM] / mixed[:, HEAD_DIM : HEAD_DIM + 1]
         ).astype(jnp.bfloat16)
 
 
-def collect_kernel(place_ref, *refs, groups, per_group):
+def collect_kernel(place_ref, *refs, per_group):
     out = refs[-1]
+    groups = len(refs) - 1
     rows = out.shape[0]
-    first = refs[0].shape[0] // rows
     for shift in range(groups):
         for head in range(per_group):
-            if shift:
-                ref, low = refs[shift + 1], head * rows
-            elif head < first:
-                ref, low = refs[0], head * rows
-            else:
-                ref, low = refs[1], (head - first) * rows
             column = column_of(place_ref, shift, head, groups, per_group)
-            out[:, pl.ds(column, HEAD_DIM)] = ref[low : low + rows, :].astype(jnp.float32)
+            piece = refs[shift][head * rows : (head + 1) * rows, :]
+            out[:, pl.ds(column, HEAD_DIM)] = piece.astype(jnp.float32)
 
 
 def exchanged(q_in, k_in, v_in, q_gain, k_gain, frames, adjacent, *, groups):
@@ -156,12 +159,12 @@
         return lax.ppermute(x, "seq", pairs)
 
     def exchange(pieces, after=None):
-        arrived = [pieces[0]]
-        for s in range(1, groups):
-            piece = pieces[s]
+        shifts = range(1, groups)
+        arrived = list(pieces)
+        for s in shifts:
             if after is not None:
-                piece, after[s] = lax.optimization_barrier((piece, after[s]))
-            arrived.append(rotated(piece, s))
+                arrived[s], after[s] = lax.optimization_barrier((arrived[s], after[s]))
+            arrived[s] = rotated(arrived[s], s)
         return arrived
 
     def swapped(x, bit):
@@ -238,45 +241,43 @@
     keys = [keys[i] for i in range(layers)]
 
     scale = math.log2(math.e) / math.sqrt(HEAD_DIM)
-    def attend(g, heads, bias):
+    def attend(query_slots, bias):
         return pl.pallas_call(
             functools.partial(
                 attend_kernel,
-                query_slot=g,
+                query_slots=query_slots,
                 groups=groups,
                 layers=layers,
-                heads=heads,
+                heads=per_group,
                 scale=scale,
             ),
-            in_specs=[SMEM] + [VMEM] * (1 + 2 * layers),
-            out_specs=VMEM,
+            in_specs=[SMEM] + [VMEM] * (len(query_slots) + 2 * layers),
+            out_specs=[VMEM] * len(query_slots),
             scratch_shapes=[pltpu.VMEM((2, devices, rows, rows), f32)],
-            out_shape=jax.ShapeDtypeStruct((len(heads) * rows, HEAD_DIM), bf16),
+            out_shape=[jax.ShapeDtypeStruct((per_group * rows, HEAD_DIM), bf16)] * len(query_slots),
             compiler_params=params,
-            name=f"attend_{g}_{heads[0]}",
-        )(bias, q_arrived[g], *keys, *values)
-
-    order = sorted(range(1, groups), key=lambda s: abs(2 * s - groups))
-    outputs, last = [None] * groups, None
-    for g in order:
-        own = attend(g, range(per_group), bias)
-        outputs[g] = rotated(own, groups - g)
+            name="attend_" + "_".join(str(g) for g in query_slots),
+        )(bias, *[q_arrived[g] for g in query_slots], *keys, *values)
+
+    outputs = [None] * groups
+    far = groups // 2
+    near = tuple(g for g in range(1, groups) if g != far)
+    for query_slots in ((far,), near, (0,)):
+        if query_slots == (0,):
+            outputs[far], bias = lax.optimization_barrier((outputs[far], bias))
+        own = attend(query_slots, bias)
         own, bias = lax.optimization_barrier((own, bias))
-    parts = []
-    for i, heads in enumerate((range(per_group - 2), range(per_group - 2, per_group))):
-        if i < len(order) - 1:
-            outputs[order[i]], bias = lax.optimization_barrier((outputs[order[i]], bias))
-        parts.append(attend(0, heads, bias))
-        parts[-1], bias = lax.optimization_barrier((parts[-1], bias))
+        for g, x in zip(query_slots, own):
+            outputs[g] = rotated(x, groups - g) if g else x
 
     return pl.pallas_call(
-        functools.partial(collect_kernel, groups=groups, per_group=per_group),
+        functools.partial(collect_kernel, per_group=per_group),
         out_shape=jax.ShapeDtypeStruct((rows, width), f32),
-        in_specs=[SMEM] + [VMEM] * (groups + 1),
+        in_specs=[SMEM] + [VMEM] * groups,
         out_specs=VMEM,
         compiler_params=params,
         name="collect",
-    )(place_row, *parts, *outputs[1:])
+    )(place_row, *outputs)
 
 
 def normalized(inputs, gain_row, square_sum, full_width):
@@ -356,7 +357,8 @@
 def groups_of(mesh, heads):
     layers = 4
     groups = mesh.shape["seq"] // layers
-    fits = mesh.shape["seq"] % layers == 0 and heads % groups == 0 and heads >= 2 * groups
+    fits = groups & (groups - 1) == 0 and mesh.shape["seq"] == groups * layers
+    fits = fits and heads % groups == 0 and heads >= 3 * groups
     return groups if fits else 1
 
 

time: 154 us -> 152 us (0.987)
  Pallas kernels: 37.8 us -> 34 us
  waiting for transfers between devices: 65.6 us -> 67.6 us
    pallas_call x6 -> x4, Pallas kernels: 35.4 us -> 31.7 us  [the longest x3 29.9 us: attend(): pl.pallas_call(functools.partial(attend_kernel, query_slots=query_slots,...]
    ppermute x12, waiting for transfers between devices: 61 us -> 63 us  [rotated(): return lax.ppermute(x, 'seq', pairs)]
  transfers between devices with their start and end apart: 18 -> 18, of which waited for: 8 -> 8; matrix products, arithmetic and copies ran while one was open for 3% -> 3% of each run, Pallas kernels for 18% -> 15%
where the time goes in v4:
time: 152 us
  waiting for transfers between devices  67.6 us (44%)
  Pallas kernels  34 us (22%)
  starting transfers between devices  25.2 us (17%)
  local copies, waits for them, and re-layouts  12.7 us (8%)
  blocking collectives  10.1 us (7%)
  other arithmetic  1.74 us (1%)
    ppermute x12, waiting for transfers between devices, rotated(): return lax.ppermute(x, 'seq', pairs)  63 us
    pallas_call x3, Pallas kernels, attend(): pl.pallas_call(functools.partial(attend_kernel, query_slots=query_slots,...  29.9 us
    ppermute x12, starting transfers between devices, rotated(): return lax.ppermute(x, 'seq', pairs)  22.5 us
    psum x1, blocking collectives, exchanged(): sums = lax.psum(sums, 'tensor')  10.1 us
    unnamed x36, local copies, waits for them, and re-layouts  9.03 us
    ppermute x6, waiting for transfers between devices, swapped(): return lax.ppermute(x, 'seq', [(i, i ^ bit) for i in range(devices)])  4.61 us
  transfers between devices with their start and end apart: 18, of which 8 were waited for; matrix products, arithmetic and copies ran while one was open for 3% of the time, Pallas kernels for 15%

profile of v4, /device:TPU:0, one launch (start us, length us, event | category | flops | bytes accessed | tf_op | source)
XLA Modules:
  0.0 151.8 jit_solution(6764486899190515200)
XLA Ops:
  0.0 1.3 copy-done.6
  1.3 1.0 value_pieces.1
  2.4 3.0 %collective-permute-start = (bf16[1280,128]{1,0:T(8,128)(2,1)}, bf16[1280,128]{1,0:T(8,128)(2,1)}, u32[]{:S(2)}, u32[]{:S(2)}) collective-permute-start(bf16[1280,128]{1,0:T(8,128)(2,1)} %get-tuple-element.67), channel_id=1, source_target_pairs={{0,8},{2,10},{4,12},{6,14},{8,16},{10,18},{12,20},{14,22},{16,24},... | collective-permute-start | bytes 983048 | tf_op jit(solution)/shard_map/ppermute | solution.py:159
  5.4 2.6 %collective-permute-start.3 = (bf16[1280,128]{1,0:T(8,128)(2,1)}, bf16[1280,128]{1,0:T(8,128)(2,1)}, u32[]{:S(2)}, u32[]{:S(2)}) collective-permute-start(bf16[1280,128]{1,0:T(8,128)(2,1)} %get-tuple-element.72), channel_id=1, source_target_pairs={{0,16},{2,18},{4,20},{6,22},{8,24},{10,26},{12,28},{14,30},{16,0},... | collective-permute-start | bytes 983048 | tf_op jit(solution)/shard_map/ppermute | solution.py:159
  8.0 1.3 collective-permute-start.6
  9.4 1.7 %copy-done.2 = f32[256,2560]{1,0:T(8,128)S(1)} copy-done((f32[256,2560]{1,0:T(8,128)S(1)}, f32[256,2560]{1,0:T(8,128)}, u32[]{:S(2)}) %copy-start.2) | copy-done | bytes 2621464
  11.1 1.7 %copy-done.4 = f32[256,2560]{1,0:T(8,128)S(1)} copy-done((f32[256,2560]{1,0:T(8,128)S(1)}, f32[256,2560]{1,0:T(8,128)}, u32[]{:S(2)}) %copy-start.4) | copy-done | bytes 2621464
  13.3 10.1 %psum.7.sums_ref = f32[256,2]{1,0:T(8,128)S(1)} all-reduce(f32[256,2]{1,0:T(8,128)S(1)} %square_sums.1), channel_id=1, replica_groups=mesh['seq'=16,'tensor'=2] {'tensor'}, use_global_device_ids=true, to_apply=%region_0.1 | all-reduce | flops 512 | bytes 4096 | tf_op jit(solution)/shard_map/psum | solution.py:196
  23.6 1.7 %copy-done.5 = f32[256,2560]{1,0:T(8,128)S(1)} copy-done((f32[256,2560]{1,0:T(8,128)S(1)}, f32[256,2560]{1,0:T(8,128)}, u32[]{:S(2)}) %copy-start.5) | copy-done | bytes 2621464
  25.3 0.9 norm_pieces.1
  26.3 3.4 %collective-permute-done.3 = bf16[1280,128]{1,0:T(8,128)(2,1)} collective-permute-done((bf16[1280,128]{1,0:T(8,128)(2,1)}, bf16[1280,128]{1,0:T(8,128)(2,1)}, u32[]{:S(2)}, u32[]{:S(2)}) %collective-permute-start.3) | collective-permute-done | bytes 327712 | tf_op jit(solution)/shard_map/ppermute | solution.py:159
  29.6 1.3 pad_maximum_fusion.refs_5_.refs_6_
  31.0 1.6 %collective-permute-start.9 = (bf16[4,1280,128]{2,1,0:T(8,128)(2,1)S(1)}, bf16[4,1280,128]{2,1,0:T(8,128)(2,1)S(1)}, u32[]{:S(2)}, u32[]{:S(2)}) collective-permute-start(bf16[4,1280,128]{2,1,0:T(8,128)(2,1)S(1)} %pad_maximum_fusion.refs_5_.refs_6_), channel_id=1, source_target_pairs={{0,4},{2,6},{4,0},{6,2},{8,12},{10,14},{12,8},{14,10},{16,20},{18,... | collective-permute-start | bytes 3932168 | tf_op jit(solution)/shard_map/ppermute | solution.py:171
  32.6 8.5 %collective-permute-start.7 = (bf16[1296,128]{1,0:T(8,128)(2,1)S(1)}, bf16[1296,128]{1,0:T(8,128)(2,1)S(1)}, u32[]{:S(2)}, u32[]{:S(2)}) collective-permute-start(bf16[1296,128]{1,0:T(8,128)(2,1)S(1)} %get-tuple-element.78), channel_id=1, source_target_pairs={{0,24},{2,26},{4,28},{6,30},{8,0},{10,2},{12,4},{14,6},{16,8},{18,... | collective-permute-start | bytes 995336 | tf_op jit(solution)/shard_map/ppermute | solution.py:159
  41.7 7.6 %collective-permute-done.7 = bf16[1296,128]{1,0:T(8,128)(2,1)S(1)} collective-permute-done((bf16[1296,128]{1,0:T(8,128)(2,1)S(1)}, bf16[1296,128]{1,0:T(8,128)(2,1)S(1)}, u32[]{:S(2)}, u32[]{:S(2)}) %collective-permute-start.7) | collective-permute-done | bytes 331808 | tf_op jit(solution)/shard_map/ppermute | solution.py:159
  49.4 20.9 %collective-permute-done.4 = bf16[1296,128]{1,0:T(8,128)(2,1)S(1)} collective-permute-done((bf16[1296,128]{1,0:T(8,128)(2,1)S(1)}, bf16[1296,128]{1,0:T(8,128)(2,1)S(1)}, u32[]{:S(2)}, u32[]{:S(2)}) %collective-permute-start.4) | collective-permute-done | bytes 331808 | tf_op jit(solution)/shard_map/ppermute | solution.py:159
  70.3 1.1 copy-done
  72.5 0.7 slice_bitcast_fusion.7
  73.2 1.4 collective-permute-start.5
  74.6 1.4 collective-permute-start.2
  78.8 3.9 %collective-permute-done.8.refs_1_ = bf16[1280,128]{1,0:T(8,128)(2,1)S(1)} collective-permute-done((bf16[1280,128]{1,0:T(8,128)(2,1)}, bf16[1280,128]{1,0:T(8,128)(2,1)S(1)}, u32[]{:S(2)}, u32[]{:S(2)}) %collective-permute-start.8) | collective-permute-done | bytes 327712 | tf_op jit(solution)/shard_map/ppermute | solution.py:159
  82.7 19.7 %collective-permute-done.5.refs_0_ = bf16[1280,128]{1,0:T(8,128)(2,1)} collective-permute-done((bf16[1280,128]{1,0:T(8,128)(2,1)}, bf16[1280,128]{1,0:T(8,128)(2,1)}, u32[]{:S(2)}, u32[]{:S(2)}) %collective-permute-start.5) | collective-permute-done | bytes 327712 | tf_op jit(solution)/shard_map/ppermute | solution.py:159
  103.0 3.7 %collective-permute-done.11.refs_2_.refs_3_ = bf16[4,1280,128]{2,1,0:T(8,128)(2,1)S(1)} collective-permute-done((bf16[4,1280,128]{2,1,0:T(8,128)(2,1)S(1)}, bf16[4,1280,128]{2,1,0:T(8,128)(2,1)S(1)}, u32[]{:S(2)}, u32[]{:S(2)}) %collective-permute-start.11) | collective-permute-done | bytes 1310752 | tf_op jit(solution)/shard_map/ppermute | solution.py:171
  106.6 0.9 collective-permute-done.12.refs_4_.refs_5_
  107.6 1.3 copy-done.1
  108.9 7.9 %attend_2.1 = bf16[1280,128]{1,0:T(8,128)(2,1)S(1)} custom-call(f32[256]{0:T(256)S(1)} %reshape.88.bias_ref, bf16[1280,128]{1,0:T(8,128)(2,1)} %collective-permute-done.5.refs_0_, bf16[4,1280,128]{2,1,0:T(8,128)(2,1)S(1)} %pad_maximum_fusion.1.refs_1_.refs_2_, bf16[4,1280,128]{2,1,0:T(8,128)(2,1)S(1)} %collective-permute-done.11.refs_2_.refs_3_, ...), custom_call_target="tpu_custom_call" | custom-call | tf_op jit(solution)/shard_map/attend_2/pallas_call | solution.py:245
  116.8 1.6 %collective-permute-start.15 = (bf16[1280,128]{1,0:T(8,128)(2,1)S(1)}, bf16[1280,128]{1,0:T(8,128)(2,1)S(1)}, u32[]{:S(2)}, u32[]{:S(2)}) collective-permute-start(bf16[1280,128]{1,0:T(8,128)(2,1)S(1)} %attend_2.1), channel_id=1, source_target_pairs={{0,16},{2,18},{4,20},{6,22},{8,24},{10,26},{12,28},{14,30},{16,0},... | collective-permute-start | bytes 983048 | tf_op jit(solution)/shard_map/ppermute | solution.py:159
  118.4 14.2 %attend_1_3.1 = (bf16[1280,128]{1,0:T(8,128)(2,1)S(1)}, bf16[1280,128]{1,0:T(8,128)(2,1)S(1)}) custom-call(f32[256]{0:T(256)S(1)} %reshape.88.bias_ref, bf16[1280,128]{1,0:T(8,128)(2,1)} %collective-permute-done.2.refs_0_, bf16[1280,128]{1,0:T(8,128)(2,1)S(1)} %collective-permute-done.8.refs_1_, bf16[4,1280,128]{2,1,0:T(8,128)(2,1)S(1)} %pad_maximum_fusion.1.refs_1_.refs_2_, ...), custom_call_target="tpu_custom_call" | custom-call | tf_op jit(solution)/shard_map/attend_1_3/pallas_call | solution.py:245
  133.1 1.6 %collective-permute-start.17 = (bf16[1280,128]{1,0:T(8,128)(2,1)S(1)}, bf16[1280,128]{1,0:T(8,128)(2,1)S(1)}, u32[]{:S(2)}, u32[]{:S(2)}) collective-permute-start(bf16[1280,128]{1,0:T(8,128)(2,1)S(1)} %get-tuple-element.110), channel_id=1, source_target_pairs={{0,8},{2,10},{4,12},{6,14},{8,16},{10,18},{12,20},{14,22},{16,24},... | collective-permute-start | bytes 983048 | tf_op jit(solution)/shard_map/ppermute | solution.py:159
  134.7 7.8 %attend_0.1.refs_0_ = bf16[1280,128]{1,0:T(8,128)(2,1)S(1)} custom-call(f32[256]{0:T(256)S(1)} %reshape.88.bias_ref, bf16[1280,128]{1,0:T(8,128)(2,1)S(1)} %get-tuple-element.106.refs_0_, bf16[4,1280,128]{2,1,0:T(8,128)(2,1)S(1)} %pad_maximum_fusion.1.refs_1_.refs_2_, bf16[4,1280,128]{2,1,0:T(8,128)(2,1)S(1)} %collective-permute-done.11.refs_2_.refs_3_, ...), custom_call_target="tpu_custom_call" | custom-call | tf_op jit(solution)/shard_map/attend_0/pallas_call | solution.py:245
  142.5 7.5 %collective-permute-done.17.refs_3_ = bf16[1280,128]{1,0:T(8,128)(2,1)S(1)} collective-permute-done((bf16[1280,128]{1,0:T(8,128)(2,1)S(1)}, bf16[1280,128]{1,0:T(8,128)(2,1)S(1)}, u32[]{:S(2)}, u32[]{:S(2)}) %collective-permute-start.17) | collective-permute-done | bytes 327712 | tf_op jit(solution)/shard_map/ppermute | solution.py:159
  149.9 1.8 %collect.1 = f32[256,2560]{1,0:T(8,128)} custom-call(s32[1]{0:T(128)} %bitcast.place_ref, bf16[1280,128]{1,0:T(8,128)(2,1)S(1)} %attend_0.1.refs_0_, bf16[1280,128]{1,0:T(8,128)(2,1)S(1)} %collective-permute-done.16.refs_1_, bf16[1280,128]{1,0:T(8,128)(2,1)S(1)} %collective-permute-done.15.refs_2_, bf16[1280,128]{1,0:T(8,128)(2,1)S(1)} %collective-permute-done.17.refs_3_), custom_call_target="tpu_custom_call" | custom-call | tf_op jit(solution)/shard_map/collect/pallas_call | solution.py:273
  (73 shorter events, 6.3 us)
Async XLA Ops:
  0.0 9.4 %copy-start.14 = (f32[2560]{0:T(1024)S(1)}, f32[2560]{0:T(1024)}, u32[]{:S(2)}) copy-start(f32[2560]{0:T(1024)} %param.10) | copy-start | bytes 30724
  0.0 9.4 %copy-start.15 = (f32[2560]{0:T(1024)S(1)}, f32[2560]{0:T(1024)}, u32[]{:S(2)}) copy-start(f32[2560]{0:T(1024)} %param.11) | copy-start | bytes 30724
  0.0 1.3 copy-start.6
  2.4 23.9 %collective-permute-start = (bf16[1280,128]{1,0:T(8,128)(2,1)}, bf16[1280,128]{1,0:T(8,128)(2,1)}, u32[]{:S(2)}, u32[]{:S(2)}) collective-permute-start(bf16[1280,128]{1,0:T(8,128)(2,1)} %get-tuple-element.67), channel_id=1, source_target_pairs={{0,8},{2,10},{4,12},{6,14},{8,16},{10,18},{12,20},{14,22},{16,24},... | collective-permute-start | bytes 983048 | tf_op jit(solution)/shard_map/ppermute | solution.py:159
  5.4 24.2 %collective-permute-start.3 = (bf16[1280,128]{1,0:T(8,128)(2,1)}, bf16[1280,128]{1,0:T(8,128)(2,1)}, u32[]{:S(2)}, u32[]{:S(2)}) collective-permute-start(bf16[1280,128]{1,0:T(8,128)(2,1)} %get-tuple-element.72), channel_id=1, source_target_pairs={{0,16},{2,18},{4,20},{6,22},{8,24},{10,26},{12,28},{14,30},{16,0},... | collective-permute-start | bytes 983048 | tf_op jit(solution)/shard_map/ppermute | solution.py:159
  8.0 21.6 %collective-permute-start.6 = (bf16[1280,128]{1,0:T(8,128)(2,1)}, bf16[1280,128]{1,0:T(8,128)(2,1)}, u32[]{:S(2)}, u32[]{:S(2)}) collective-permute-start(bf16[1280,128]{1,0:T(8,128)(2,1)} %get-tuple-element.77), channel_id=1, source_target_pairs={{0,24},{2,26},{4,28},{6,30},{8,0},{10,2},{12,4},{14,6},{16,8},{18,... | collective-permute-start | bytes 983048 | tf_op jit(solution)/shard_map/ppermute | solution.py:159
  9.4 1.7 %copy-start.2 = (f32[256,2560]{1,0:T(8,128)S(1)}, f32[256,2560]{1,0:T(8,128)}, u32[]{:S(2)}) copy-start(f32[256,2560]{1,0:T(8,128)} %q_ref.1) | copy-start | bytes 7864324
  11.1 1.7 %copy-start.4 = (f32[256,2560]{1,0:T(8,128)S(1)}, f32[256,2560]{1,0:T(8,128)}, u32[]{:S(2)}) copy-start(f32[256,2560]{1,0:T(8,128)} %k_ref.1) | copy-start | bytes 7864324
  12.9 10.5 %copy-start.17 = (s32[32]{0:T(128)S(1)}, s32[32]{0:T(128)}, u32[]{:S(2)}) copy-start(s32[32]{0:T(128)} %param.12) | copy-start | bytes 388
  12.9 10.6 %copy-start.16 = (s32[2,32]{1,0:T(2,128)S(1)}, s32[2,32]{1,0:T(2,128)}, u32[]{:S(2)}) copy-start(s32[2,32]{1,0:T(2,128)} %param.13) | copy-start | bytes 772
  12.9 10.7 %copy-start.3 = (f32[256,2560]{1,0:T(8,128)S(1)}, f32[256,2560]{1,0:T(8,128)}, u32[]{:S(2)}) copy-start(f32[256,2560]{1,0:T(8,128)} %q_ref.1) | copy-start | bytes 7864324
  23.6 1.7 %copy-start.5 = (f32[256,2560]{1,0:T(8,128)S(1)}, f32[256,2560]{1,0:T(8,128)}, u32[]{:S(2)}) copy-start(f32[256,2560]{1,0:T(8,128)} %k_ref.1) | copy-start | bytes 7864324
  26.2 45.2 %copy-start.7 = (bf16[1296,128]{1,0:T(8,128)(2,1)}, bf16[1296,128]{1,0:T(8,128)(2,1)S(1)}, u32[]{:S(2)}) copy-start(bf16[1296,128]{1,0:T(8,128)(2,1)S(1)} %get-tuple-element.88) | copy-start | bytes 995332
  26.2 45.5 %copy-start.8 = (bf16[1280,128]{1,0:T(8,128)(2,1)}, bf16[1280,128]{1,0:T(8,128)(2,1)S(1)}, u32[]{:S(2)}) copy-start(bf16[1280,128]{1,0:T(8,128)(2,1)S(1)} %get-tuple-element.69) | copy-start | bytes 983044
  26.2 45.5 %copy-start.9 = (bf16[1280,128]{1,0:T(8,128)(2,1)}, bf16[1280,128]{1,0:T(8,128)(2,1)S(1)}, u32[]{:S(2)}) copy-start(bf16[1280,128]{1,0:T(8,128)(2,1)S(1)} %get-tuple-element.74) | copy-start | bytes 983044
  26.3 45.5 %copy-start.10 = (bf16[1280,128]{1,0:T(8,128)(2,1)}, bf16[1280,128]{1,0:T(8,128)(2,1)S(1)}, u32[]{:S(2)}) copy-start(bf16[1280,128]{1,0:T(8,128)(2,1)S(1)} %get-tuple-element.79) | copy-start | bytes 983044
  31.0 39.3 %collective-permute-start.9 = (bf16[4,1280,128]{2,1,0:T(8,128)(2,1)S(1)}, bf16[4,1280,128]{2,1,0:T(8,128)(2,1)S(1)}, u32[]{:S(2)}, u32[]{:S(2)}) collective-permute-start(bf16[4,1280,128]{2,1,0:T(8,128)(2,1)S(1)} %pad_maximum_fusion.refs_5_.refs_6_), channel_id=1, source_target_pairs={{0,4},{2,6},{4,0},{6,2},{8,12},{10,14},{12,8},{14,10},{16,20},{18,... | collective-permute-start | bytes 3932168 | tf_op jit(solution)/shard_map/ppermute | solution.py:171
  32.6 16.8 %collective-permute-start.7 = (bf16[1296,128]{1,0:T(8,128)(2,1)S(1)}, bf16[1296,128]{1,0:T(8,128)(2,1)S(1)}, u32[]{:S(2)}, u32[]{:S(2)}) collective-permute-start(bf16[1296,128]{1,0:T(8,128)(2,1)S(1)} %get-tuple-element.78), channel_id=1, source_target_pairs={{0,24},{2,26},{4,28},{6,30},{8,0},{10,2},{12,4},{14,6},{16,8},{18,... | collective-permute-start | bytes 995336 | tf_op jit(solution)/shard_map/ppermute | solution.py:159
  41.1 29.2 %collective-permute-start.4 = (bf16[1296,128]{1,0:T(8,128)(2,1)S(1)}, bf16[1296,128]{1,0:T(8,128)(2,1)S(1)}, u32[]{:S(2)}, u32[]{:S(2)}) collective-permute-start(bf16[1296,128]{1,0:T(8,128)(2,1)S(1)} %get-tuple-element.73), channel_id=1, source_target_pairs={{0,16},{2,18},{4,20},{6,22},{8,24},{10,26},{12,28},{14,30},{16,0},... | collective-permute-start | bytes 995336 | tf_op jit(solution)/shard_map/ppermute | solution.py:159
  41.5 28.7 %collective-permute-start.1 = (bf16[1296,128]{1,0:T(8,128)(2,1)S(1)}, bf16[1296,128]{1,0:T(8,128)(2,1)S(1)}, u32[]{:S(2)}, u32[]{:S(2)}) collective-permute-start(bf16[1296,128]{1,0:T(8,128)(2,1)S(1)} %get-tuple-element.68), channel_id=1, source_target_pairs={{0,8},{2,10},{4,12},{6,14},{8,16},{10,18},{12,20},{14,22},{16,24},... | collective-permute-start | bytes 995336 | tf_op jit(solution)/shard_map/ppermute | solution.py:159
  49.4 22.1 %copy-start.11 = (bf16[1296,128]{1,0:T(8,128)(2,1)}, bf16[1296,128]{1,0:T(8,128)(2,1)S(1)}, u32[]{:S(2)}) copy-start(bf16[1296,128]{1,0:T(8,128)(2,1)S(1)} %collective-permute-done.7) | copy-start | bytes 995332
  71.8 30.7 %collective-permute-start.10 = (bf16[4,1280,128]{2,1,0:T(8,128)(2,1)S(1)}, bf16[4,1280,128]{2,1,0:T(8,128)(2,1)}, u32[]{:S(2)}, u32[]{:S(2)}) collective-permute-start(bf16[4,1280,128]{2,1,0:T(8,128)(2,1)S(1)} %pad_maximum_fusion.1.refs_1_.refs_2_), channel_id=1, source_target_pairs={{0,4},{2,6},{4,0},{6,2},{8,12},{10,14},{12,8},{14,10},{16,20},{18,... | collective-permute-start | bytes 3932168 | tf_op jit(solution)/shard_map/ppermute | solution.py:171
  73.2 9.5 %collective-permute-start.8 = (bf16[1280,128]{1,0:T(8,128)(2,1)}, bf16[1280,128]{1,0:T(8,128)(2,1)S(1)}, u32[]{:S(2)}, u32[]{:S(2)}) collective-permute-start(bf16[1280,128]{1,0:T(8,128)(2,1)} %copy-done.10), channel_id=1, source_target_pairs={{0,24},{2,26},{4,28},{6,30},{8,0},{10,2},{12,4},{14,6},{16,8},{18,... | collective-permute-start | bytes 983048 | tf_op jit(solution)/shard_map/ppermute | solution.py:159
  73.2 29.2 %collective-permute-start.5 = (bf16[1280,128]{1,0:T(8,128)(2,1)}, bf16[1280,128]{1,0:T(8,128)(2,1)}, u32[]{:S(2)}, u32[]{:S(2)}) collective-permute-start(bf16[1280,128]{1,0:T(8,128)(2,1)} %copy-done.9), channel_id=1, source_target_pairs={{0,16},{2,18},{4,20},{6,22},{8,24},{10,26},{12,28},{14,30},{16,0},... | collective-permute-start | bytes 983048 | tf_op jit(solution)/shard_map/ppermute | solution.py:159
  74.6 27.9 %collective-permute-start.2 = (bf16[1280,128]{1,0:T(8,128)(2,1)}, bf16[1280,128]{1,0:T(8,128)(2,1)}, u32[]{:S(2)}, u32[]{:S(2)}) collective-permute-start(bf16[1280,128]{1,0:T(8,128)(2,1)} %copy-done.8), channel_id=1, source_target_pairs={{0,8},{2,10},{4,12},{6,14},{8,16},{10,18},{12,20},{14,22},{16,24},... | collective-permute-start | bytes 983048 | tf_op jit(solution)/shard_map/ppermute | solution.py:159
  78.8 24.2 %collective-permute-start.13 = (bf16[4,1280,128]{2,1,0:T(8,128)(2,1)S(1)}, bf16[4,1280,128]{2,1,0:T(8,128)(2,1)S(1)}, u32[]{:S(2)}, u32[]{:S(2)}) collective-permute-start(bf16[4,1280,128]{2,1,0:T(8,128)(2,1)S(1)} %pad_maximum_fusion.refs_5_.refs_6_), channel_id=1, source_target_pairs={{0,2},{2,0},{4,6},{6,4},{8,10},{10,8},{12,14},{14,12},{16,18},{18,... | collective-permute-start | bytes 3932168 | tf_op jit(solution)/shard_map/ppermute | solution.py:171
  82.7 20.2 %collective-permute-start.14 = (bf16[4,1280,128]{2,1,0:T(8,128)(2,1)}, bf16[4,1280,128]{2,1,0:T(8,128)(2,1)S(1)}, u32[]{:S(2)}, u32[]{:S(2)}) collective-permute-start(bf16[4,1280,128]{2,1,0:T(8,128)(2,1)} %copy-done), channel_id=1, source_target_pairs={{0,2},{2,0},{4,6},{6,4},{8,10},{10,8},{12,14},{14,12},{16,18},{18,... | collective-permute-start | bytes 3932168 | tf_op jit(solution)/shard_map/ppermute | solution.py:171
  102.4 4.2 %collective-permute-start.11 = (bf16[4,1280,128]{2,1,0:T(8,128)(2,1)S(1)}, bf16[4,1280,128]{2,1,0:T(8,128)(2,1)S(1)}, u32[]{:S(2)}, u32[]{:S(2)}) collective-permute-start(bf16[4,1280,128]{2,1,0:T(8,128)(2,1)S(1)} %pad_maximum_fusion.1.refs_1_.refs_2_), channel_id=1, source_target_pairs={{0,2},{2,0},{4,6},{6,4},{8,10},{10,8},{12,14},{14,12},{16,18},{18,... | collective-permute-start | bytes 3932168 | tf_op jit(solution)/shard_map/ppermute | solution.py:171
  102.4 5.1 %collective-permute-start.12 = (bf16[4,1280,128]{2,1,0:T(8,128)(2,1)}, bf16[4,1280,128]{2,1,0:T(8,128)(2,1)S(1)}, u32[]{:S(2)}, u32[]{:S(2)}) collective-permute-start(bf16[4,1280,128]{2,1,0:T(8,128)(2,1)} %collective-permute-done.10.refs_3_.refs_4_), channel_id=1, source_target_pairs={{0,2},{2,0},{4,6},{6,4},{8,10},{10,8},{12,14},{14,12},{16,18},{18,... | collective-permute-start | bytes 3932168 | tf_op jit(solution)/shard_map/ppermute | solution.py:171
  116.8 17.9 %collective-permute-start.15 = (bf16[1280,128]{1,0:T(8,128)(2,1)S(1)}, bf16[1280,128]{1,0:T(8,128)(2,1)S(1)}, u32[]{:S(2)}, u32[]{:S(2)}) collective-permute-start(bf16[1280,128]{1,0:T(8,128)(2,1)S(1)} %attend_2.1), channel_id=1, source_target_pairs={{0,16},{2,18},{4,20},{6,22},{8,24},{10,26},{12,28},{14,30},{16,0},... | collective-permute-start | bytes 983048 | tf_op jit(solution)/shard_map/ppermute | solution.py:159
  132.6 9.9 %collective-permute-start.16 = (bf16[1280,128]{1,0:T(8,128)(2,1)S(1)}, bf16[1280,128]{1,0:T(8,128)(2,1)S(1)}, u32[]{:S(2)}, u32[]{:S(2)}) collective-permute-start(bf16[1280,128]{1,0:T(8,128)(2,1)S(1)} %get-tuple-element.108), channel_id=1, source_target_pairs={{0,24},{2,26},{4,28},{6,30},{8,0},{10,2},{12,4},{14,6},{16,8},{18,... | collective-permute-start | bytes 983048 | tf_op jit(solution)/shard_map/ppermute | solution.py:159
  133.1 16.9 %collective-permute-start.17 = (bf16[1280,128]{1,0:T(8,128)(2,1)S(1)}, bf16[1280,128]{1,0:T(8,128)(2,1)S(1)}, u32[]{:S(2)}, u32[]{:S(2)}) collective-permute-start(bf16[1280,128]{1,0:T(8,128)(2,1)S(1)} %get-tuple-element.110), channel_id=1, source_target_pairs={{0,8},{2,10},{4,12},{6,14},{8,16},{10,18},{12,20},{14,22},{16,24},... | collective-permute-start | bytes 983048 | tf_op jit(solution)/shard_map/ppermute | solution.py:159
  (4 other events, 5.0 us)

commit v5 on v4

--- a/solution.py
+++ b/solution.py
@@ -126,15 +126,16 @@
         ).astype(jnp.bfloat16)
 
 
-def collect_kernel(place_ref, *refs, per_group):
+def collect_kernel(place_ref, *refs, count):
     out = refs[-1]
-    groups = len(refs) - 1
     rows = out.shape[0]
-    for shift in range(groups):
-        for head in range(per_group):
-            column = column_of(place_ref, shift, head, groups, per_group)
-            piece = refs[shift][head * rows : (head + 1) * rows, :]
-            out[:, pl.ds(column, HEAD_DIM)] = piece.astype(jnp.float32)
+    for step in range(count):
+
+        @pl.when(pl.program_id(0) == step)
+        def _():
+            for head in range(out.shape[1] // HEAD_DIM):
+                piece = refs[step][head * rows : (head + 1) * rows, :]
+                out[:, head * HEAD_DIM : (head + 1) * HEAD_DIM] = piece.astype(jnp.float32)
 
 
 def exchanged(q_in, k_in, v_in, q_gain, k_gain, frames, adjacent, *, groups):
@@ -270,14 +271,28 @@
         for g, x in zip(query_slots, own):
             outputs[g] = rotated(x, groups - g) if g else x
 
-    return pl.pallas_call(
-        functools.partial(collect_kernel, per_group=per_group),
-        out_shape=jax.ShapeDtypeStruct((rows, width), f32),
-        in_specs=[SMEM] + [VMEM] * groups,
-        out_specs=VMEM,
-        compiler_params=params,
-        name="collect",
-    )(place_row, *outputs)
+    def collect(shifts, base):
+        def columns(step, place_ref):
+            shift = shifts[-1]
+            for i in reversed(range(len(shifts) - 1)):
+                shift = jnp.where(step == i, shifts[i], shift)
+            return 0, lax.rem(place_ref[0] + shift, groups)
+
+        return pl.pallas_call(
+            functools.partial(collect_kernel, count=len(shifts)),
+            grid_spec=pltpu.PrefetchScalarGridSpec(
+                num_scalar_prefetch=1,
+                grid=(len(shifts),),
+                in_specs=[VMEM] * len(shifts) + [ANY] * len(base),
+                out_specs=pl.BlockSpec((rows, width // groups), columns),
+            ),
+            out_shape=jax.ShapeDtypeStruct((rows, width), f32),
+            input_output_aliases={1 + len(shifts): 0} if base else {},
+            compiler_params=params,
+            name=f"collect_{shifts[0]}",
+        )(place_row, *[outputs[g] for g in shifts], *base)
+
+    return collect(near, [collect((0, far), [])])
 
 
 def normalized(inputs, gain_row, square_sum, full_width):

time: 152 us -> 152 us (level)
  transfers between devices with their start and end apart: 18 -> 18, of which waited for: 8 -> 8; matrix products, arithmetic and copies ran while one was open for 3% -> 3% of each run, Pallas kernels for 15% -> 16%
where the time goes in v5:
time: 152 us; the launch traced here: 151 us
  waiting for transfers between devices  66.4 us (44%)
  Pallas kernels  34.5 us (23%)
  starting transfers between devices  25.2 us (17%)
  local copies, waits for them, and re-layouts  12.7 us (8%)
  blocking collectives  10.1 us (7%)
  other arithmetic  1.74 us (1%)
    ppermute x12, waiting for transfers between devices, rotated(): return lax.ppermute(x, 'seq', pairs)  61.8 us
    pallas_call x3, Pallas kernels, attend(): pl.pallas_call(functools.partial(attend_kernel, query_slots=query_slots,...  29.9 us
    ppermute x12, starting transfers between devices, rotated(): return lax.ppermute(x, 'seq', pairs)  22.5 us
    psum x1, blocking collectives, exchanged(): sums = lax.psum(sums, 'tensor')  10.1 us
    unnamed x36, local copies, waits for them, and re-layouts  9.03 us
    ppermute x6, waiting for transfers between devices, swapped(): return lax.ppermute(x, 'seq', [(i, i ^ bit) for i in range(devices)])  4.61 us
  transfers between devices with their start and end apart: 18, of which 8 were waited for; matrix products, arithmetic and copies ran while one was open for 3% of the time, Pallas kernels for 16%

profile of v5, /device:TPU:0, one launch (start us, length us, event | category | flops | bytes accessed | tf_op | source)
XLA Modules:
  0.0 151.0 jit_solution(15523377987340086111)
XLA Ops:
  0.0 1.3 copy-done.6
  1.3 1.0 value_pieces.1
  2.4 3.0 %collective-permute-start = (bf16[1280,128]{1,0:T(8,128)(2,1)}, bf16[1280,128]{1,0:T(8,128)(2,1)}, u32[]{:S(2)}, u32[]{:S(2)}) collective-permute-start(bf16[1280,128]{1,0:T(8,128)(2,1)} %get-tuple-element.67), channel_id=1, source_target_pairs={{0,8},{2,10},{4,12},{6,14},{8,16},{10,18},{12,20},{14,22},{16,24},... | collective-permute-start | bytes 983048 | tf_op jit(solution)/shard_map/ppermute | solution.py:160
  5.4 2.6 %collective-permute-start.3 = (bf16[1280,128]{1,0:T(8,128)(2,1)}, bf16[1280,128]{1,0:T(8,128)(2,1)}, u32[]{:S(2)}, u32[]{:S(2)}) collective-permute-start(bf16[1280,128]{1,0:T(8,128)(2,1)} %get-tuple-element.72), channel_id=1, source_target_pairs={{0,16},{2,18},{4,20},{6,22},{8,24},{10,26},{12,28},{14,30},{16,0},... | collective-permute-start | bytes 983048 | tf_op jit(solution)/shard_map/ppermute | solution.py:160
  8.0 1.3 collective-permute-start.6
  9.4 1.7 %copy-done.2 = f32[256,2560]{1,0:T(8,128)S(1)} copy-done((f32[256,2560]{1,0:T(8,128)S(1)}, f32[256,2560]{1,0:T(8,128)}, u32[]{:S(2)}) %copy-start.2) | copy-done | bytes 2621464
  11.1 1.7 %copy-done.4 = f32[256,2560]{1,0:T(8,128)S(1)} copy-done((f32[256,2560]{1,0:T(8,128)S(1)}, f32[256,2560]{1,0:T(8,128)}, u32[]{:S(2)}) %copy-start.4) | copy-done | bytes 2621464
  13.3 10.1 %psum.7.sums_ref = f32[256,2]{1,0:T(8,128)S(1)} all-reduce(f32[256,2]{1,0:T(8,128)S(1)} %square_sums.1), channel_id=1, replica_groups=mesh['seq'=16,'tensor'=2] {'tensor'}, use_global_device_ids=true, to_apply=%region_0.1 | all-reduce | flops 512 | bytes 4096 | tf_op jit(solution)/shard_map/psum | solution.py:197
  23.6 1.7 %copy-done.5 = f32[256,2560]{1,0:T(8,128)S(1)} copy-done((f32[256,2560]{1,0:T(8,128)S(1)}, f32[256,2560]{1,0:T(8,128)}, u32[]{:S(2)}) %copy-start.5) | copy-done | bytes 2621464
  25.3 0.9 norm_pieces.1
  26.3 3.4 %collective-permute-done.3 = bf16[1280,128]{1,0:T(8,128)(2,1)} collective-permute-done((bf16[1280,128]{1,0:T(8,128)(2,1)}, bf16[1280,128]{1,0:T(8,128)(2,1)}, u32[]{:S(2)}, u32[]{:S(2)}) %collective-permute-start.3) | collective-permute-done | bytes 327712 | tf_op jit(solution)/shard_map/ppermute | solution.py:160
  29.6 1.3 pad_maximum_fusion.refs_5_.refs_6_
  31.0 1.6 %collective-permute-start.9 = (bf16[4,1280,128]{2,1,0:T(8,128)(2,1)S(1)}, bf16[4,1280,128]{2,1,0:T(8,128)(2,1)S(1)}, u32[]{:S(2)}, u32[]{:S(2)}) collective-permute-start(bf16[4,1280,128]{2,1,0:T(8,128)(2,1)S(1)} %pad_maximum_fusion.refs_5_.refs_6_), channel_id=1, source_target_pairs={{0,4},{2,6},{4,0},{6,2},{8,12},{10,14},{12,8},{14,10},{16,20},{18,... | collective-permute-start | bytes 3932168 | tf_op jit(solution)/shard_map/ppermute | solution.py:172
  32.6 8.5 %collective-permute-start.7 = (bf16[1296,128]{1,0:T(8,128)(2,1)S(1)}, bf16[1296,128]{1,0:T(8,128)(2,1)S(1)}, u32[]{:S(2)}, u32[]{:S(2)}) collective-permute-start(bf16[1296,128]{1,0:T(8,128)(2,1)S(1)} %get-tuple-element.78), channel_id=1, source_target_pairs={{0,24},{2,26},{4,28},{6,30},{8,0},{10,2},{12,4},{14,6},{16,8},{18,... | collective-permute-start | bytes 995336 | tf_op jit(solution)/shard_map/ppermute | solution.py:160
  41.7 7.6 %collective-permute-done.7 = bf16[1296,128]{1,0:T(8,128)(2,1)S(1)} collective-permute-done((bf16[1296,128]{1,0:T(8,128)(2,1)S(1)}, bf16[1296,128]{1,0:T(8,128)(2,1)S(1)}, u32[]{:S(2)}, u32[]{:S(2)}) %collective-permute-start.7) | collective-permute-done | bytes 331808 | tf_op jit(solution)/shard_map/ppermute | solution.py:160
  49.4 20.9 %collective-permute-done.4 = bf16[1296,128]{1,0:T(8,128)(2,1)S(1)} collective-permute-done((bf16[1296,128]{1,0:T(8,128)(2,1)S(1)}, bf16[1296,128]{1,0:T(8,128)(2,1)S(1)}, u32[]{:S(2)}, u32[]{:S(2)}) %collective-permute-start.4) | collective-permute-done | bytes 331808 | tf_op jit(solution)/shard_map/ppermute | solution.py:160
  70.3 1.1 copy-done
  73.2 1.4 collective-permute-start.5
  74.6 1.4 collective-permute-start.2
  78.8 3.9 %collective-permute-done.8.refs_1_ = bf16[1280,128]{1,0:T(8,128)(2,1)S(1)} collective-permute-done((bf16[1280,128]{1,0:T(8,128)(2,1)}, bf16[1280,128]{1,0:T(8,128)(2,1)S(1)}, u32[]{:S(2)}, u32[]{:S(2)}) %collective-permute-start.8) | collective-permute-done | bytes 327712 | tf_op jit(solution)/shard_map/ppermute | solution.py:160
  82.7 19.7 %collective-permute-done.5.refs_0_ = bf16[1280,128]{1,0:T(8,128)(2,1)} collective-permute-done((bf16[1280,128]{1,0:T(8,128)(2,1)}, bf16[1280,128]{1,0:T(8,128)(2,1)}, u32[]{:S(2)}, u32[]{:S(2)}) %collective-permute-start.5) | collective-permute-done | bytes 327712 | tf_op jit(solution)/shard_map/ppermute | solution.py:160
  103.0 3.7 %collective-permute-done.11.refs_2_.refs_3_ = bf16[4,1280,128]{2,1,0:T(8,128)(2,1)S(1)} collective-permute-done((bf16[4,1280,128]{2,1,0:T(8,128)(2,1)S(1)}, bf16[4,1280,128]{2,1,0:T(8,128)(2,1)S(1)}, u32[]{:S(2)}, u32[]{:S(2)}) %collective-permute-start.11) | collective-permute-done | bytes 1310752 | tf_op jit(solution)/shard_map/ppermute | solution.py:172
  106.6 0.9 collective-permute-done.12.refs_4_.refs_5_
  107.6 1.3 copy-done.1
  108.9 7.9 %attend_2.1 = bf16[1280,128]{1,0:T(8,128)(2,1)S(1)} custom-call(f32[256]{0:T(256)S(1)} %reshape.88.bias_ref, bf16[1280,128]{1,0:T(8,128)(2,1)} %collective-permute-done.5.refs_0_, bf16[4,1280,128]{2,1,0:T(8,128)(2,1)S(1)} %pad_maximum_fusion.1.refs_1_.refs_2_, bf16[4,1280,128]{2,1,0:T(8,128)(2,1)S(1)} %collective-permute-done.11.refs_2_.refs_3_, ...), custom_call_target="tpu_custom_call" | custom-call | tf_op jit(solution)/shard_map/attend_2/pallas_call | solution.py:246
  116.8 1.6 %collective-permute-start.17 = (bf16[1280,128]{1,0:T(8,128)(2,1)S(1)}, bf16[1280,128]{1,0:T(8,128)(2,1)S(1)}, u32[]{:S(2)}, u32[]{:S(2)}) collective-permute-start(bf16[1280,128]{1,0:T(8,128)(2,1)S(1)} %attend_2.1), channel_id=1, source_target_pairs={{0,16},{2,18},{4,20},{6,22},{8,24},{10,26},{12,28},{14,30},{16,0},... | collective-permute-start | bytes 983048 | tf_op jit(solution)/shard_map/ppermute | solution.py:160
  118.4 14.2 %attend_1_3.1 = (bf16[1280,128]{1,0:T(8,128)(2,1)S(1)}, bf16[1280,128]{1,0:T(8,128)(2,1)S(1)}) custom-call(f32[256]{0:T(256)S(1)} %reshape.88.bias_ref, bf16[1280,128]{1,0:T(8,128)(2,1)} %collective-permute-done.2.refs_0_, bf16[1280,128]{1,0:T(8,128)(2,1)S(1)} %collective-permute-done.8.refs_1_, bf16[4,1280,128]{2,1,0:T(8,128)(2,1)S(1)} %pad_maximum_fusion.1.refs_1_.refs_2_, ...), custom_call_target="tpu_custom_call" | custom-call | tf_op jit(solution)/shard_map/attend_1_3/pallas_call | solution.py:246
  133.1 1.6 %collective-permute-start.16 = (bf16[1280,128]{1,0:T(8,128)(2,1)S(1)}, bf16[1280,128]{1,0:T(8,128)(2,1)S(1)}, u32[]{:S(2)}, u32[]{:S(2)}) collective-permute-start(bf16[1280,128]{1,0:T(8,128)(2,1)S(1)} %get-tuple-element.104), channel_id=1, source_target_pairs={{0,8},{2,10},{4,12},{6,14},{8,16},{10,18},{12,20},{14,22},{16,24},... | collective-permute-start | bytes 983048 | tf_op jit(solution)/shard_map/ppermute | solution.py:160
  134.7 7.8 %attend_0.1.refs_0_ = bf16[1280,128]{1,0:T(8,128)(2,1)S(1)} custom-call(f32[256]{0:T(256)S(1)} %reshape.88.bias_ref, bf16[1280,128]{1,0:T(8,128)(2,1)S(1)} %get-tuple-element.108.refs_0_, bf16[4,1280,128]{2,1,0:T(8,128)(2,1)S(1)} %pad_maximum_fusion.1.refs_1_.refs_2_, bf16[4,1280,128]{2,1,0:T(8,128)(2,1)S(1)} %collective-permute-done.11.refs_2_.refs_3_, ...), custom_call_target="tpu_custom_call" | custom-call | tf_op jit(solution)/shard_map/attend_0/pallas_call | solution.py:246
  142.4 1.1 collect_0.1.refs_2_
  143.6 6.3 %collective-permute-done.16.refs_1_ = bf16[1280,128]{1,0:T(8,128)(2,1)S(1)} collective-permute-done((bf16[1280,128]{1,0:T(8,128)(2,1)S(1)}, bf16[1280,128]{1,0:T(8,128)(2,1)S(1)}, u32[]{:S(2)}, u32[]{:S(2)}) %collective-permute-start.16) | collective-permute-done | bytes 327712 | tf_op jit(solution)/shard_map/ppermute | solution.py:160
  149.9 1.1 collect_1.1
  (74 shorter events, 7.0 us)
Async XLA Ops:
  0.0 9.4 %copy-start.14 = (f32[2560]{0:T(1024)S(1)}, f32[2560]{0:T(1024)}, u32[]{:S(2)}) copy-start(f32[2560]{0:T(1024)} %param.10) | copy-start | bytes 30724
  0.0 9.4 %copy-start.15 = (f32[2560]{0:T(1024)S(1)}, f32[2560]{0:T(1024)}, u32[]{:S(2)}) copy-start(f32[2560]{0:T(1024)} %param.11) | copy-start | bytes 30724
  0.0 1.3 copy-start.6
  2.4 23.9 %collective-permute-start = (bf16[1280,128]{1,0:T(8,128)(2,1)}, bf16[1280,128]{1,0:T(8,128)(2,1)}, u32[]{:S(2)}, u32[]{:S(2)}) collective-permute-start(bf16[1280,128]{1,0:T(8,128)(2,1)} %get-tuple-element.67), channel_id=1, source_target_pairs={{0,8},{2,10},{4,12},{6,14},{8,16},{10,18},{12,20},{14,22},{16,24},... | collective-permute-start | bytes 983048 | tf_op jit(solution)/shard_map/ppermute | solution.py:160
  5.4 24.2 %collective-permute-start.3 = (bf16[1280,128]{1,0:T(8,128)(2,1)}, bf16[1280,128]{1,0:T(8,128)(2,1)}, u32[]{:S(2)}, u32[]{:S(2)}) collective-permute-start(bf16[1280,128]{1,0:T(8,128)(2,1)} %get-tuple-element.72), channel_id=1, source_target_pairs={{0,16},{2,18},{4,20},{6,22},{8,24},{10,26},{12,28},{14,30},{16,0},... | collective-permute-start | bytes 983048 | tf_op jit(solution)/shard_map/ppermute | solution.py:160
  8.0 21.6 %collective-permute-start.6 = (bf16[1280,128]{1,0:T(8,128)(2,1)}, bf16[1280,128]{1,0:T(8,128)(2,1)}, u32[]{:S(2)}, u32[]{:S(2)}) collective-permute-start(bf16[1280,128]{1,0:T(8,128)(2,1)} %get-tuple-element.77), channel_id=1, source_target_pairs={{0,24},{2,26},{4,28},{6,30},{8,0},{10,2},{12,4},{14,6},{16,8},{18,... | collective-permute-start | bytes 983048 | tf_op jit(solution)/shard_map/ppermute | solution.py:160
  9.4 1.7 %copy-start.2 = (f32[256,2560]{1,0:T(8,128)S(1)}, f32[256,2560]{1,0:T(8,128)}, u32[]{:S(2)}) copy-start(f32[256,2560]{1,0:T(8,128)} %q_ref.1) | copy-start | bytes 7864324
  11.1 1.7 %copy-start.4 = (f32[256,2560]{1,0:T(8,128)S(1)}, f32[256,2560]{1,0:T(8,128)}, u32[]{:S(2)}) copy-start(f32[256,2560]{1,0:T(8,128)} %k_ref.1) | copy-start | bytes 7864324
  12.9 10.5 %copy-start.17 = (s32[32]{0:T(128)S(1)}, s32[32]{0:T(128)}, u32[]{:S(2)}) copy-start(s32[32]{0:T(128)} %param.12) | copy-start | bytes 388
  12.9 10.6 %copy-start.16 = (s32[2,32]{1,0:T(2,128)S(1)}, s32[2,32]{1,0:T(2,128)}, u32[]{:S(2)}) copy-start(s32[2,32]{1,0:T(2,128)} %param.13) | copy-start | bytes 772
  12.9 10.7 %copy-start.3 = (f32[256,2560]{1,0:T(8,128)S(1)}, f32[256,2560]{1,0:T(8,128)}, u32[]{:S(2)}) copy-start(f32[256,2560]{1,0:T(8,128)} %q_ref.1) | copy-start | bytes 7864324
  23.6 1.7 %copy-start.5 = (f32[256,2560]{1,0:T(8,128)S(1)}, f32[256,2560]{1,0:T(8,128)}, u32[]{:S(2)}) copy-start(f32[256,2560]{1,0:T(8,128)} %k_ref.1) | copy-start | bytes 7864324
  26.2 45.2 %copy-start.7 = (bf16[1296,128]{1,0:T(8,128)(2,1)}, bf16[1296,128]{1,0:T(8,128)(2,1)S(1)}, u32[]{:S(2)}) copy-start(bf16[1296,128]{1,0:T(8,128)(2,1)S(1)} %get-tuple-element.88) | copy-start | bytes 995332
  26.2 45.5 %copy-start.8 = (bf16[1280,128]{1,0:T(8,128)(2,1)}, bf16[1280,128]{1,0:T(8,128)(2,1)S(1)}, u32[]{:S(2)}) copy-start(bf16[1280,128]{1,0:T(8,128)(2,1)S(1)} %get-tuple-element.69) | copy-start | bytes 983044
  26.2 45.5 %copy-start.9 = (bf16[1280,128]{1,0:T(8,128)(2,1)}, bf16[1280,128]{1,0:T(8,128)(2,1)S(1)}, u32[]{:S(2)}) copy-start(bf16[1280,128]{1,0:T(8,128)(2,1)S(1)} %get-tuple-element.74) | copy-start | bytes 983044
  26.3 45.5 %copy-start.10 = (bf16[1280,128]{1,0:T(8,128)(2,1)}, bf16[1280,128]{1,0:T(8,128)(2,1)S(1)}, u32[]{:S(2)}) copy-start(bf16[1280,128]{1,0:T(8,128)(2,1)S(1)} %get-tuple-element.79) | copy-start | bytes 983044
  31.0 39.3 %collective-permute-start.9 = (bf16[4,1280,128]{2,1,0:T(8,128)(2,1)S(1)}, bf16[4,1280,128]{2,1,0:T(8,128)(2,1)S(1)}, u32[]{:S(2)}, u32[]{:S(2)}) collective-permute-start(bf16[4,1280,128]{2,1,0:T(8,128)(2,1)S(1)} %pad_maximum_fusion.refs_5_.refs_6_), channel_id=1, source_target_pairs={{0,4},{2,6},{4,0},{6,2},{8,12},{10,14},{12,8},{14,10},{16,20},{18,... | collective-permute-start | bytes 3932168 | tf_op jit(solution)/shard_map/ppermute | solution.py:172
  32.6 16.8 %collective-permute-start.7 = (bf16[1296,128]{1,0:T(8,128)(2,1)S(1)}, bf16[1296,128]{1,0:T(8,128)(2,1)S(1)}, u32[]{:S(2)}, u32[]{:S(2)}) collective-permute-start(bf16[1296,128]{1,0:T(8,128)(2,1)S(1)} %get-tuple-element.78), channel_id=1, source_target_pairs={{0,24},{2,26},{4,28},{6,30},{8,0},{10,2},{12,4},{14,6},{16,8},{18,... | collective-permute-start | bytes 995336 | tf_op jit(solution)/shard_map/ppermute | solution.py:160
  41.1 29.2 %collective-permute-start.4 = (bf16[1296,128]{1,0:T(8,128)(2,1)S(1)}, bf16[1296,128]{1,0:T(8,128)(2,1)S(1)}, u32[]{:S(2)}, u32[]{:S(2)}) collective-permute-start(bf16[1296,128]{1,0:T(8,128)(2,1)S(1)} %get-tuple-element.73), channel_id=1, source_target_pairs={{0,16},{2,18},{4,20},{6,22},{8,24},{10,26},{12,28},{14,30},{16,0},... | collective-permute-start | bytes 995336 | tf_op jit(solution)/shard_map/ppermute | solution.py:160
  41.5 28.7 %collective-permute-start.1 = (bf16[1296,128]{1,0:T(8,128)(2,1)S(1)}, bf16[1296,128]{1,0:T(8,128)(2,1)S(1)}, u32[]{:S(2)}, u32[]{:S(2)}) collective-permute-start(bf16[1296,128]{1,0:T(8,128)(2,1)S(1)} %get-tuple-element.68), channel_id=1, source_target_pairs={{0,8},{2,10},{4,12},{6,14},{8,16},{10,18},{12,20},{14,22},{16,24},... | collective-permute-start | bytes 995336 | tf_op jit(solution)/shard_map/ppermute | solution.py:160
  49.4 22.1 %copy-start.11 = (bf16[1296,128]{1,0:T(8,128)(2,1)}, bf16[1296,128]{1,0:T(8,128)(2,1)S(1)}, u32[]{:S(2)}) copy-start(bf16[1296,128]{1,0:T(8,128)(2,1)S(1)} %collective-permute-done.7) | copy-start | bytes 995332
  71.8 30.7 %collective-permute-start.10 = (bf16[4,1280,128]{2,1,0:T(8,128)(2,1)S(1)}, bf16[4,1280,128]{2,1,0:T(8,128)(2,1)}, u32[]{:S(2)}, u32[]{:S(2)}) collective-permute-start(bf16[4,1280,128]{2,1,0:T(8,128)(2,1)S(1)} %pad_maximum_fusion.1.refs_1_.refs_2_), channel_id=1, source_target_pairs={{0,4},{2,6},{4,0},{6,2},{8,12},{10,14},{12,8},{14,10},{16,20},{18,... | collective-permute-start | bytes 3932168 | tf_op jit(solution)/shard_map/ppermute | solution.py:172
  73.2 9.5 %collective-permute-start.8 = (bf16[1280,128]{1,0:T(8,128)(2,1)}, bf16[1280,128]{1,0:T(8,128)(2,1)S(1)}, u32[]{:S(2)}, u32[]{:S(2)}) collective-permute-start(bf16[1280,128]{1,0:T(8,128)(2,1)} %copy-done.10), channel_id=1, source_target_pairs={{0,24},{2,26},{4,28},{6,30},{8,0},{10,2},{12,4},{14,6},{16,8},{18,... | collective-permute-start | bytes 983048 | tf_op jit(solution)/shard_map/ppermute | solution.py:160
  73.2 29.2 %collective-permute-start.5 = (bf16[1280,128]{1,0:T(8,128)(2,1)}, bf16[1280,128]{1,0:T(8,128)(2,1)}, u32[]{:S(2)}, u32[]{:S(2)}) collective-permute-start(bf16[1280,128]{1,0:T(8,128)(2,1)} %copy-done.9), channel_id=1, source_target_pairs={{0,16},{2,18},{4,20},{6,22},{8,24},{10,26},{12,28},{14,30},{16,0},... | collective-permute-start | bytes 983048 | tf_op jit(solution)/shard_map/ppermute | solution.py:160
  74.6 27.9 %collective-permute-start.2 = (bf16[1280,128]{1,0:T(8,128)(2,1)}, bf16[1280,128]{1,0:T(8,128)(2,1)}, u32[]{:S(2)}, u32[]{:S(2)}) collective-permute-start(bf16[1280,128]{1,0:T(8,128)(2,1)} %copy-done.8), channel_id=1, source_target_pairs={{0,8},{2,10},{4,12},{6,14},{8,16},{10,18},{12,20},{14,22},{16,24},... | collective-permute-start | bytes 983048 | tf_op jit(solution)/shard_map/ppermute | solution.py:160
  78.8 24.2 %collective-permute-start.13 = (bf16[4,1280,128]{2,1,0:T(8,128)(2,1)S(1)}, bf16[4,1280,128]{2,1,0:T(8,128)(2,1)S(1)}, u32[]{:S(2)}, u32[]{:S(2)}) collective-permute-start(bf16[4,1280,128]{2,1,0:T(8,128)(2,1)S(1)} %pad_maximum_fusion.refs_5_.refs_6_), channel_id=1, source_target_pairs={{0,2},{2,0},{4,6},{6,4},{8,10},{10,8},{12,14},{14,12},{16,18},{18,... | collective-permute-start | bytes 3932168 | tf_op jit(solution)/shard_map/ppermute | solution.py:172
  82.7 20.2 %collective-permute-start.14 = (bf16[4,1280,128]{2,1,0:T(8,128)(2,1)}, bf16[4,1280,128]{2,1,0:T(8,128)(2,1)S(1)}, u32[]{:S(2)}, u32[]{:S(2)}) collective-permute-start(bf16[4,1280,128]{2,1,0:T(8,128)(2,1)} %copy-done), channel_id=1, source_target_pairs={{0,2},{2,0},{4,6},{6,4},{8,10},{10,8},{12,14},{14,12},{16,18},{18,... | collective-permute-start | bytes 3932168 | tf_op jit(solution)/shard_map/ppermute | solution.py:172
  102.4 4.2 %collective-permute-start.11 = (bf16[4,1280,128]{2,1,0:T(8,128)(2,1)S(1)}, bf16[4,1280,128]{2,1,0:T(8,128)(2,1)S(1)}, u32[]{:S(2)}, u32[]{:S(2)}) collective-permute-start(bf16[4,1280,128]{2,1,0:T(8,128)(2,1)S(1)} %pad_maximum_fusion.1.refs_1_.refs_2_), channel_id=1, source_target_pairs={{0,2},{2,0},{4,6},{6,4},{8,10},{10,8},{12,14},{14,12},{16,18},{18,... | collective-permute-start | bytes 3932168 | tf_op jit(solution)/shard_map/ppermute | solution.py:172
  102.4 5.1 %collective-permute-start.12 = (bf16[4,1280,128]{2,1,0:T(8,128)(2,1)}, bf16[4,1280,128]{2,1,0:T(8,128)(2,1)S(1)}, u32[]{:S(2)}, u32[]{:S(2)}) collective-permute-start(bf16[4,1280,128]{2,1,0:T(8,128)(2,1)} %collective-permute-done.10.refs_3_.refs_4_), channel_id=1, source_target_pairs={{0,2},{2,0},{4,6},{6,4},{8,10},{10,8},{12,14},{14,12},{16,18},{18,... | collective-permute-start | bytes 3932168 | tf_op jit(solution)/shard_map/ppermute | solution.py:172
  116.8 17.9 %collective-permute-start.17 = (bf16[1280,128]{1,0:T(8,128)(2,1)S(1)}, bf16[1280,128]{1,0:T(8,128)(2,1)S(1)}, u32[]{:S(2)}, u32[]{:S(2)}) collective-permute-start(bf16[1280,128]{1,0:T(8,128)(2,1)S(1)} %attend_2.1), channel_id=1, source_target_pairs={{0,16},{2,18},{4,20},{6,22},{8,24},{10,26},{12,28},{14,30},{16,0},... | collective-permute-start | bytes 983048 | tf_op jit(solution)/shard_map/ppermute | solution.py:160
  132.6 11.0 %collective-permute-start.15 = (bf16[1280,128]{1,0:T(8,128)(2,1)S(1)}, bf16[1280,128]{1,0:T(8,128)(2,1)S(1)}, u32[]{:S(2)}, u32[]{:S(2)}) collective-permute-start(bf16[1280,128]{1,0:T(8,128)(2,1)S(1)} %get-tuple-element.103), channel_id=1, source_target_pairs={{0,24},{2,26},{4,28},{6,30},{8,0},{10,2},{12,4},{14,6},{16,8},{18,... | collective-permute-start | bytes 983048 | tf_op jit(solution)/shard_map/ppermute | solution.py:160
  133.1 16.9 %collective-permute-start.16 = (bf16[1280,128]{1,0:T(8,128)(2,1)S(1)}, bf16[1280,128]{1,0:T(8,128)(2,1)S(1)}, u32[]{:S(2)}, u32[]{:S(2)}) collective-permute-start(bf16[1280,128]{1,0:T(8,128)(2,1)S(1)} %get-tuple-element.104), channel_id=1, source_target_pairs={{0,8},{2,10},{4,12},{6,14},{8,16},{10,18},{12,20},{14,22},{16,24},... | collective-permute-start | bytes 983048 | tf_op jit(solution)/shard_map/ppermute | solution.py:160
  (4 other events, 5.0 us)

commit v6 on v5

--- a/solution.py
+++ b/solution.py
@@ -210,7 +210,7 @@
     )(place_row, sums, q_in, k_in, q_gain.reshape(1, width), k_gain.reshape(1, width), mask_rows)
     k_arrived = exchange(pieces[:groups], v_arrived)
     v_stack = jnp.stack(v_arrived)
-    q_arrived = exchange(pieces[groups:], k_arrived)
+    q_arrived = exchange(pieces[groups:], [k_arrived[groups - 1]] * groups)
 
     low = per_group * rows
     known = jnp.stack([x[low : low + blk, :blocks] for x in k_arrived]).astype(f32)

time: 152 us -> 150 us (0.987)
  waiting for transfers between devices: 66.4 us -> 63 us
    ppermute x12, waiting for transfers between devices: 61.8 us -> 52.4 us  [rotated(): return lax.ppermute(x, 'seq', pairs)]
    ppermute x6, waiting for transfers between devices: 4.61 us -> 10.7 us  [swapped(): return lax.ppermute(x, 'seq', [(i, i ^ bit) for i in range(devices)])]
  transfers between devices with their start and end apart: 18 -> 18, of which waited for: 8 -> 10; matrix products, arithmetic and copies ran while one was open for 3% -> 3% of each run, Pallas kernels for 16% -> 16%
where the time goes in v6:
time: 150 us; the launch traced here: 149 us
  waiting for transfers between devices  63 us (42%)
  Pallas kernels  34.5 us (23%)
  starting transfers between devices  26.5 us (18%)
  local copies, waits for them, and re-layouts  12.6 us (8%)
  blocking collectives  10.4 us (7%)
  other arithmetic  1.74 us (1%)
    ppermute x12, waiting for transfers between devices, rotated(): return lax.ppermute(x, 'seq', pairs)  52.4 us
    pallas_call x3, Pallas kernels, attend(): pl.pallas_call(functools.partial(attend_kernel, query_slots=query_slots,...  29.9 us
    ppermute x12, starting transfers between devices, rotated(): return lax.ppermute(x, 'seq', pairs)  22.8 us
    ppermute x6, waiting for transfers between devices, swapped(): return lax.ppermute(x, 'seq', [(i, i ^ bit) for i in range(devices)])  10.7 us
    psum x1, blocking collectives, exchanged(): sums = lax.psum(sums, 'tensor')  10.4 us
    unnamed x36, local copies, waits for them, and re-layouts  8.97 us
    ppermute x6, starting transfers between devices, swapped(): return lax.ppermute(x, 'seq', [(i, i ^ bit) for i in range(devices)])  3.75 us
  transfers between devices with their start and end apart: 18, of which 10 were waited for; matrix products, arithmetic and copies ran while one was open for 3% of the time, Pallas kernels for 16%

profile of v6, /device:TPU:0, one launch (start us, length us, event | category | flops | bytes accessed | tf_op | source)
XLA Modules:
  0.0 149.2 jit_solution(9998337722961530850)
XLA Ops:
  0.0 1.3 copy-done.6
  1.3 1.0 value_pieces.1
  2.4 5.0 %collective-permute-start = (bf16[1280,128]{1,0:T(8,128)(2,1)}, bf16[1280,128]{1,0:T(8,128)(2,1)}, u32[]{:S(2)}, u32[]{:S(2)}) collective-permute-start(bf16[1280,128]{1,0:T(8,128)(2,1)} %get-tuple-element.64), channel_id=1, source_target_pairs={{0,24},{2,26},{4,28},{6,30},{8,0},{10,2},{12,4},{14,6},{16,8},{18,... | collective-permute-start | bytes 983048 | tf_op jit(solution)/shard_map/ppermute | solution.py:160
  8.5 1.7 %copy-done.2 = f32[256,2560]{1,0:T(8,128)S(1)} copy-done((f32[256,2560]{1,0:T(8,128)S(1)}, f32[256,2560]{1,0:T(8,128)}, u32[]{:S(2)}) %copy-start.2) | copy-done | bytes 2621464
  10.2 1.7 %copy-done.4 = f32[256,2560]{1,0:T(8,128)S(1)} copy-done((f32[256,2560]{1,0:T(8,128)S(1)}, f32[256,2560]{1,0:T(8,128)}, u32[]{:S(2)}) %copy-start.4) | copy-done | bytes 2621464
  12.4 10.4 %psum.7.sums_ref = f32[256,2]{1,0:T(8,128)S(1)} all-reduce(f32[256,2]{1,0:T(8,128)S(1)} %square_sums.1), channel_id=1, replica_groups=mesh['seq'=16,'tensor'=2] {'tensor'}, use_global_device_ids=true, to_apply=%region_0.1 | all-reduce | flops 512 | bytes 4096 | tf_op jit(solution)/shard_map/psum | solution.py:197
  23.0 1.7 %copy-done.5 = f32[256,2560]{1,0:T(8,128)S(1)} copy-done((f32[256,2560]{1,0:T(8,128)S(1)}, f32[256,2560]{1,0:T(8,128)}, u32[]{:S(2)}) %copy-start.5) | copy-done | bytes 2621464
  25.7 10.0 %collective-permute-done.7 = bf16[1280,128]{1,0:T(8,128)(2,1)} collective-permute-done((bf16[1280,128]{1,0:T(8,128)(2,1)}, bf16[1280,128]{1,0:T(8,128)(2,1)}, u32[]{:S(2)}, u32[]{:S(2)}) %collective-permute-start.7) | collective-permute-done | bytes 327712 | tf_op jit(solution)/shard_map/ppermute | solution.py:160
  35.7 1.3 pad_maximum_fusion.refs_5_.refs_6_
  37.0 1.6 %collective-permute-start.9 = (bf16[4,1280,128]{2,1,0:T(8,128)(2,1)S(1)}, bf16[4,1280,128]{2,1,0:T(8,128)(2,1)S(1)}, u32[]{:S(2)}, u32[]{:S(2)}) collective-permute-start(bf16[4,1280,128]{2,1,0:T(8,128)(2,1)S(1)} %pad_maximum_fusion.refs_5_.refs_6_), channel_id=1, source_target_pairs={{0,4},{2,6},{4,0},{6,2},{8,12},{10,14},{12,8},{14,10},{16,20},{18,... | collective-permute-start | bytes 3932168 | tf_op jit(solution)/shard_map/ppermute | solution.py:172
  38.6 3.2 %collective-permute-start.6 = (bf16[1296,128]{1,0:T(8,128)(2,1)S(1)}, bf16[1296,128]{1,0:T(8,128)(2,1)S(1)}, u32[]{:S(2)}, u32[]{:S(2)}) collective-permute-start(bf16[1296,128]{1,0:T(8,128)(2,1)S(1)} %get-tuple-element.74), channel_id=1, source_target_pairs={{0,8},{2,10},{4,12},{6,14},{8,16},{10,18},{12,20},{14,22},{16,24},... | collective-permute-start | bytes 995336 | tf_op jit(solution)/shard_map/ppermute | solution.py:160
  42.5 19.4 %collective-permute-done.8 = bf16[1296,128]{1,0:T(8,128)(2,1)S(1)} collective-permute-done((bf16[1296,128]{1,0:T(8,128)(2,1)S(1)}, bf16[1296,128]{1,0:T(8,128)(2,1)S(1)}, u32[]{:S(2)}, u32[]{:S(2)}) %collective-permute-start.8) | collective-permute-done | bytes 331808 | tf_op jit(solution)/shard_map/ppermute | solution.py:160
  61.9 1.5 %collective-permute-done.1 = bf16[1296,128]{1,0:T(8,128)(2,1)S(1)} collective-permute-done((bf16[1296,128]{1,0:T(8,128)(2,1)S(1)}, bf16[1296,128]{1,0:T(8,128)(2,1)S(1)}, u32[]{:S(2)}, u32[]{:S(2)}) %collective-permute-start.1) | collective-permute-done | bytes 331808 | tf_op jit(solution)/shard_map/ppermute | solution.py:160
  63.4 3.3 %collective-permute-done.9.refs_7_.refs_8_ = bf16[4,1280,128]{2,1,0:T(8,128)(2,1)S(1)} collective-permute-done((bf16[4,1280,128]{2,1,0:T(8,128)(2,1)S(1)}, bf16[4,1280,128]{2,1,0:T(8,128)(2,1)S(1)}, u32[]{:S(2)}, u32[]{:S(2)}) %collective-permute-start.9) | collective-permute-done | bytes 1310752 | tf_op jit(solution)/shard_map/ppermute | solution.py:172
  66.7 1.1 copy-done
  68.1 1.6 %collective-permute-start.10 = (bf16[4,1280,128]{2,1,0:T(8,128)(2,1)S(1)}, bf16[4,1280,128]{2,1,0:T(8,128)(2,1)}, u32[]{:S(2)}, u32[]{:S(2)}) collective-permute-start(bf16[4,1280,128]{2,1,0:T(8,128)(2,1)S(1)} %pad_maximum_fusion.1.refs_1_.refs_2_), channel_id=1, source_target_pairs={{0,4},{2,6},{4,0},{6,2},{8,12},{10,14},{12,8},{14,10},{16,20},{18,... | collective-permute-start | bytes 3932168 | tf_op jit(solution)/shard_map/ppermute | solution.py:172
  70.6 1.8 %collective-permute-start.2 = (bf16[1280,128]{1,0:T(8,128)(2,1)}, bf16[1280,128]{1,0:T(8,128)(2,1)S(1)}, u32[]{:S(2)}, u32[]{:S(2)}) collective-permute-start(bf16[1280,128]{1,0:T(8,128)(2,1)} %copy-done.10), channel_id=1, source_target_pairs={{0,8},{2,10},{4,12},{6,14},{8,16},{10,18},{12,20},{14,22},{16,24},... | collective-permute-start | bytes 983048 | tf_op jit(solution)/shard_map/ppermute | solution.py:160
  72.4 1.1 collective-permute-start.3
  73.5 1.9 %collective-permute-start.4 = (bf16[1280,128]{1,0:T(8,128)(2,1)}, bf16[1280,128]{1,0:T(8,128)(2,1)}, u32[]{:S(2)}, u32[]{:S(2)}) collective-permute-start(bf16[1280,128]{1,0:T(8,128)(2,1)} %copy-done.8), channel_id=1, source_target_pairs={{0,24},{2,26},{4,28},{6,30},{8,0},{10,2},{12,4},{14,6},{16,8},{18,... | collective-permute-start | bytes 983048 | tf_op jit(solution)/shard_map/ppermute | solution.py:160
  78.3 5.1 %collective-permute-done.2.refs_0_ = bf16[1280,128]{1,0:T(8,128)(2,1)S(1)} collective-permute-done((bf16[1280,128]{1,0:T(8,128)(2,1)}, bf16[1280,128]{1,0:T(8,128)(2,1)S(1)}, u32[]{:S(2)}, u32[]{:S(2)}) %collective-permute-start.2) | collective-permute-done | bytes 327712 | tf_op jit(solution)/shard_map/ppermute | solution.py:160
  83.4 10.9 %collective-permute-done.3.refs_0_ = bf16[1280,128]{1,0:T(8,128)(2,1)} collective-permute-done((bf16[1280,128]{1,0:T(8,128)(2,1)}, bf16[1280,128]{1,0:T(8,128)(2,1)}, u32[]{:S(2)}, u32[]{:S(2)}) %collective-permute-start.3) | collective-permute-done | bytes 327712 | tf_op jit(solution)/shard_map/ppermute | solution.py:160
  94.2 2.8 %collective-permute-done.10.refs_3_.refs_4_ = bf16[4,1280,128]{2,1,0:T(8,128)(2,1)} collective-permute-done((bf16[4,1280,128]{2,1,0:T(8,128)(2,1)S(1)}, bf16[4,1280,128]{2,1,0:T(8,128)(2,1)}, u32[]{:S(2)}, u32[]{:S(2)}) %collective-permute-start.10) | collective-permute-done | bytes 1310752 | tf_op jit(solution)/shard_map/ppermute | solution.py:172
  97.5 4.4 %collective-permute-done.11.refs_2_.refs_3_ = bf16[4,1280,128]{2,1,0:T(8,128)(2,1)S(1)} collective-permute-done((bf16[4,1280,128]{2,1,0:T(8,128)(2,1)S(1)}, bf16[4,1280,128]{2,1,0:T(8,128)(2,1)S(1)}, u32[]{:S(2)}, u32[]{:S(2)}) %collective-permute-start.11) | collective-permute-done | bytes 1310752 | tf_op jit(solution)/shard_map/ppermute | solution.py:172
  102.1 1.3 copy-done.1
  103.5 7.9 %attend_2.1 = bf16[1280,128]{1,0:T(8,128)(2,1)S(1)} custom-call(f32[256]{0:T(256)S(1)} %reshape.88.bias_ref, bf16[1280,128]{1,0:T(8,128)(2,1)} %collective-permute-done.3.refs_0_, bf16[4,1280,128]{2,1,0:T(8,128)(2,1)S(1)} %pad_maximum_fusion.1.refs_1_.refs_2_, bf16[4,1280,128]{2,1,0:T(8,128)(2,1)S(1)} %collective-permute-done.11.refs_2_.refs_3_, ...), custom_call_target="tpu_custom_call" | custom-call | tf_op jit(solution)/shard_map/attend_2/pallas_call | solution.py:246
  111.4 4.9 %collective-permute-start.17 = (bf16[1280,128]{1,0:T(8,128)(2,1)S(1)}, bf16[1280,128]{1,0:T(8,128)(2,1)S(1)}, u32[]{:S(2)}, u32[]{:S(2)}) collective-permute-start(bf16[1280,128]{1,0:T(8,128)(2,1)S(1)} %attend_2.1), channel_id=1, source_target_pairs={{0,16},{2,18},{4,20},{6,22},{8,24},{10,26},{12,28},{14,30},{16,0},... | collective-permute-start | bytes 983048 | tf_op jit(solution)/shard_map/ppermute | solution.py:160
  116.3 14.2 %attend_1_3.1 = (bf16[1280,128]{1,0:T(8,128)(2,1)S(1)}, bf16[1280,128]{1,0:T(8,128)(2,1)S(1)}) custom-call(f32[256]{0:T(256)S(1)} %reshape.88.bias_ref, bf16[1280,128]{1,0:T(8,128)(2,1)S(1)} %collective-permute-done.2.refs_0_, bf16[1280,128]{1,0:T(8,128)(2,1)} %collective-permute-done.4.refs_1_, bf16[4,1280,128]{2,1,0:T(8,128)(2,1)S(1)} %pad_maximum_fusion.1.refs_1_.refs_2_, ...), custom_call_target="tpu_custom_call" | custom-call | tf_op jit(solution)/shard_map/attend_1_3/pallas_call | solution.py:246
  130.5 2.3 %collective-permute-start.15 = (bf16[1280,128]{1,0:T(8,128)(2,1)S(1)}, bf16[1280,128]{1,0:T(8,128)(2,1)S(1)}, u32[]{:S(2)}, u32[]{:S(2)}) collective-permute-start(bf16[1280,128]{1,0:T(8,128)(2,1)S(1)} %get-tuple-element.97), channel_id=1, source_target_pairs={{0,24},{2,26},{4,28},{6,30},{8,0},{10,2},{12,4},{14,6},{16,8},{18,... | collective-permute-start | bytes 983048 | tf_op jit(solution)/shard_map/ppermute | solution.py:160
  133.6 7.8 %attend_0.1.refs_0_ = bf16[1280,128]{1,0:T(8,128)(2,1)S(1)} custom-call(f32[256]{0:T(256)S(1)} %reshape.88.bias_ref, bf16[1280,128]{1,0:T(8,128)(2,1)S(1)} %get-tuple-element.102.refs_0_, bf16[4,1280,128]{2,1,0:T(8,128)(2,1)S(1)} %pad_maximum_fusion.1.refs_1_.refs_2_, bf16[4,1280,128]{2,1,0:T(8,128)(2,1)S(1)} %collective-permute-done.11.refs_2_.refs_3_, ...), custom_call_target="tpu_custom_call" | custom-call | tf_op jit(solution)/shard_map/attend_0/pallas_call | solution.py:246
  141.4 1.1 collect_0.1.refs_2_
  142.6 5.5 %collective-permute-done.15.refs_0_ = bf16[1280,128]{1,0:T(8,128)(2,1)S(1)} collective-permute-done((bf16[1280,128]{1,0:T(8,128)(2,1)S(1)}, bf16[1280,128]{1,0:T(8,128)(2,1)S(1)}, u32[]{:S(2)}, u32[]{:S(2)}) %collective-permute-start.15) | collective-permute-done | bytes 327712 | tf_op jit(solution)/shard_map/ppermute | solution.py:160
  148.1 1.1 collect_1.1
  (74 shorter events, 8.8 us)
Async XLA Ops:
  0.0 8.5 %copy-start.14 = (f32[2560]{0:T(1024)S(1)}, f32[2560]{0:T(1024)}, u32[]{:S(2)}) copy-start(f32[2560]{0:T(1024)} %param.10) | copy-start | bytes 30724
  0.0 8.5 %copy-start.15 = (f32[2560]{0:T(1024)S(1)}, f32[2560]{0:T(1024)}, u32[]{:S(2)}) copy-start(f32[2560]{0:T(1024)} %param.11) | copy-start | bytes 30724
  2.4 23.3 %collective-permute-start = (bf16[1280,128]{1,0:T(8,128)(2,1)}, bf16[1280,128]{1,0:T(8,128)(2,1)}, u32[]{:S(2)}, u32[]{:S(2)}) collective-permute-start(bf16[1280,128]{1,0:T(8,128)(2,1)} %get-tuple-element.64), channel_id=1, source_target_pairs={{0,24},{2,26},{4,28},{6,30},{8,0},{10,2},{12,4},{14,6},{16,8},{18,... | collective-permute-start | bytes 983048 | tf_op jit(solution)/shard_map/ppermute | solution.py:160
  7.4 18.2 %collective-permute-start.5 = (bf16[1280,128]{1,0:T(8,128)(2,1)}, bf16[1280,128]{1,0:T(8,128)(2,1)}, u32[]{:S(2)}, u32[]{:S(2)}) collective-permute-start(bf16[1280,128]{1,0:T(8,128)(2,1)} %get-tuple-element.73), channel_id=1, source_target_pairs={{0,8},{2,10},{4,12},{6,14},{8,16},{10,18},{12,20},{14,22},{16,24},... | collective-permute-start | bytes 983048 | tf_op jit(solution)/shard_map/ppermute | solution.py:160
  7.4 28.2 %collective-permute-start.7 = (bf16[1280,128]{1,0:T(8,128)(2,1)}, bf16[1280,128]{1,0:T(8,128)(2,1)}, u32[]{:S(2)}, u32[]{:S(2)}) collective-permute-start(bf16[1280,128]{1,0:T(8,128)(2,1)} %get-tuple-element.76), channel_id=1, source_target_pairs={{0,16},{2,18},{4,20},{6,22},{8,24},{10,26},{12,28},{14,30},{16,0},... | collective-permute-start | bytes 983048 | tf_op jit(solution)/shard_map/ppermute | solution.py:160
  8.5 1.7 %copy-start.2 = (f32[256,2560]{1,0:T(8,128)S(1)}, f32[256,2560]{1,0:T(8,128)}, u32[]{:S(2)}) copy-start(f32[256,2560]{1,0:T(8,128)} %q_ref.1) | copy-start | bytes 7864324
  12.0 10.8 %copy-start.17 = (s32[32]{0:T(128)S(1)}, s32[32]{0:T(128)}, u32[]{:S(2)}) copy-start(s32[32]{0:T(128)} %param.12) | copy-start | bytes 388
  12.0 10.9 %copy-start.16 = (s32[2,32]{1,0:T(2,128)S(1)}, s32[2,32]{1,0:T(2,128)}, u32[]{:S(2)}) copy-start(s32[2,32]{1,0:T(2,128)} %param.13) | copy-start | bytes 772
  12.0 11.0 %copy-start.3 = (f32[256,2560]{1,0:T(8,128)S(1)}, f32[256,2560]{1,0:T(8,128)}, u32[]{:S(2)}) copy-start(f32[256,2560]{1,0:T(8,128)} %q_ref.1) | copy-start | bytes 7864324
  23.0 1.7 %copy-start.5 = (f32[256,2560]{1,0:T(8,128)S(1)}, f32[256,2560]{1,0:T(8,128)}, u32[]{:S(2)}) copy-start(f32[256,2560]{1,0:T(8,128)} %k_ref.1) | copy-start | bytes 7864324
  25.6 42.2 %copy-start.7 = (bf16[1296,128]{1,0:T(8,128)(2,1)}, bf16[1296,128]{1,0:T(8,128)(2,1)S(1)}, u32[]{:S(2)}) copy-start(bf16[1296,128]{1,0:T(8,128)(2,1)S(1)} %get-tuple-element.82) | copy-start | bytes 995332
  25.6 42.5 %copy-start.8 = (bf16[1280,128]{1,0:T(8,128)(2,1)}, bf16[1280,128]{1,0:T(8,128)(2,1)S(1)}, u32[]{:S(2)}) copy-start(bf16[1280,128]{1,0:T(8,128)(2,1)S(1)} %get-tuple-element.70) | copy-start | bytes 983044
  25.6 42.5 %copy-start.9 = (bf16[1280,128]{1,0:T(8,128)(2,1)}, bf16[1280,128]{1,0:T(8,128)(2,1)S(1)}, u32[]{:S(2)}) copy-start(bf16[1280,128]{1,0:T(8,128)(2,1)S(1)} %get-tuple-element.68) | copy-start | bytes 983044
  25.6 42.5 %copy-start.10 = (bf16[1280,128]{1,0:T(8,128)(2,1)}, bf16[1280,128]{1,0:T(8,128)(2,1)S(1)}, u32[]{:S(2)}) copy-start(bf16[1280,128]{1,0:T(8,128)(2,1)S(1)} %get-tuple-element.66) | copy-start | bytes 983044
  37.0 29.7 %collective-permute-start.9 = (bf16[4,1280,128]{2,1,0:T(8,128)(2,1)S(1)}, bf16[4,1280,128]{2,1,0:T(8,128)(2,1)S(1)}, u32[]{:S(2)}, u32[]{:S(2)}) collective-permute-start(bf16[4,1280,128]{2,1,0:T(8,128)(2,1)S(1)} %pad_maximum_fusion.refs_5_.refs_6_), channel_id=1, source_target_pairs={{0,4},{2,6},{4,0},{6,2},{8,12},{10,14},{12,8},{14,10},{16,20},{18,... | collective-permute-start | bytes 3932168 | tf_op jit(solution)/shard_map/ppermute | solution.py:172
  38.6 23.3 %collective-permute-start.8 = (bf16[1296,128]{1,0:T(8,128)(2,1)S(1)}, bf16[1296,128]{1,0:T(8,128)(2,1)S(1)}, u32[]{:S(2)}, u32[]{:S(2)}) collective-permute-start(bf16[1296,128]{1,0:T(8,128)(2,1)S(1)} %get-tuple-element.77), channel_id=1, source_target_pairs={{0,16},{2,18},{4,20},{6,22},{8,24},{10,26},{12,28},{14,30},{16,0},... | collective-permute-start | bytes 995336 | tf_op jit(solution)/shard_map/ppermute | solution.py:160
  38.6 23.3 %collective-permute-start.6 = (bf16[1296,128]{1,0:T(8,128)(2,1)S(1)}, bf16[1296,128]{1,0:T(8,128)(2,1)S(1)}, u32[]{:S(2)}, u32[]{:S(2)}) collective-permute-start(bf16[1296,128]{1,0:T(8,128)(2,1)S(1)} %get-tuple-element.74), channel_id=1, source_target_pairs={{0,8},{2,10},{4,12},{6,14},{8,16},{10,18},{12,20},{14,22},{16,24},... | collective-permute-start | bytes 995336 | tf_op jit(solution)/shard_map/ppermute | solution.py:160
  41.8 21.6 %collective-permute-start.1 = (bf16[1296,128]{1,0:T(8,128)(2,1)S(1)}, bf16[1296,128]{1,0:T(8,128)(2,1)S(1)}, u32[]{:S(2)}, u32[]{:S(2)}) collective-permute-start(bf16[1296,128]{1,0:T(8,128)(2,1)S(1)} %get-tuple-element.65), channel_id=1, source_target_pairs={{0,24},{2,26},{4,28},{6,30},{8,0},{10,2},{12,4},{14,6},{16,8},{18,... | collective-permute-start | bytes 995336 | tf_op jit(solution)/shard_map/ppermute | solution.py:160
  61.9 6.0 %copy-start.11 = (bf16[1296,128]{1,0:T(8,128)(2,1)}, bf16[1296,128]{1,0:T(8,128)(2,1)S(1)}, u32[]{:S(2)}) copy-start(bf16[1296,128]{1,0:T(8,128)(2,1)S(1)} %collective-permute-done.8) | copy-start | bytes 995332
  61.9 6.0 %copy-start.12 = (bf16[1296,128]{1,0:T(8,128)(2,1)}, bf16[1296,128]{1,0:T(8,128)(2,1)S(1)}, u32[]{:S(2)}) copy-start(bf16[1296,128]{1,0:T(8,128)(2,1)S(1)} %collective-permute-done.6) | copy-start | bytes 995332
  63.4 4.5 %copy-start.13 = (bf16[1296,128]{1,0:T(8,128)(2,1)}, bf16[1296,128]{1,0:T(8,128)(2,1)S(1)}, u32[]{:S(2)}) copy-start(bf16[1296,128]{1,0:T(8,128)(2,1)S(1)} %collective-permute-done.1) | copy-start | bytes 995332
  68.1 28.9 %collective-permute-start.10 = (bf16[4,1280,128]{2,1,0:T(8,128)(2,1)S(1)}, bf16[4,1280,128]{2,1,0:T(8,128)(2,1)}, u32[]{:S(2)}, u32[]{:S(2)}) collective-permute-start(bf16[4,1280,128]{2,1,0:T(8,128)(2,1)S(1)} %pad_maximum_fusion.1.refs_1_.refs_2_), channel_id=1, source_target_pairs={{0,4},{2,6},{4,0},{6,2},{8,12},{10,14},{12,8},{14,10},{16,20},{18,... | collective-permute-start | bytes 3932168 | tf_op jit(solution)/shard_map/ppermute | solution.py:172
  70.6 12.8 %collective-permute-start.2 = (bf16[1280,128]{1,0:T(8,128)(2,1)}, bf16[1280,128]{1,0:T(8,128)(2,1)S(1)}, u32[]{:S(2)}, u32[]{:S(2)}) collective-permute-start(bf16[1280,128]{1,0:T(8,128)(2,1)} %copy-done.10), channel_id=1, source_target_pairs={{0,8},{2,10},{4,12},{6,14},{8,16},{10,18},{12,20},{14,22},{16,24},... | collective-permute-start | bytes 983048 | tf_op jit(solution)/shard_map/ppermute | solution.py:160
  72.4 21.9 %collective-permute-start.3 = (bf16[1280,128]{1,0:T(8,128)(2,1)}, bf16[1280,128]{1,0:T(8,128)(2,1)}, u32[]{:S(2)}, u32[]{:S(2)}) collective-permute-start(bf16[1280,128]{1,0:T(8,128)(2,1)} %copy-done.9), channel_id=1, source_target_pairs={{0,16},{2,18},{4,20},{6,22},{8,24},{10,26},{12,28},{14,30},{16,0},... | collective-permute-start | bytes 983048 | tf_op jit(solution)/shard_map/ppermute | solution.py:160
  73.5 20.8 %collective-permute-start.4 = (bf16[1280,128]{1,0:T(8,128)(2,1)}, bf16[1280,128]{1,0:T(8,128)(2,1)}, u32[]{:S(2)}, u32[]{:S(2)}) collective-permute-start(bf16[1280,128]{1,0:T(8,128)(2,1)} %copy-done.8), channel_id=1, source_target_pairs={{0,24},{2,26},{4,28},{6,30},{8,0},{10,2},{12,4},{14,6},{16,8},{18,... | collective-permute-start | bytes 983048 | tf_op jit(solution)/shard_map/ppermute | solution.py:160
  78.2 19.3 %collective-permute-start.13 = (bf16[4,1280,128]{2,1,0:T(8,128)(2,1)S(1)}, bf16[4,1280,128]{2,1,0:T(8,128)(2,1)S(1)}, u32[]{:S(2)}, u32[]{:S(2)}) collective-permute-start(bf16[4,1280,128]{2,1,0:T(8,128)(2,1)S(1)} %pad_maximum_fusion.refs_5_.refs_6_), channel_id=1, source_target_pairs={{0,2},{2,0},{4,6},{6,4},{8,10},{10,8},{12,14},{14,12},{16,18},{18,... | collective-permute-start | bytes 3932168 | tf_op jit(solution)/shard_map/ppermute | solution.py:172
  83.4 14.2 %collective-permute-start.14 = (bf16[4,1280,128]{2,1,0:T(8,128)(2,1)}, bf16[4,1280,128]{2,1,0:T(8,128)(2,1)S(1)}, u32[]{:S(2)}, u32[]{:S(2)}) collective-permute-start(bf16[4,1280,128]{2,1,0:T(8,128)(2,1)} %copy-done), channel_id=1, source_target_pairs={{0,2},{2,0},{4,6},{6,4},{8,10},{10,8},{12,14},{14,12},{16,18},{18,... | collective-permute-start | bytes 3932168 | tf_op jit(solution)/shard_map/ppermute | solution.py:172
  97.0 4.9 %collective-permute-start.11 = (bf16[4,1280,128]{2,1,0:T(8,128)(2,1)S(1)}, bf16[4,1280,128]{2,1,0:T(8,128)(2,1)S(1)}, u32[]{:S(2)}, u32[]{:S(2)}) collective-permute-start(bf16[4,1280,128]{2,1,0:T(8,128)(2,1)S(1)} %pad_maximum_fusion.1.refs_1_.refs_2_), channel_id=1, source_target_pairs={{0,2},{2,0},{4,6},{6,4},{8,10},{10,8},{12,14},{14,12},{16,18},{18,... | collective-permute-start | bytes 3932168 | tf_op jit(solution)/shard_map/ppermute | solution.py:172
  97.0 5.1 %collective-permute-start.12 = (bf16[4,1280,128]{2,1,0:T(8,128)(2,1)}, bf16[4,1280,128]{2,1,0:T(8,128)(2,1)S(1)}, u32[]{:S(2)}, u32[]{:S(2)}) collective-permute-start(bf16[4,1280,128]{2,1,0:T(8,128)(2,1)} %collective-permute-done.10.refs_3_.refs_4_), channel_id=1, source_target_pairs={{0,2},{2,0},{4,6},{6,4},{8,10},{10,8},{12,14},{14,12},{16,18},{18,... | collective-permute-start | bytes 3932168 | tf_op jit(solution)/shard_map/ppermute | solution.py:172
  111.4 22.3 %collective-permute-start.17 = (bf16[1280,128]{1,0:T(8,128)(2,1)S(1)}, bf16[1280,128]{1,0:T(8,128)(2,1)S(1)}, u32[]{:S(2)}, u32[]{:S(2)}) collective-permute-start(bf16[1280,128]{1,0:T(8,128)(2,1)S(1)} %attend_2.1), channel_id=1, source_target_pairs={{0,16},{2,18},{4,20},{6,22},{8,24},{10,26},{12,28},{14,30},{16,0},... | collective-permute-start | bytes 983048 | tf_op jit(solution)/shard_map/ppermute | solution.py:160
  130.5 17.6 %collective-permute-start.15 = (bf16[1280,128]{1,0:T(8,128)(2,1)S(1)}, bf16[1280,128]{1,0:T(8,128)(2,1)S(1)}, u32[]{:S(2)}, u32[]{:S(2)}) collective-permute-start(bf16[1280,128]{1,0:T(8,128)(2,1)S(1)} %get-tuple-element.97), channel_id=1, source_target_pairs={{0,24},{2,26},{4,28},{6,30},{8,0},{10,2},{12,4},{14,6},{16,8},{18,... | collective-permute-start | bytes 983048 | tf_op jit(solution)/shard_map/ppermute | solution.py:160
  132.8 15.2 %collective-permute-start.16 = (bf16[1280,128]{1,0:T(8,128)(2,1)S(1)}, bf16[1280,128]{1,0:T(8,128)(2,1)S(1)}, u32[]{:S(2)}, u32[]{:S(2)}) collective-permute-start(bf16[1280,128]{1,0:T(8,128)(2,1)S(1)} %get-tuple-element.98), channel_id=1, source_target_pairs={{0,8},{2,10},{4,12},{6,14},{8,16},{10,18},{12,20},{14,22},{16,24},... | collective-permute-start | bytes 983048 | tf_op jit(solution)/shard_map/ppermute | solution.py:160
  (4 other events, 5.5 us)

commit v7 on v6

--- a/solution.py
+++ b/solution.py
@@ -24,13 +24,24 @@
     return pl.multiple_of((group * per_group + head) * HEAD_DIM, HEAD_DIM)
 
 
-def value_kernel(place_ref, v_ref, *outs, per_group):
-    groups = len(outs)
+def value_kernel(place_ref, v_ref, *refs, per_group):
+    outs, semaphores = refs[:-1], refs[-1]
     rows = v_ref.shape[0]
+    copies = []
     for shift, out in enumerate(outs):
         for head in range(per_group):
-            column = column_of(place_ref, shift, head, groups, per_group)
-            out[head * rows : (head + 1) * rows, :] = v_ref[:, pl.ds(column, HEAD_DIM)]
+            column = column_of(place_ref, shift, head, len(outs), per_group)
+            copies.append(
+                pltpu.make_async_copy(
+                    v_ref.at[:, pl.ds(column, HEAD_DIM)],
+                    out.at[pl.ds(head * rows, rows), :],
+                    semaphores.at[len(copies)],
+                )
+            )
+    for copy in copies:
+        copy.start()
+    for copy in copies:
+        copy.wait()
 
 
 def square_sums_kernel(q_ref, k_ref, out_ref):
@@ -179,8 +190,9 @@
     v_pieces = pl.pallas_call(
         functools.partial(value_kernel, per_group=per_group),
         out_shape=[jax.ShapeDtypeStruct((per_group * rows, HEAD_DIM), bf16)] * groups,
-        in_specs=[SMEM, VMEM],
-        out_specs=[VMEM] * groups,
+        in_specs=[SMEM, ANY],
+        out_specs=[ANY] * groups,
+        scratch_shapes=[pltpu.SemaphoreType.DMA((groups * per_group,))],
         compiler_params=params,
         name="value_pieces",
     )(place_row, v_in)

time: 150 us -> 150 us (level)
  no operation moved by 1% of the time
where the time goes in v7:
time: 150 us; the launch traced here: 149 us
  waiting for transfers between devices  63.1 us (42%)
  Pallas kernels  34.6 us (23%)
  starting transfers between devices  26.6 us (18%)
  local copies, waits for them, and re-layouts  12.6 us (8%)
  blocking collectives  10.4 us (7%)
  other arithmetic  1.74 us (1%)
    ppermute x12, waiting for transfers between devices, rotated(): return lax.ppermute(x, 'seq', pairs)  52.4 us
    pallas_call x3, Pallas kernels, attend(): pl.pallas_call(functools.partial(attend_kernel, query_slots=query_slots,...  29.9 us
    ppermute x12, starting transfers between devices, rotated(): return lax.ppermute(x, 'seq', pairs)  22.8 us
    ppermute x6, waiting for transfers between devices, swapped(): return lax.ppermute(x, 'seq', [(i, i ^ bit) for i in range(devices)])  10.7 us
    psum x1, blocking collectives, exchanged(): sums = lax.psum(sums, 'tensor')  10.4 us
    unnamed x36, local copies, waits for them, and re-layouts  8.97 us
    ppermute x6, starting transfers between devices, swapped(): return lax.ppermute(x, 'seq', [(i, i ^ bit) for i in range(devices)])  3.75 us
  transfers between devices with their start and end apart: 18, of which 10 were waited for; matrix products, arithmetic and copies ran while one was open for 3% of the time, Pallas kernels for 16%

profile of v7, /device:TPU:0, one launch (start us, length us, event | category | flops | bytes accessed | tf_op | source)
XLA Modules:
  0.0 149.3 jit_solution(11356148405612679759)
XLA Ops:
  0.0 1.3 copy-done.6
  1.3 1.2 value_pieces.1
  2.5 5.1 %collective-permute-start = (bf16[1280,128]{1,0:T(8,128)(2,1)}, bf16[1280,128]{1,0:T(8,128)(2,1)}, u32[]{:S(2)}, u32[]{:S(2)}) collective-permute-start(bf16[1280,128]{1,0:T(8,128)(2,1)} %get-tuple-element.64), channel_id=1, source_target_pairs={{0,24},{2,26},{4,28},{6,30},{8,0},{10,2},{12,4},{14,6},{16,8},{18,... | collective-permute-start | bytes 983048 | tf_op jit(solution)/shard_map/ppermute | solution.py:171
  8.7 1.7 %copy-done.2 = f32[256,2560]{1,0:T(8,128)S(1)} copy-done((f32[256,2560]{1,0:T(8,128)S(1)}, f32[256,2560]{1,0:T(8,128)}, u32[]{:S(2)}) %copy-start.2) | copy-done | bytes 2621464
  10.4 1.7 %copy-done.4 = f32[256,2560]{1,0:T(8,128)S(1)} copy-done((f32[256,2560]{1,0:T(8,128)S(1)}, f32[256,2560]{1,0:T(8,128)}, u32[]{:S(2)}) %copy-start.4) | copy-done | bytes 2621464
  12.6 10.4 %psum.7.sums_ref = f32[256,2]{1,0:T(8,128)S(1)} all-reduce(f32[256,2]{1,0:T(8,128)S(1)} %square_sums.1), channel_id=1, replica_groups=mesh['seq'=16,'tensor'=2] {'tensor'}, use_global_device_ids=true, to_apply=%region_0.1 | all-reduce | flops 512 | bytes 4096 | tf_op jit(solution)/shard_map/psum | solution.py:209
  23.2 1.7 %copy-done.5 = f32[256,2560]{1,0:T(8,128)S(1)} copy-done((f32[256,2560]{1,0:T(8,128)S(1)}, f32[256,2560]{1,0:T(8,128)}, u32[]{:S(2)}) %copy-start.5) | copy-done | bytes 2621464
  25.8 10.0 %collective-permute-done.7 = bf16[1280,128]{1,0:T(8,128)(2,1)} collective-permute-done((bf16[1280,128]{1,0:T(8,128)(2,1)}, bf16[1280,128]{1,0:T(8,128)(2,1)}, u32[]{:S(2)}, u32[]{:S(2)}) %collective-permute-start.7) | collective-permute-done | bytes 327712 | tf_op jit(solution)/shard_map/ppermute | solution.py:171
  35.9 1.3 pad_maximum_fusion.refs_5_.refs_6_
  37.2 1.6 %collective-permute-start.9 = (bf16[4,1280,128]{2,1,0:T(8,128)(2,1)S(1)}, bf16[4,1280,128]{2,1,0:T(8,128)(2,1)S(1)}, u32[]{:S(2)}, u32[]{:S(2)}) collective-permute-start(bf16[4,1280,128]{2,1,0:T(8,128)(2,1)S(1)} %pad_maximum_fusion.refs_5_.refs_6_), channel_id=1, source_target_pairs={{0,4},{2,6},{4,0},{6,2},{8,12},{10,14},{12,8},{14,10},{16,20},{18,... | collective-permute-start | bytes 3932168 | tf_op jit(solution)/shard_map/ppermute | solution.py:183
  38.8 3.2 %collective-permute-start.6 = (bf16[1296,128]{1,0:T(8,128)(2,1)S(1)}, bf16[1296,128]{1,0:T(8,128)(2,1)S(1)}, u32[]{:S(2)}, u32[]{:S(2)}) collective-permute-start(bf16[1296,128]{1,0:T(8,128)(2,1)S(1)} %get-tuple-element.74), channel_id=1, source_target_pairs={{0,8},{2,10},{4,12},{6,14},{8,16},{10,18},{12,20},{14,22},{16,24},... | collective-permute-start | bytes 995336 | tf_op jit(solution)/shard_map/ppermute | solution.py:171
  42.7 19.4 %collective-permute-done.8 = bf16[1296,128]{1,0:T(8,128)(2,1)S(1)} collective-permute-done((bf16[1296,128]{1,0:T(8,128)(2,1)S(1)}, bf16[1296,128]{1,0:T(8,128)(2,1)S(1)}, u32[]{:S(2)}, u32[]{:S(2)}) %collective-permute-start.8) | collective-permute-done | bytes 331808 | tf_op jit(solution)/shard_map/ppermute | solution.py:171
  62.1 1.5 %collective-permute-done.1 = bf16[1296,128]{1,0:T(8,128)(2,1)S(1)} collective-permute-done((bf16[1296,128]{1,0:T(8,128)(2,1)S(1)}, bf16[1296,128]{1,0:T(8,128)(2,1)S(1)}, u32[]{:S(2)}, u32[]{:S(2)}) %collective-permute-start.1) | collective-permute-done | bytes 331808 | tf_op jit(solution)/shard_map/ppermute | solution.py:171
  63.6 3.3 %collective-permute-done.9.refs_7_.refs_8_ = bf16[4,1280,128]{2,1,0:T(8,128)(2,1)S(1)} collective-permute-done((bf16[4,1280,128]{2,1,0:T(8,128)(2,1)S(1)}, bf16[4,1280,128]{2,1,0:T(8,128)(2,1)S(1)}, u32[]{:S(2)}, u32[]{:S(2)}) %collective-permute-start.9) | collective-permute-done | bytes 1310752 | tf_op jit(solution)/shard_map/ppermute | solution.py:183
  66.9 1.1 copy-done
  68.3 1.6 %collective-permute-start.10 = (bf16[4,1280,128]{2,1,0:T(8,128)(2,1)S(1)}, bf16[4,1280,128]{2,1,0:T(8,128)(2,1)}, u32[]{:S(2)}, u32[]{:S(2)}) collective-permute-start(bf16[4,1280,128]{2,1,0:T(8,128)(2,1)S(1)} %pad_maximum_fusion.1.refs_1_.refs_2_), channel_id=1, source_target_pairs={{0,4},{2,6},{4,0},{6,2},{8,12},{10,14},{12,8},{14,10},{16,20},{18,... | collective-permute-start | bytes 3932168 | tf_op jit(solution)/shard_map/ppermute | solution.py:183
  70.7 1.8 %collective-permute-start.2 = (bf16[1280,128]{1,0:T(8,128)(2,1)}, bf16[1280,128]{1,0:T(8,128)(2,1)S(1)}, u32[]{:S(2)}, u32[]{:S(2)}) collective-permute-start(bf16[1280,128]{1,0:T(8,128)(2,1)} %copy-done.10), channel_id=1, source_target_pairs={{0,8},{2,10},{4,12},{6,14},{8,16},{10,18},{12,20},{14,22},{16,24},... | collective-permute-start | bytes 983048 | tf_op jit(solution)/shard_map/ppermute | solution.py:171
  72.6 1.1 collective-permute-start.3
  73.6 1.9 %collective-permute-start.4 = (bf16[1280,128]{1,0:T(8,128)(2,1)}, bf16[1280,128]{1,0:T(8,128)(2,1)}, u32[]{:S(2)}, u32[]{:S(2)}) collective-permute-start(bf16[1280,128]{1,0:T(8,128)(2,1)} %copy-done.8), channel_id=1, source_target_pairs={{0,24},{2,26},{4,28},{6,30},{8,0},{10,2},{12,4},{14,6},{16,8},{18,... | collective-permute-start | bytes 983048 | tf_op jit(solution)/shard_map/ppermute | solution.py:171
  78.5 5.1 %collective-permute-done.2.refs_0_ = bf16[1280,128]{1,0:T(8,128)(2,1)S(1)} collective-permute-done((bf16[1280,128]{1,0:T(8,128)(2,1)}, bf16[1280,128]{1,0:T(8,128)(2,1)S(1)}, u32[]{:S(2)}, u32[]{:S(2)}) %collective-permute-start.2) | collective-permute-done | bytes 327712 | tf_op jit(solution)/shard_map/ppermute | solution.py:171
  83.5 10.9 %collective-permute-done.3.refs_0_ = bf16[1280,128]{1,0:T(8,128)(2,1)} collective-permute-done((bf16[1280,128]{1,0:T(8,128)(2,1)}, bf16[1280,128]{1,0:T(8,128)(2,1)}, u32[]{:S(2)}, u32[]{:S(2)}) %collective-permute-start.3) | collective-permute-done | bytes 327712 | tf_op jit(solution)/shard_map/ppermute | solution.py:171
  94.4 2.8 %collective-permute-done.10.refs_3_.refs_4_ = bf16[4,1280,128]{2,1,0:T(8,128)(2,1)} collective-permute-done((bf16[4,1280,128]{2,1,0:T(8,128)(2,1)S(1)}, bf16[4,1280,128]{2,1,0:T(8,128)(2,1)}, u32[]{:S(2)}, u32[]{:S(2)}) %collective-permute-start.10) | collective-permute-done | bytes 1310752 | tf_op jit(solution)/shard_map/ppermute | solution.py:183
  97.7 4.4 %collective-permute-done.11.refs_2_.refs_3_ = bf16[4,1280,128]{2,1,0:T(8,128)(2,1)S(1)} collective-permute-done((bf16[4,1280,128]{2,1,0:T(8,128)(2,1)S(1)}, bf16[4,1280,128]{2,1,0:T(8,128)(2,1)S(1)}, u32[]{:S(2)}, u32[]{:S(2)}) %collective-permute-start.11) | collective-permute-done | bytes 1310752 | tf_op jit(solution)/shard_map/ppermute | solution.py:183
  102.3 1.3 copy-done.1
  103.6 7.9 %attend_2.1 = bf16[1280,128]{1,0:T(8,128)(2,1)S(1)} custom-call(f32[256]{0:T(256)S(1)} %reshape.88.bias_ref, bf16[1280,128]{1,0:T(8,128)(2,1)} %collective-permute-done.3.refs_0_, bf16[4,1280,128]{2,1,0:T(8,128)(2,1)S(1)} %pad_maximum_fusion.1.refs_1_.refs_2_, bf16[4,1280,128]{2,1,0:T(8,128)(2,1)S(1)} %collective-permute-done.11.refs_2_.refs_3_, ...), custom_call_target="tpu_custom_call" | custom-call | tf_op jit(solution)/shard_map/attend_2/pallas_call | solution.py:258
  111.5 4.9 %collective-permute-start.17 = (bf16[1280,128]{1,0:T(8,128)(2,1)S(1)}, bf16[1280,128]{1,0:T(8,128)(2,1)S(1)}, u32[]{:S(2)}, u32[]{:S(2)}) collective-permute-start(bf16[1280,128]{1,0:T(8,128)(2,1)S(1)} %attend_2.1), channel_id=1, source_target_pairs={{0,16},{2,18},{4,20},{6,22},{8,24},{10,26},{12,28},{14,30},{16,0},... | collective-permute-start | bytes 983048 | tf_op jit(solution)/shard_map/ppermute | solution.py:171
  116.5 14.2 %attend_1_3.1 = (bf16[1280,128]{1,0:T(8,128)(2,1)S(1)}, bf16[1280,128]{1,0:T(8,128)(2,1)S(1)}) custom-call(f32[256]{0:T(256)S(1)} %reshape.88.bias_ref, bf16[1280,128]{1,0:T(8,128)(2,1)S(1)} %collective-permute-done.2.refs_0_, bf16[1280,128]{1,0:T(8,128)(2,1)} %collective-permute-done.4.refs_1_, bf16[4,1280,128]{2,1,0:T(8,128)(2,1)S(1)} %pad_maximum_fusion.1.refs_1_.refs_2_, ...), custom_call_target="tpu_custom_call" | custom-call | tf_op jit(solution)/shard_map/attend_1_3/pallas_call | solution.py:258
  130.7 2.3 %collective-permute-start.15 = (bf16[1280,128]{1,0:T(8,128)(2,1)S(1)}, bf16[1280,128]{1,0:T(8,128)(2,1)S(1)}, u32[]{:S(2)}, u32[]{:S(2)}) collective-permute-start(bf16[1280,128]{1,0:T(8,128)(2,1)S(1)} %get-tuple-element.97), channel_id=1, source_target_pairs={{0,24},{2,26},{4,28},{6,30},{8,0},{10,2},{12,4},{14,6},{16,8},{18,... | collective-permute-start | bytes 983048 | tf_op jit(solution)/shard_map/ppermute | solution.py:171
  133.8 7.8 %attend_0.1.refs_0_ = bf16[1280,128]{1,0:T(8,128)(2,1)S(1)} custom-call(f32[256]{0:T(256)S(1)} %reshape.88.bias_ref, bf16[1280,128]{1,0:T(8,128)(2,1)S(1)} %get-tuple-element.102.refs_0_, bf16[4,1280,128]{2,1,0:T(8,128)(2,1)S(1)} %pad_maximum_fusion.1.refs_1_.refs_2_, bf16[4,1280,128]{2,1,0:T(8,128)(2,1)S(1)} %collective-permute-done.11.refs_2_.refs_3_, ...), custom_call_target="tpu_custom_call" | custom-call | tf_op jit(solution)/shard_map/attend_0/pallas_call | solution.py:258
  141.6 1.1 collect_0.1.refs_2_
  142.7 5.5 %collective-permute-done.15.refs_0_ = bf16[1280,128]{1,0:T(8,128)(2,1)S(1)} collective-permute-done((bf16[1280,128]{1,0:T(8,128)(2,1)S(1)}, bf16[1280,128]{1,0:T(8,128)(2,1)S(1)}, u32[]{:S(2)}, u32[]{:S(2)}) %collective-permute-start.15) | collective-permute-done | bytes 327712 | tf_op jit(solution)/shard_map/ppermute | solution.py:171
  148.2 1.1 collect_1.1
  (74 shorter events, 8.8 us)
Async XLA Ops:
  0.0 8.6 %copy-start.14 = (f32[2560]{0:T(1024)S(1)}, f32[2560]{0:T(1024)}, u32[]{:S(2)}) copy-start(f32[2560]{0:T(1024)} %param.10) | copy-start | bytes 30724
  0.0 8.6 %copy-start.15 = (f32[2560]{0:T(1024)S(1)}, f32[2560]{0:T(1024)}, u32[]{:S(2)}) copy-start(f32[2560]{0:T(1024)} %param.11) | copy-start | bytes 30724
  2.5 23.3 %collective-permute-start = (bf16[1280,128]{1,0:T(8,128)(2,1)}, bf16[1280,128]{1,0:T(8,128)(2,1)}, u32[]{:S(2)}, u32[]{:S(2)}) collective-permute-start(bf16[1280,128]{1,0:T(8,128)(2,1)} %get-tuple-element.64), channel_id=1, source_target_pairs={{0,24},{2,26},{4,28},{6,30},{8,0},{10,2},{12,4},{14,6},{16,8},{18,... | collective-permute-start | bytes 983048 | tf_op jit(solution)/shard_map/ppermute | solution.py:171
  7.6 18.2 %collective-permute-start.5 = (bf16[1280,128]{1,0:T(8,128)(2,1)}, bf16[1280,128]{1,0:T(8,128)(2,1)}, u32[]{:S(2)}, u32[]{:S(2)}) collective-permute-start(bf16[1280,128]{1,0:T(8,128)(2,1)} %get-tuple-element.73), channel_id=1, source_target_pairs={{0,8},{2,10},{4,12},{6,14},{8,16},{10,18},{12,20},{14,22},{16,24},... | collective-permute-start | bytes 983048 | tf_op jit(solution)/shard_map/ppermute | solution.py:171
  7.6 28.2 %collective-permute-start.7 = (bf16[1280,128]{1,0:T(8,128)(2,1)}, bf16[1280,128]{1,0:T(8,128)(2,1)}, u32[]{:S(2)}, u32[]{:S(2)}) collective-permute-start(bf16[1280,128]{1,0:T(8,128)(2,1)} %get-tuple-element.76), channel_id=1, source_target_pairs={{0,16},{2,18},{4,20},{6,22},{8,24},{10,26},{12,28},{14,30},{16,0},... | collective-permute-start | bytes 983048 | tf_op jit(solution)/shard_map/ppermute | solution.py:171
  8.7 1.7 %copy-start.2 = (f32[256,2560]{1,0:T(8,128)S(1)}, f32[256,2560]{1,0:T(8,128)}, u32[]{:S(2)}) copy-start(f32[256,2560]{1,0:T(8,128)} %q_ref.1) | copy-start | bytes 7864324
  12.1 10.8 %copy-start.17 = (s32[32]{0:T(128)S(1)}, s32[32]{0:T(128)}, u32[]{:S(2)}) copy-start(s32[32]{0:T(128)} %param.12) | copy-start | bytes 388
  12.1 10.9 %copy-start.16 = (s32[2,32]{1,0:T(2,128)S(1)}, s32[2,32]{1,0:T(2,128)}, u32[]{:S(2)}) copy-start(s32[2,32]{1,0:T(2,128)} %param.13) | copy-start | bytes 772
  12.2 11.0 %copy-start.3 = (f32[256,2560]{1,0:T(8,128)S(1)}, f32[256,2560]{1,0:T(8,128)}, u32[]{:S(2)}) copy-start(f32[256,2560]{1,0:T(8,128)} %q_ref.1) | copy-start | bytes 7864324
  23.1 1.7 %copy-start.5 = (f32[256,2560]{1,0:T(8,128)S(1)}, f32[256,2560]{1,0:T(8,128)}, u32[]{:S(2)}) copy-start(f32[256,2560]{1,0:T(8,128)} %k_ref.1) | copy-start | bytes 7864324
  25.8 42.2 %copy-start.7 = (bf16[1296,128]{1,0:T(8,128)(2,1)}, bf16[1296,128]{1,0:T(8,128)(2,1)S(1)}, u32[]{:S(2)}) copy-start(bf16[1296,128]{1,0:T(8,128)(2,1)S(1)} %get-tuple-element.82) | copy-start | bytes 995332
  25.8 42.5 %copy-start.8 = (bf16[1280,128]{1,0:T(8,128)(2,1)}, bf16[1280,128]{1,0:T(8,128)(2,1)S(1)}, u32[]{:S(2)}) copy-start(bf16[1280,128]{1,0:T(8,128)(2,1)S(1)} %get-tuple-element.70) | copy-start | bytes 983044
  25.8 42.5 %copy-start.9 = (bf16[1280,128]{1,0:T(8,128)(2,1)}, bf16[1280,128]{1,0:T(8,128)(2,1)S(1)}, u32[]{:S(2)}) copy-start(bf16[1280,128]{1,0:T(8,128)(2,1)S(1)} %get-tuple-element.68) | copy-start | bytes 983044
  25.8 42.5 %copy-start.10 = (bf16[1280,128]{1,0:T(8,128)(2,1)}, bf16[1280,128]{1,0:T(8,128)(2,1)S(1)}, u32[]{:S(2)}) copy-start(bf16[1280,128]{1,0:T(8,128)(2,1)S(1)} %get-tuple-element.66) | copy-start | bytes 983044
  37.2 29.7 %collective-permute-start.9 = (bf16[4,1280,128]{2,1,0:T(8,128)(2,1)S(1)}, bf16[4,1280,128]{2,1,0:T(8,128)(2,1)S(1)}, u32[]{:S(2)}, u32[]{:S(2)}) collective-permute-start(bf16[4,1280,128]{2,1,0:T(8,128)(2,1)S(1)} %pad_maximum_fusion.refs_5_.refs_6_), channel_id=1, source_target_pairs={{0,4},{2,6},{4,0},{6,2},{8,12},{10,14},{12,8},{14,10},{16,20},{18,... | collective-permute-start | bytes 3932168 | tf_op jit(solution)/shard_map/ppermute | solution.py:183
  38.8 23.3 %collective-permute-start.8 = (bf16[1296,128]{1,0:T(8,128)(2,1)S(1)}, bf16[1296,128]{1,0:T(8,128)(2,1)S(1)}, u32[]{:S(2)}, u32[]{:S(2)}) collective-permute-start(bf16[1296,128]{1,0:T(8,128)(2,1)S(1)} %get-tuple-element.77), channel_id=1, source_target_pairs={{0,16},{2,18},{4,20},{6,22},{8,24},{10,26},{12,28},{14,30},{16,0},... | collective-permute-start | bytes 995336 | tf_op jit(solution)/shard_map/ppermute | solution.py:171
  38.8 23.3 %collective-permute-start.6 = (bf16[1296,128]{1,0:T(8,128)(2,1)S(1)}, bf16[1296,128]{1,0:T(8,128)(2,1)S(1)}, u32[]{:S(2)}, u32[]{:S(2)}) collective-permute-start(bf16[1296,128]{1,0:T(8,128)(2,1)S(1)} %get-tuple-element.74), channel_id=1, source_target_pairs={{0,8},{2,10},{4,12},{6,14},{8,16},{10,18},{12,20},{14,22},{16,24},... | collective-permute-start | bytes 995336 | tf_op jit(solution)/shard_map/ppermute | solution.py:171
  42.0 21.6 %collective-permute-start.1 = (bf16[1296,128]{1,0:T(8,128)(2,1)S(1)}, bf16[1296,128]{1,0:T(8,128)(2,1)S(1)}, u32[]{:S(2)}, u32[]{:S(2)}) collective-permute-start(bf16[1296,128]{1,0:T(8,128)(2,1)S(1)} %get-tuple-element.65), channel_id=1, source_target_pairs={{0,24},{2,26},{4,28},{6,30},{8,0},{10,2},{12,4},{14,6},{16,8},{18,... | collective-permute-start | bytes 995336 | tf_op jit(solution)/shard_map/ppermute | solution.py:171
  62.1 6.0 %copy-start.11 = (bf16[1296,128]{1,0:T(8,128)(2,1)}, bf16[1296,128]{1,0:T(8,128)(2,1)S(1)}, u32[]{:S(2)}) copy-start(bf16[1296,128]{1,0:T(8,128)(2,1)S(1)} %collective-permute-done.8) | copy-start | bytes 995332
  62.1 6.0 %copy-start.12 = (bf16[1296,128]{1,0:T(8,128)(2,1)}, bf16[1296,128]{1,0:T(8,128)(2,1)S(1)}, u32[]{:S(2)}) copy-start(bf16[1296,128]{1,0:T(8,128)(2,1)S(1)} %collective-permute-done.6) | copy-start | bytes 995332
  63.6 4.5 %copy-start.13 = (bf16[1296,128]{1,0:T(8,128)(2,1)}, bf16[1296,128]{1,0:T(8,128)(2,1)S(1)}, u32[]{:S(2)}) copy-start(bf16[1296,128]{1,0:T(8,128)(2,1)S(1)} %collective-permute-done.1) | copy-start | bytes 995332
  68.3 28.9 %collective-permute-start.10 = (bf16[4,1280,128]{2,1,0:T(8,128)(2,1)S(1)}, bf16[4,1280,128]{2,1,0:T(8,128)(2,1)}, u32[]{:S(2)}, u32[]{:S(2)}) collective-permute-start(bf16[4,1280,128]{2,1,0:T(8,128)(2,1)S(1)} %pad_maximum_fusion.1.refs_1_.refs_2_), channel_id=1, source_target_pairs={{0,4},{2,6},{4,0},{6,2},{8,12},{10,14},{12,8},{14,10},{16,20},{18,... | collective-permute-start | bytes 3932168 | tf_op jit(solution)/shard_map/ppermute | solution.py:183
  70.7 12.8 %collective-permute-start.2 = (bf16[1280,128]{1,0:T(8,128)(2,1)}, bf16[1280,128]{1,0:T(8,128)(2,1)S(1)}, u32[]{:S(2)}, u32[]{:S(2)}) collective-permute-start(bf16[1280,128]{1,0:T(8,128)(2,1)} %copy-done.10), channel_id=1, source_target_pairs={{0,8},{2,10},{4,12},{6,14},{8,16},{10,18},{12,20},{14,22},{16,24},... | collective-permute-start | bytes 983048 | tf_op jit(solution)/shard_map/ppermute | solution.py:171
  72.6 21.9 %collective-permute-start.3 = (bf16[1280,128]{1,0:T(8,128)(2,1)}, bf16[1280,128]{1,0:T(8,128)(2,1)}, u32[]{:S(2)}, u32[]{:S(2)}) collective-permute-start(bf16[1280,128]{1,0:T(8,128)(2,1)} %copy-done.9), channel_id=1, source_target_pairs={{0,16},{2,18},{4,20},{6,22},{8,24},{10,26},{12,28},{14,30},{16,0},... | collective-permute-start | bytes 983048 | tf_op jit(solution)/shard_map/ppermute | solution.py:171
  73.6 20.8 %collective-permute-start.4 = (bf16[1280,128]{1,0:T(8,128)(2,1)}, bf16[1280,128]{1,0:T(8,128)(2,1)}, u32[]{:S(2)}, u32[]{:S(2)}) collective-permute-start(bf16[1280,128]{1,0:T(8,128)(2,1)} %copy-done.8), channel_id=1, source_target_pairs={{0,24},{2,26},{4,28},{6,30},{8,0},{10,2},{12,4},{14,6},{16,8},{18,... | collective-permute-start | bytes 983048 | tf_op jit(solution)/shard_map/ppermute | solution.py:171
  78.4 19.3 %collective-permute-start.13 = (bf16[4,1280,128]{2,1,0:T(8,128)(2,1)S(1)}, bf16[4,1280,128]{2,1,0:T(8,128)(2,1)S(1)}, u32[]{:S(2)}, u32[]{:S(2)}) collective-permute-start(bf16[4,1280,128]{2,1,0:T(8,128)(2,1)S(1)} %pad_maximum_fusion.refs_5_.refs_6_), channel_id=1, source_target_pairs={{0,2},{2,0},{4,6},{6,4},{8,10},{10,8},{12,14},{14,12},{16,18},{18,... | collective-permute-start | bytes 3932168 | tf_op jit(solution)/shard_map/ppermute | solution.py:183
  83.5 14.2 %collective-permute-start.14 = (bf16[4,1280,128]{2,1,0:T(8,128)(2,1)}, bf16[4,1280,128]{2,1,0:T(8,128)(2,1)S(1)}, u32[]{:S(2)}, u32[]{:S(2)}) collective-permute-start(bf16[4,1280,128]{2,1,0:T(8,128)(2,1)} %copy-done), channel_id=1, source_target_pairs={{0,2},{2,0},{4,6},{6,4},{8,10},{10,8},{12,14},{14,12},{16,18},{18,... | collective-permute-start | bytes 3932168 | tf_op jit(solution)/shard_map/ppermute | solution.py:183
  97.2 4.9 %collective-permute-start.11 = (bf16[4,1280,128]{2,1,0:T(8,128)(2,1)S(1)}, bf16[4,1280,128]{2,1,0:T(8,128)(2,1)S(1)}, u32[]{:S(2)}, u32[]{:S(2)}) collective-permute-start(bf16[4,1280,128]{2,1,0:T(8,128)(2,1)S(1)} %pad_maximum_fusion.1.refs_1_.refs_2_), channel_id=1, source_target_pairs={{0,2},{2,0},{4,6},{6,4},{8,10},{10,8},{12,14},{14,12},{16,18},{18,... | collective-permute-start | bytes 3932168 | tf_op jit(solution)/shard_map/ppermute | solution.py:183
  97.2 5.1 %collective-permute-start.12 = (bf16[4,1280,128]{2,1,0:T(8,128)(2,1)}, bf16[4,1280,128]{2,1,0:T(8,128)(2,1)S(1)}, u32[]{:S(2)}, u32[]{:S(2)}) collective-permute-start(bf16[4,1280,128]{2,1,0:T(8,128)(2,1)} %collective-permute-done.10.refs_3_.refs_4_), channel_id=1, source_target_pairs={{0,2},{2,0},{4,6},{6,4},{8,10},{10,8},{12,14},{14,12},{16,18},{18,... | collective-permute-start | bytes 3932168 | tf_op jit(solution)/shard_map/ppermute | solution.py:183
  111.5 22.3 %collective-permute-start.17 = (bf16[1280,128]{1,0:T(8,128)(2,1)S(1)}, bf16[1280,128]{1,0:T(8,128)(2,1)S(1)}, u32[]{:S(2)}, u32[]{:S(2)}) collective-permute-start(bf16[1280,128]{1,0:T(8,128)(2,1)S(1)} %attend_2.1), channel_id=1, source_target_pairs={{0,16},{2,18},{4,20},{6,22},{8,24},{10,26},{12,28},{14,30},{16,0},... | collective-permute-start | bytes 983048 | tf_op jit(solution)/shard_map/ppermute | solution.py:171
  130.7 17.6 %collective-permute-start.15 = (bf16[1280,128]{1,0:T(8,128)(2,1)S(1)}, bf16[1280,128]{1,0:T(8,128)(2,1)S(1)}, u32[]{:S(2)}, u32[]{:S(2)}) collective-permute-start(bf16[1280,128]{1,0:T(8,128)(2,1)S(1)} %get-tuple-element.97), channel_id=1, source_target_pairs={{0,24},{2,26},{4,28},{6,30},{8,0},{10,2},{12,4},{14,6},{16,8},{18,... | collective-permute-start | bytes 983048 | tf_op jit(solution)/shard_map/ppermute | solution.py:171
  133.0 15.2 %collective-permute-start.16 = (bf16[1280,128]{1,0:T(8,128)(2,1)S(1)}, bf16[1280,128]{1,0:T(8,128)(2,1)S(1)}, u32[]{:S(2)}, u32[]{:S(2)}) collective-permute-start(bf16[1280,128]{1,0:T(8,128)(2,1)S(1)} %get-tuple-element.98), channel_id=1, source_target_pairs={{0,8},{2,10},{4,12},{6,14},{8,16},{10,18},{12,20},{14,22},{16,24},... | collective-permute-start | bytes 983048 | tf_op jit(solution)/shard_map/ppermute | solution.py:171
  (4 other events, 5.5 us)
